TPU v7x, 256 devices: a whole 4x4x8 slice. The times are simulated.
256 devices in a mesh: ep: 128 (over x, z, y), tp: 2 (over core).
Axes of the slice: x: 4, y: 4, z: 8, core: 2. Of those that a mesh axis runs over, the one named last changes fastest.
Arguments:
- query: bfloat16 [128, 32, 8192], P('ep', None, 'tp'), may hold values from -100 to 100
- new_kv: bfloat16 [2, 128, 32, 512], P(None, 'ep', None, 'tp'), may hold values from -4 to 4
- cache: bfloat16 [2, 128, 128, 512], P(None, 'ep', None, 'tp'), may hold values from -4 to 4
- cache_len: int32 [128], P('ep'), may hold values from 2 to 128
- parents: int32 [128, 32], P('ep'), may hold values from 0 to 30, as said below
- hidden: bfloat16 [4096, 4096], P('ep', 'tp'), may hold values from -6 to 6
- moe_gain: float32 [4096], replicated, may hold values from 0.5 to 1.5
- routes: int32 [4096, 8], P('ep'), may hold values from 0 to 127, all different within a row; in each aligned block of 32 rows (0 to 31, 32 to 63, ...) at most 4 rows name the same one
- gates: float32 [4096, 8], P('ep'), may hold values from 0.05 to 1
- w_gate: bfloat16 [128, 4096, 768], P('ep', None, 'tp'), may hold values from -0.09375 to 0.09375
- w_up: bfloat16 [128, 4096, 768], P('ep', None, 'tp'), may hold values from -0.09375 to 0.09375
- w_down: bfloat16 [128, 768, 4096], P('ep', 'tp'), may hold values from -0.21875 to 0.21875
- accept: int32 [128], P('ep'), may hold values from 0 to 31
- final_gain: float32 [4096], replicated, may hold values from 0.5 to 1.5
- medusa_w: bfloat16 [2, 4096, 4096], P(None, ('ep', 'tp')), may hold values from -0.09375 to 0.09375
- medusa_b: float32 [2, 4096], P(None, ('ep', 'tp')), may hold values from -3 to 3
- lm_head: bfloat16 [77824, 4096], P(('ep', 'tp')), may hold values from -12 to 12
Outputs:
- attended: bfloat16 [128, 32, 8192], P('ep', None, 'tp')
- layer_out: bfloat16 [4096, 4096], P('ep', 'tp')
- logprob: float32 [2, 128, 77824], P(None, None, ('ep', 'tp'))
Inputs may be any that keep to these rules, and one draw needn't show every extreme that they name: `routes`: each token names 8 different experts; among the tokens of one index of ep no expert is named more than 4 times. `parents`: node 0 is the root and names itself; every other node i names a parent below i.
All inputs are finite; a program needn't handle non-finite values.
Results may differ from a plain program's by a relative error of at most 0.0049.
Values may be sent and summed in bfloat16 or wider, within the bound.
No kernel may reach another device: no remote copies, remote signals or barrier semaphores. Data moves between devices by JAX's collectives and lax.ppermute only.
A program may use at most 128 MiB of HBM per device.

v0:
```python
import jax
import jax.numpy as jnp
from jax import lax
from jax.sharding import PartitionSpec as P

HD = 128
TOPK = 8
NODES = 32
REQ_DEV = 1


eps_norm = 1e-06


def ancestors(parent):
    count = parent.shape[-1]
    nodes = jnp.arange(count, dtype=jnp.int32)
    direct = (nodes[None, :] == parent[:, None]) | (nodes[None, :] == nodes[:, None])
    reach = direct.astype(jnp.float32)
    for level_index in range(max(1, (count - 1).bit_length())):
        reach = jnp.minimum(jnp.dot(reach, reach, precision=lax.Precision.HIGHEST), 1.0)
    return reach > 0.5


def tree_attention(query, new_keys, new_values, cache_keys, cache_values, length, parent):
    nodes = query.shape[0]
    kv_heads = cache_keys.shape[-1] // HD
    group = query.shape[-1] // HD // kv_heads
    keys = jnp.concatenate([cache_keys, new_keys], 0).reshape(-1, kv_heads, HD)
    values = jnp.concatenate([cache_values, new_values], 0).reshape(-1, kv_heads, HD)
    queries = query.reshape(nodes, kv_heads, group, HD)
    scores = jnp.einsum(
        "nkgd,skd->kgns", queries, keys, preferred_element_type=jnp.float32
    ) * HD ** (-0.5)
    places = jnp.arange(cache_keys.shape[0], dtype=jnp.int32)
    cache_seen = jnp.broadcast_to((places < length)[None, :], (nodes, cache_keys.shape[0]))
    visible = jnp.concatenate([cache_seen, ancestors(parent)], 1)
    scores = jnp.where(visible[None, None], scores, -jnp.inf)
    largest = jnp.max(scores, -1, keepdims=True)
    expo = jnp.exp(scores - largest)
    weight = (expo / jnp.sum(expo, -1, keepdims=True)).astype(jnp.bfloat16)
    mixed = jnp.einsum("kgns,skd->nkgd", weight, values, preferred_element_type=jnp.float32)
    return mixed.astype(jnp.bfloat16).reshape(nodes, -1)


def rms_scaled(values_in, gain):
    values = values_in.astype(jnp.float32)
    factor = lax.rsqrt(jnp.mean(values * values, -1, keepdims=True) + eps_norm)
    return (values * factor * gain).astype(jnp.bfloat16)


def expert_block(received, w_gate, w_up, w_down):
    sources, count, width = received.shape
    inputs = received.reshape(sources * count, width)
    gate_part = jnp.dot(inputs, w_gate[0], preferred_element_type=jnp.float32)
    up_part = jnp.dot(inputs, w_up[0], preferred_element_type=jnp.float32)
    activation = (jax.nn.silu(gate_part) * up_part).astype(jnp.bfloat16)
    partial_out = jnp.dot(activation, w_down[0], preferred_element_type=jnp.float32)
    partial_out = partial_out.reshape(sources, count, width)
    finished = lax.psum_scatter(partial_out, "tp", scatter_dimension=2, tiled=True).astype(
        jnp.bfloat16
    )
    return lax.all_to_all(finished, "ep", split_axis=0, concat_axis=0, tiled=True)


def on_device(
    query,
    new_kv,
    cache,
    cache_len,
    parents,
    hidden,
    moe_gain,
    routes,
    gates,
    w_gate,
    w_up,
    w_down,
    accept,
    final_gain,
    medusa_w,
    medusa_b,
    lm_head,
):
    attended = jax.vmap(tree_attention)(
        query, new_kv[0], new_kv[1], cache[0], cache[1], cache_len, parents
    )
    pair_count = lax.axis_size("tp")
    pair_index = lax.axis_index("tp")
    whole_rows = lax.all_gather(hidden, "tp", axis=1, tiled=True)
    normed = rms_scaled(whole_rows, moe_gain)
    token_count, width = normed.shape
    half_width = width // pair_count
    expert_count = lax.axis_size("ep")
    capacity = max(2, 2 * TOPK * NODES * REQ_DEV // expert_count)
    picks = routes.reshape(-1)
    onehot = (picks[:, None] == jnp.arange(expert_count, dtype=jnp.int32)[None, :]).astype(
        jnp.int32
    )
    ranking = jnp.sum(jnp.cumsum(onehot, 0) * onehot, -1) - 1
    slot_index = picks * capacity + ranking
    placed = (
        jnp.arange(expert_count * capacity, dtype=jnp.int32)[:, None, None]
        == slot_index.reshape(token_count, TOPK)[None]
    )
    chooser = jnp.any(placed, -1).astype(jnp.bfloat16)
    outgoing = jnp.dot(chooser, normed, preferred_element_type=jnp.float32).astype(jnp.bfloat16)
    outgoing = outgoing.reshape(expert_count, capacity, width)
    returned = expert_block(
        lax.all_to_all(outgoing, "ep", split_axis=0, concat_axis=0, tiled=True),
        w_gate,
        w_up,
        w_down,
    )
    picked_out = returned.reshape(expert_count * capacity, half_width)[slot_index]
    picked_out = picked_out.reshape(token_count, TOPK, half_width)
    share = gates / jnp.sum(gates, -1, keepdims=True)
    mixture = jnp.sum(share[:, :, None] * picked_out.astype(jnp.float32), 1)
    layer_out = (hidden.astype(jnp.float32) + mixture).astype(jnp.bfloat16)
    local_requests = accept.shape[0]
    by_request = layer_out.reshape(local_requests, NODES, half_width)
    chosen = by_request[jnp.arange(local_requests), accept]
    gathered = lax.all_gather(chosen, ("ep", "tp"), axis=0, tiled=True)
    gathered = gathered.reshape(expert_count, pair_count, local_requests, half_width)
    full_rows = jnp.transpose(gathered, (0, 2, 1, 3)).reshape(expert_count * local_requests, width)
    final = rms_scaled(full_rows, final_gain)
    block_width = medusa_w.shape[1]
    offset = (lax.axis_index("ep") * pair_count + pair_index) * block_width
    inner = jnp.einsum("ri,koi->kro", final, medusa_w, preferred_element_type=jnp.float32)
    own_part = lax.dynamic_slice_in_dim(final, offset, block_width, 1).astype(jnp.float32)
    head_part = (own_part[None] + jax.nn.silu(inner + medusa_b[:, None, :])).astype(jnp.bfloat16)
    heads = lax.all_gather(head_part, ("ep", "tp"), axis=2, tiled=True)
    logits = jnp.einsum("krd,vd->krv", heads, lm_head, preferred_element_type=jnp.float32)
    local_largest = jnp.max(logits, -1)
    largest = lax.pmax(local_largest, ("ep", "tp"))
    totals = lax.psum(jnp.sum(jnp.exp(logits - largest[..., None]), -1), ("ep", "tp"))
    logprob = logits - (largest + jnp.log(totals))[..., None]
    return (attended, layer_out, logprob)


def solution(mesh):
    in_specs = (
        P("ep", None, "tp"),
        P(None, "ep", None, "tp"),
        P(None, "ep", None, "tp"),
        P("ep"),
        P("ep", None),
        P("ep", "tp"),
        P(),
        P("ep", None),
        P("ep", None),
        P("ep", None, "tp"),
        P("ep", None, "tp"),
        P("ep", "tp", None),
        P("ep"),
        P(),
        P(None, ("ep", "tp"), None),
        P(None, ("ep", "tp")),
        P(("ep", "tp"), None),
    )
    out_specs = (P("ep", None, "tp"), P("ep", "tp"), P(None, None, ("ep", "tp")))
    return jax.shard_map(
        on_device, mesh=mesh, in_specs=in_specs, out_specs=out_specs, check_vma=False
    )
```

profile of v0, /device:TPU:1, one launch (start us, length us, event | category | flops | bytes accessed | tf_op | source)
XLA Modules:
  0.0 634.0 jit_solution(16390676531232098231)
XLA Ops:
  7.2 0.9 copy.102
  9.8 5.2 all_gather.9
  15.2 4.0 convolution_convert_fusion
  19.2 7.2 %reshape.250 = bf16[128,4,4096]{2,1,0:T(4,128)(2,1)} reshape(bf16[512,4096]{1,0:T(8,128)(2,1)} %convolution_convert_fusion) | data formatting | bytes 8388608 | tf_op jit(solution)/shard_map/reshape | solution.py:108
  26.4 107.0 %all_to_all.10 = bf16[128,4,4096]{2,1,0:T(4,128)(2,1)} all-to-all(bf16[128,4,4096]{2,1,0:T(4,128)(2,1)} %reshape.250), channel_id=1, replica_groups=mesh['ep'=128,'tp'=2] {'ep'}, dimensions={0} | all-to-all | bytes 8388608 | tf_op jit(solution)/shard_map/all_to_all | solution.py:110
  133.4 6.9 %reshape.251 = bf16[512,4096]{1,0:T(8,128)(2,1)} reshape(bf16[128,4,4096]{2,1,0:T(4,128)(2,1)} %all_to_all.10) | data formatting | bytes 8388608 | tf_op jit(solution)/shard_map/reshape | solution.py:54
  140.4 5.6 fusion.4
  146.0 3.1 fusion.13
  149.1 1.1 dot_general.51
  150.2 5.6 fusion
  155.8 21.7 %reduce-scatter.2.cloned.1.call-done = f32[128,4,2048]{2,0,1:T(8,128)} async-done(((f32[128,4,4096]{2,0,1:T(8,128)}), f32[128,4,2048]{2,0,1:T(8,128)}) %reduce-scatter.2.cloned.1.call-update) | async-done | bytes 4194320 | tf_op jit(solution)/shard_map/reduce_scatter | solution.py:60
  177.5 2.5 convert_element_type.74
  180.0 2.9 copy.108
  183.0 14.6 %all-to-all-start.1 = ((bf16[128,4,2048]{2,1,0:T(4,128)(2,1)}), bf16[128,4,2048]{2,1,0:T(4,128)(2,1)}, u32[]{:S(2)}, u32[]{:S(2)}) async-start(bf16[128,4,2048]{2,1,0:T(4,128)(2,1)} %copy.108), calls=%async_computation.2 | async-start | bytes 4194304 | tf_op jit(solution)/shard_map/all_to_all | solution.py:63
  198.5 48.1 %all-to-all-done.1 = bf16[128,4,2048]{2,1,0:T(4,128)(2,1)} async-done(((bf16[128,4,2048]{2,1,0:T(4,128)(2,1)}), bf16[128,4,2048]{2,1,0:T(4,128)(2,1)}, u32[]{:S(2)}, u32[]{:S(2)}) %all-to-all-start.1) | async-done | bytes 2097184 | tf_op jit(solution)/shard_map/all_to_all | solution.py:63
  246.6 2.5 reshape.252
  249.1 1.4 gather_fusion
  250.5 1.0 fusion.8
  251.5 0.6 dynamic-slice_bitcast_fusion
  252.2 102.0 %all-gather.6.cloned.1.call-done = bf16[256,1,2048]{2,1,0:T(2,128)(2,1)} async-done(((bf16[1,1,2048]{2,1,0:T(2,128)(2,1)}), bf16[256,1,2048]{2,1,0:T(2,128)(2,1)}) %all-gather.6.cloned.1.call-update) | async-done | bytes 1048592 | tf_op jit(solution)/shard_map/all_gather | solution.py:123
  354.3 9.6 %multiply_reduce_fusion = (f32[256]{0:T(256)S(1)}, f32[256,2048]{1,0:T(8,128)S(1)}) fusion(bf16[256,1,2048]{2,1,0:T(2,128)(2,1)} %all-gather.6.cloned.1.call-done), kind=kLoop, calls=%fused_computation.12 | loop fusion | flops 1572608 | bytes 3146752 | tf_op jit(solution)/shard_map/reduce_sum | solution.py:48
  363.9 2.0 reshape.277
  365.8 1.9 copy.109
  368.1 0.7 multiply_convert_fusion
  368.8 1.8 add_convert_fusion.1
  371.0 0.7 fusion.50
  375.0 0.8 reshape.248
  375.8 98.5 %all-gather.4.cloned.1.call-done = bf16[2,128,4096]{1,2,0:T(8,128)(2,1)} async-done(((bf16[2,128,16]{1,2,0:T(8,128)(2,1)}), bf16[2,128,4096]{1,2,0:T(8,128)(2,1)}) %all-gather.4.cloned.1.call-update) | async-done | bytes 2097168 | tf_op jit(solution)/shard_map/all_gather | solution.py:132
  474.2 3.2 fusion.52
  477.4 76.8 %pmax.7 = f32[2,128]{1,0:T(2,128)S(1)} all-reduce(f32[2,128]{1,0:T(2,128)S(1)} %get-tuple-element.24), channel_id=1, replica_groups=mesh['ep'=128,'tp'=2] {'ep','tp'}, use_global_device_ids=true, to_apply=%region_13.14 | all-reduce | flops 256 | bytes 2048 | tf_op jit(solution)/shard_map/pmax | solution.py:135
  554.3 72.4 %psum.7 = f32[2,128]{1,0:T(2,128)S(1)} all-reduce(f32[2,128]{1,0:T(2,128)S(1)} %exponential_reduce_fusion), channel_id=1, replica_groups=mesh['ep'=128,'tp'=2] {'ep','tp'}, use_global_device_ids=true, to_apply=%region_15.16 | all-reduce | flops 256 | bytes 2048 | tf_op jit(solution)/shard_map/psum | solution.py:136
  626.7 0.7 broadcast_subtract_fusion
  (84 shorter events, 5.3 us)
Async XLA Ops:
  7.2 143.0 %copy-start = (bf16[1,384,4096]{2,1,0:T(8,128)(2,1)S(1)}, bf16[1,384,4096]{2,1,0:T(8,128)(2,1)}, u32[]{:S(2)}) copy-start(bf16[1,384,4096]{2,1,0:T(8,128)(2,1)} %param.28) | copy-start | bytes 9437188
  7.2 170.3 %reduce-scatter.2.cloned.1.call-start = ((), (), s32[]{:S(2)}) async-start(), calls=%async_computation.3 | async-start | bytes 12582912 | tf_op jit(solution)/shard_map/reduce_scatter | solution.py:60
  8.9 0.6 copy-start.9
  140.4 5.6 copy-start.2
  140.4 5.6 copy-start.11
  183.0 14.7 %copy-start.8 = (f32[32,8]{0,1:T(8,128)S(1)}, f32[32,8]{0,1:T(8,128)}, u32[]{:S(2)}) copy-start(f32[32,8]{0,1:T(8,128)} %param.25) | copy-start | bytes 3076
  183.0 15.5 %copy-start.10 = (s32[256]{0:T(256)S(1)}, s32[256]{0:T(256)}, u32[]{:S(2)}) copy-start(s32[256]{0:T(256)} %copy-done.9) | copy-start | bytes 3076
  183.0 63.6 %all-to-all-start.1 = ((bf16[128,4,2048]{2,1,0:T(4,128)(2,1)}), bf16[128,4,2048]{2,1,0:T(4,128)(2,1)}, u32[]{:S(2)}, u32[]{:S(2)}) async-start(bf16[128,4,2048]{2,1,0:T(4,128)(2,1)} %copy.108), calls=%async_computation.2 | async-start | bytes 4194304 | tf_op jit(solution)/shard_map/all_to_all | solution.py:63
  197.5 156.8 %all-gather.6.cloned.1.call-start = ((), (), s32[]{:S(2)}) async-start(), calls=%async_computation.5 | async-start | bytes 2105344 | tf_op jit(solution)/shard_map/all_gather | solution.py:123
  249.1 2.3 copy-start.3
  251.5 0.7 copy-start.5
  252.2 222.1 %all-gather.4.cloned.1.call-start = ((), (), s32[]{:S(2)}) async-start(), calls=%async_computation.4 | async-start | bytes 2105344 | tf_op jit(solution)/shard_map/all_gather | solution.py:132
  365.8 2.2 copy-start.7
  367.8 2.9 copy-start.6
  368.1 3.7 copy-start.4
  368.8 4.0 copy-start.12
  374.9 252.5 %copy-start.1 = (bf16[1,384,4096]{2,1,0:T(8,128)(2,1)S(1)}, bf16[1,384,4096]{2,1,0:T(8,128)(2,1)}, u32[]{:S(2)}) copy-start(bf16[1,384,4096]{2,1,0:T(8,128)(2,1)} %param.28) | copy-start | bytes 9437188
Sparse Core Ops, SparseCore 0:
  155.9 21.5 reduce-scatter.1
  252.3 101.9 all-gather.5
  370.8 103.4 all-gather.3
where the time goes:
time: 635 us; the launch traced here: 634 us
  waiting for transfers between devices  270 us (43%)
  blocking collectives  261 us (41%)
  local copies, waits for them, and re-layouts  31 us (5%)
  matrix products  24.9 us (4%)
  other arithmetic  16 us (3%)
  between operations  15.5 us (2%)
  starting transfers between devices  14.7 us (2%)
    all_to_all x1, blocking collectives, on_device(): lax.all_to_all(outgoing, 'ep', split_axis=0, concat_axis=0, tiled=True)  107 us
    all_gather x1, waiting for transfers between devices, on_device(): gathered = lax.all_gather(chosen, ('ep', 'tp'), axis=0, tiled=True)  102 us
    all_gather x1, waiting for transfers between devices, on_device(): heads = lax.all_gather(head_part, ('ep', 'tp'), axis=2, tiled=True)  98.5 us
    pmax x1, blocking collectives, on_device(): largest = lax.pmax(local_largest, ('ep', 'tp'))  76.8 us
    psum x1, blocking collectives, on_device(): lax.psum(jnp.sum(jnp.exp(logits - largest[..., None]), -1), ('ep', 'tp'))  72.4 us
    all_to_all x1, waiting for transfers between devices, expert_block(): lax.all_to_all(finished, 'ep', split_axis=0, concat_axis=0, tiled=True)  48.1 us
    reduce_scatter x1, waiting for transfers between devices, expert_block(): lax.psum_scatter(partial_out, 'tp', scatter_dimension=2, tiled=True)  21.7 us
    all_to_all x1, starting transfers between devices, expert_block(): lax.all_to_all(finished, 'ep', split_axis=0, concat_axis=0, tiled=True)  14.6 us
  transfers between devices with their start and end apart: 4, of which 4 were waited for; matrix products, arithmetic and copies ran while one was open for 1% of the time, Pallas kernels for 0%

commit v1 on v0

v1 whole, which is shorter than its diff:
```python
import jax
import jax.numpy as jnp
from jax import lax
from jax.sharding import Mesh, PartitionSpec as P

HD = 128
TOPK = 8
NODES = 32
CAP = 4
EXPERTS = 128
D = 4096
HALF = D // 2

eps_norm = 1e-06
EP = ("x", "z", "y")
TP = "c"
ALL = ("x", "z", "y", "c")
SWAP = [(0, 1), (1, 0)]


def ancestors(parent):
    count = parent.shape[-1]
    nodes = jnp.arange(count, dtype=jnp.int32)
    direct = (nodes[None, :] == parent[:, None]) | (nodes[None, :] == nodes[:, None])
    reach = direct.astype(jnp.float32)
    for level_index in range(max(1, (count - 1).bit_length())):
        reach = jnp.minimum(jnp.dot(reach, reach, precision=lax.Precision.HIGHEST), 1.0)
    return reach > 0.5


def tree_attention(query, new_keys, new_values, cache_keys, cache_values, length, parent):
    nodes = query.shape[0]
    kv_heads = cache_keys.shape[-1] // HD
    group = query.shape[-1] // HD // kv_heads
    keys = jnp.concatenate([cache_keys, new_keys], 0).reshape(-1, kv_heads, HD)
    values = jnp.concatenate([cache_values, new_values], 0).reshape(-1, kv_heads, HD)
    queries = query.reshape(nodes, kv_heads, group, HD)
    scores = jnp.einsum(
        "nkgd,skd->kgns", queries, keys, preferred_element_type=jnp.float32
    ) * HD ** (-0.5)
    places = jnp.arange(cache_keys.shape[0], dtype=jnp.int32)
    cache_seen = jnp.broadcast_to((places < length)[None, :], (nodes, cache_keys.shape[0]))
    visible = jnp.concatenate([cache_seen, ancestors(parent)], 1)
    scores = jnp.where(visible[None, None], scores, -jnp.inf)
    largest = jnp.max(scores, -1, keepdims=True)
    expo = jnp.exp(scores - largest)
    weight = (expo / jnp.sum(expo, -1, keepdims=True)).astype(jnp.bfloat16)
    mixed = jnp.einsum("kgns,skd->nkgd", weight, values, preferred_element_type=jnp.float32)
    return mixed.astype(jnp.bfloat16).reshape(nodes, -1)


def swap(value):
    return lax.ppermute(value, TP, SWAP)


def spread(value, axes, count):
    copies = jnp.broadcast_to(value[None], (count,) + value.shape)
    return lax.all_to_all(copies, axes, 0, 0, tiled=True)


def pair(index, own, other, axis):
    first = jnp.where(index == 0, own, other)
    second = jnp.where(index == 0, other, own)
    return jnp.concatenate([first, second], axis)


def dot32(left, right):
    return jnp.dot(left, right, preferred_element_type=jnp.float32)


def own_scaled(own, square_sum, own_gain):
    factor = lax.rsqrt(square_sum / D + eps_norm)
    return (own * factor * own_gain).astype(jnp.bfloat16)


def merged(stats):
    tops, sums = stats[:, :2], stats[:, 2:]
    top = jnp.max(tops, 0)
    return jnp.concatenate([top, jnp.sum(sums * jnp.exp(tops - top[None]), 0)], 0)


def on_device(
    query,
    new_kv,
    cache,
    cache_len,
    parents,
    hidden,
    moe_gain,
    routes,
    gates,
    w_gate,
    w_up,
    w_down,
    accept,
    final_gain,
    medusa_w,
    medusa_b,
    lm_head,
):
    core = lax.axis_index(TP)
    own_at, other_at = core * HALF, (1 - core) * HALF

    def own_half(array, axis):
        return lax.dynamic_slice_in_dim(array, own_at, HALF, axis)

    def other_half(array, axis):
        return lax.dynamic_slice_in_dim(array, other_at, HALF, axis)

    attended = jax.vmap(tree_attention)(
        query, new_kv[0], new_kv[1], cache[0], cache[1], cache_len, parents
    )

    down_own = own_half(w_down[0], 1)
    down_other = swap(other_half(w_down[0], 1))

    rows = hidden.astype(jnp.float32)
    squares = lax.psum(jnp.sum(rows * rows, -1, keepdims=True), TP)
    normed = own_scaled(rows, squares, own_half(moe_gain, 0))

    picks = routes.reshape(-1)
    onehot = picks[:, None] == jnp.arange(EXPERTS, dtype=jnp.int32)[None, :]
    onehot = onehot.astype(jnp.int32)
    ranking = jnp.sum(jnp.cumsum(onehot, 0) * onehot, -1) - 1
    slot_index = (picks * CAP + ranking).reshape(NODES, TOPK)
    places = jnp.arange(EXPERTS * CAP, dtype=jnp.int32)[:, None, None] == slot_index[None]
    chooser = jnp.any(places, -1).astype(jnp.bfloat16)
    outgoing = dot32(chooser, normed).astype(jnp.bfloat16).reshape(EXPERTS, CAP, HALF)
    arrived = lax.all_to_all(outgoing, EP, 0, 0, tiled=True).reshape(EXPERTS * CAP, HALF)
    arrived_other = swap(arrived)

    gate_part = dot32(arrived, own_half(w_gate[0], 0)) + dot32(
        arrived_other, other_half(w_gate[0], 0)
    )
    up_part = dot32(arrived, own_half(w_up[0], 0)) + dot32(arrived_other, other_half(w_up[0], 0))
    activation = (jax.nn.silu(gate_part) * up_part).astype(jnp.bfloat16)
    finished = dot32(activation, down_own) + dot32(swap(activation), down_other)
    finished = finished.astype(jnp.bfloat16).reshape(EXPERTS, CAP, HALF)
    returned = lax.all_to_all(finished, EP, 0, 0, tiled=True).reshape(EXPERTS * CAP, HALF)

    share = gates / jnp.sum(gates, -1, keepdims=True)
    picked_out = returned[slot_index.reshape(-1)].reshape(NODES, TOPK, HALF)
    mixture = jnp.sum(share[:, :, None] * picked_out.astype(jnp.float32), 1)
    layer_out = (rows + mixture).astype(jnp.bfloat16)

    chosen = layer_out[accept[0]].reshape(16, 128)
    chosen_own = spread(chosen, EP, EXPERTS).reshape(EXPERTS, HALF)
    chosen_other = swap(chosen_own)
    wide_own, wide_other = chosen_own.astype(jnp.float32), chosen_other.astype(jnp.float32)
    squares = jnp.sum(wide_own * wide_own, -1, keepdims=True) + jnp.sum(
        wide_other * wide_other, -1, keepdims=True
    )
    final = pair(
        core,
        own_scaled(wide_own, squares, own_half(final_gain, 0)),
        own_scaled(wide_other, squares, other_half(final_gain, 0)),
        1,
    )
    block = medusa_w.shape[1]
    index = (lax.axis_index("x") * 8 + lax.axis_index("z")) * 4 + lax.axis_index("y")
    offset = (index * 2 + core) * block
    inner = jnp.einsum("koi,ri->kor", medusa_w, final, preferred_element_type=jnp.float32)
    own_part = lax.dynamic_slice_in_dim(final, offset, block, 1).astype(jnp.float32).T
    head_part = own_part[None] + jax.nn.silu(inner + medusa_b[:, :, None])
    head_part = head_part.astype(jnp.bfloat16).reshape(2 * block, EXPERTS)

    heads_own = spread(head_part, EP, EXPERTS)
    heads_other = swap(heads_own)
    both = pair(core, heads_own[:, None], heads_other[:, None], 1)
    both = both.reshape(EXPERTS, 2, 2, block, EXPERTS)
    heads = jnp.transpose(both, (2, 0, 1, 3, 4)).reshape(2, D, EXPERTS)
    logits = jnp.einsum("kdr,vd->krv", heads, lm_head, preferred_element_type=jnp.float32)
    top = jnp.max(logits, -1)
    sums = jnp.sum(jnp.exp(logits - top[..., None]), -1)
    stats = jnp.concatenate([top, sums], 0)
    stats = merged(spread(stats, ("x", "y", "c"), 32))
    stats = merged(spread(stats, "z", 8))
    logprob = logits - (stats[:2] + jnp.log(stats[2:]))[..., None]
    return (attended, layer_out, logprob)


def solution(mesh):
    fine = Mesh(mesh.devices.reshape(4, 8, 4, 2), ALL)
    in_specs = (
        P(EP, None, TP),
        P(None, EP, None, TP),
        P(None, EP, None, TP),
        P(EP),
        P(EP, None),
        P(EP, TP),
        P(),
        P(EP, None),
        P(EP, None),
        P(EP, None, TP),
        P(EP, None, TP),
        P(EP, TP, None),
        P(EP),
        P(),
        P(None, ALL, None),
        P(None, ALL),
        P(ALL, None),
    )
    out_specs = (P(EP, None, TP), P(EP, TP), P(None, None, ALL))
    return jax.shard_map(
        on_device, mesh=fine, in_specs=in_specs, out_specs=out_specs, check_vma=False
    )
```

time: 635 us -> 292 us (0.46)
  waiting for transfers between devices: 270 us -> 77.5 us
  blocking collectives: 261 us -> 95.1 us
  starting transfers between devices: 14.7 us -> 33.7 us
  between operations: 15.5 us -> 2.41 us
  local copies, waits for them, and re-layouts: 31 us -> 42.8 us
    all_gather x2 -> x0, waiting for transfers between devices: 201 us -> none  [the longest x1 102 us: on_device(): gathered = lax.all_gather(chosen, ('ep', 'tp'), axis=0, tiled=True)]
    pmax x1 -> x0, blocking collectives: 76.8 us -> none  [on_device(): largest = lax.pmax(local_largest, ('ep', 'tp'))]
    psum x1, blocking collectives: 72.4 us -> 5.36 us  [on_device(): squares = lax.psum(jnp.sum(rows * rows, -1, keepdims=True), TP)]
    all_to_all x1 -> x4, waiting for transfers between devices: 48.1 us -> 77.1 us  [the longest x1 48.3 us: on_device(): lax.all_to_all(finished, EP, 0, 0, tiled=True).reshape(EXPERTS * CAP, HALF)]
    reduce_scatter x1 -> x0, waiting for transfers between devices: 21.7 us -> none  [expert_block(): lax.psum_scatter(partial_out, 'tp', scatter_dimension=2, tiled=True)]
    all_to_all x1 -> x2, blocking collectives: 107 us -> 89.8 us  [the longest x1 63.3 us: on_device(): lax.all_to_all(outgoing, EP, 0, 0, tiled=True).reshape(EXPERTS * CAP, HALF)]
    ppermute x0 -> x5, starting transfers between devices: none -> 10.1 us  [swap(): return lax.ppermute(value, TP, SWAP)]
    all_to_all x1 -> x4, starting transfers between devices: 14.6 us -> 23.6 us  [the longest x3 15.7 us: spread(): return lax.all_to_all(copies, axes, 0, 0, tiled=True)]
  transfers between devices with their start and end apart: 4 -> 9, of which waited for: 4 -> 5; matrix products, arithmetic and copies ran while one was open for 1% -> 10% of each run, Pallas kernels for 0% -> 0%
where the time goes in v1:
time: 292 us; the launch traced here: 290 us
  blocking collectives  95.1 us (33%)
  waiting for transfers between devices  77.5 us (27%)
  local copies, waits for them, and re-layouts  42.8 us (15%)
  starting transfers between devices  33.7 us (12%)
  matrix products  23.7 us (8%)
  other arithmetic  14.7 us (5%)
    all_to_all x1, blocking collectives, on_device(): lax.all_to_all(outgoing, EP, 0, 0, tiled=True).reshape(EXPERTS * CAP, HALF)  63.3 us
    all_to_all x1, waiting for transfers between devices, on_device(): lax.all_to_all(finished, EP, 0, 0, tiled=True).reshape(EXPERTS * CAP, HALF)  48.3 us
    all_to_all x3, waiting for transfers between devices, spread(): return lax.all_to_all(copies, axes, 0, 0, tiled=True)  28.8 us
    all_to_all x1, blocking collectives, spread(): return lax.all_to_all(copies, axes, 0, 0, tiled=True)  26.4 us
    dot_general x7, matrix products, dot32(): return jnp.dot(left, right, preferred_element_type=jnp.float32)  16.6 us
    all_to_all x3, starting transfers between devices, spread(): return lax.all_to_all(copies, axes, 0, 0, tiled=True)  15.7 us
    ppermute x5, starting transfers between devices, swap(): return lax.ppermute(value, TP, SWAP)  10.1 us
    unnamed x42, local copies, waits for them, and re-layouts  9.32 us
  transfers between devices with their start and end apart: 9, of which 5 were waited for; matrix products, arithmetic and copies ran while one was open for 10% of the time, Pallas kernels for 0%

profile of v1, /device:TPU:1, one launch (start us, length us, event | category | flops | bytes accessed | tf_op | source)
XLA Modules:
  0.0 290.0 jit_solution(3512669416426185229)
XLA Ops:
  3.7 5.4 %psum.7 = f32[32,1]{0,1:T(1,128)S(1)} all-reduce(f32[32,1]{0,1:T(1,128)S(1)} %bitcast.157), channel_id=1, replica_groups=mesh['x'=4,'z'=8,'y'=4,'c'=2] {'c'}, use_global_device_ids=true, to_apply=%region_8.9 | all-reduce | flops 32 | bytes 256 | tf_op jit(solution)/shard_map/psum | solution.py:118
  9.8 3.0 %convolution_convert_fusion = bf16[512,2048]{1,0:T(8,128)(2,1)} fusion(pred[512,32]{0,1:T(8,128)(4,1)S(1)} %fusion.37, bf16[32,2048]{1,0:T(8,128)(2,1)} %param.22, f32[2048]{0:T(1024)S(1)} %dynamic_slice.45, f32[32]{0:T(128)S(1)} %rsqrt_bitcast_fusion), kind=kOutput, calls=%fused_computation.2 | convolution fusion | flops 68419584 | bytes 2252928 | tf_op jit(solution)/shard_map/dot_general | solution.py:68
  12.8 4.1 %reshape.272 = bf16[128,4,2048]{2,1,0:T(4,128)(2,1)} reshape(bf16[512,2048]{1,0:T(8,128)(2,1)} %convolution_convert_fusion) | data formatting | bytes 4194304 | tf_op jit(solution)/shard_map/reshape | solution.py:128
  16.9 63.3 %all_to_all.30 = bf16[128,4,2048]{2,1,0:T(4,128)(2,1)} all-to-all(bf16[128,4,2048]{2,1,0:T(4,128)(2,1)} %reshape.272), channel_id=1, replica_groups=mesh['x'=4,'z'=8,'y'=4,'c'=2] {'x','z','y'}, dimensions={0} | all-to-all | bytes 4194304 | tf_op jit(solution)/shard_map/all_to_all | solution.py:129
  80.2 4.0 %reshape.273 = bf16[512,2048]{1,0:T(8,128)(2,1)} reshape(bf16[128,4,2048]{2,1,0:T(4,128)(2,1)} %all_to_all.30) | data formatting | bytes 4194304 | tf_op jit(solution)/shard_map/reshape | solution.py:129
  84.2 3.8 %collective-permute-start = (bf16[512,2048]{1,0:T(8,128)(2,1)}, bf16[512,2048]{1,0:T(8,128)(2,1)}, u32[]{:S(2)}, u32[]{:S(2)}) collective-permute-start(bf16[512,2048]{1,0:T(8,128)(2,1)} %reshape.273), channel_id=1, source_target_pairs={{0,1},{1,0},{2,3},{3,2},{4,5},{5,4},{6,7},{7,6},{8,9},{9,8},{10,11... | collective-permute-start | bytes 6291464 | tf_op jit(solution)/shard_map/ppermute | solution.py:53
  89.5 2.7 fusion.11
  94.1 2.9 fusion.19
  97.0 2.9 %multiply_convert_fusion.1 = bf16[512,384]{1,0:T(8,128)(2,1)S(1)} fusion(f32[512,384]{1,0:T(8,128)S(1)} %fusion.19, f32[512,384]{1,0:T(8,128)S(1)} %fusion.7, bf16[512,2048]{1,0:T(8,128)(2,1)} %collective-permute-done, bf16[1,4096,384]{2,1,0:T(8,128)(2,1)S(1)} %copy-done.14, s32[]{:T(128)S(6)} %select_n.61), kind=kOutput, calls=%fused_computation.56 | convolution fusion | flops 806682624 | bytes 5636100 | tf_op jit(solution)/shard_map/dot_general | solution.py:68
  101.8 2.6 add_convert_fusion
  104.4 4.1 %reshape.274 = bf16[128,4,2048]{2,1,0:T(4,128)(2,1)} reshape(bf16[512,2048]{1,0:T(8,128)(2,1)} %add_convert_fusion) | data formatting | bytes 4194304 | tf_op jit(solution)/shard_map/reshape | solution.py:138
  108.5 7.9 %all-to-all-start.1 = ((bf16[128,4,2048]{2,1,0:T(4,128)(2,1)}), bf16[128,4,2048]{2,1,0:T(4,128)(2,1)}, u32[]{:S(2)}, u32[]{:S(2)}) async-start(bf16[128,4,2048]{2,1,0:T(4,128)(2,1)} %reshape.274), calls=%async_computation.1 | async-start | bytes 4194304 | tf_op jit(solution)/shard_map/all_to_all | solution.py:139
  117.3 48.3 %all-to-all-done.1 = bf16[128,4,2048]{2,1,0:T(4,128)(2,1)} async-done(((bf16[128,4,2048]{2,1,0:T(4,128)(2,1)}), bf16[128,4,2048]{2,1,0:T(4,128)(2,1)}, u32[]{:S(2)}, u32[]{:S(2)}) %all-to-all-start.1) | async-done | bytes 2097184 | tf_op jit(solution)/shard_map/all_to_all | solution.py:139
  165.6 4.0 %reshape.275 = bf16[512,2048]{1,0:T(8,128)(2,1)} reshape(bf16[128,4,2048]{2,1,0:T(4,128)(2,1)} %all-to-all-done.1) | data formatting | bytes 4194304 | tf_op jit(solution)/shard_map/reshape | solution.py:139
  169.6 5.2 %gather_fusion = bf16[256,2048]{1,0:T(8,128)(2,1)} fusion(bf16[512,2048]{1,0:T(8,128)(2,1)} %reshape.275, s32[1024]{0:T(1024)S(1)} %pad_clamp_fusion), kind=kCustom, calls=%fused_computation | custom fusion | bytes 2098176 | tf_op jit(solution)/shard_map/gather | solution.py:142
  174.8 2.2 fusion.2
  177.8 26.4 %all_to_all.31 = bf16[128,16,128]{2,1,0:T(8,128)(2,1)S(1)} all-to-all(bf16[128,16,128]{2,1,0:T(8,128)(2,1)S(1)} %broadcast_in_dim.36), channel_id=1, replica_groups=mesh['x'=4,'z'=8,'y'=4,'c'=2] {'x','z','y'}, dimensions={0} | all-to-all | bytes 1048576 | tf_op jit(solution)/shard_map/all_to_all | solution.py:58
  206.0 3.4 %collective-permute-start.3 = (bf16[128,2048]{1,0:T(8,128)(2,1)}, bf16[128,2048]{1,0:T(8,128)(2,1)}, u32[]{:S(2)}, u32[]{:S(2)}) collective-permute-start(bf16[128,2048]{1,0:T(8,128)(2,1)} %bitcast.133), channel_id=1, source_target_pairs={{0,1},{1,0},{2,3},{3,2},{4,5},{5,4},{6,7},{7,6},{8,9},{9,8},{10,11... | collective-permute-start | bytes 1572872 | tf_op jit(solution)/shard_map/ppermute | solution.py:53
  209.4 2.1 multiply_reduce_fusion
  215.6 1.8 add_convert_fusion.1
  218.5 7.3 %all-to-all-start.3 = ((bf16[128,32,128]{2,1,0:T(8,128)(2,1)}), bf16[128,32,128]{2,1,0:T(8,128)(2,1)}, u32[]{:S(2)}, u32[]{:S(2)}) async-start(bf16[128,32,128]{2,1,0:T(8,128)(2,1)} %broadcast_in_dim.38), calls=%async_computation.3 | async-start | bytes 2097152 | tf_op jit(solution)/shard_map/all_to_all | solution.py:58
  229.0 24.6 %all-to-all-done.3 = bf16[128,32,128]{2,1,0:T(8,128)(2,1)} async-done(((bf16[128,32,128]{2,1,0:T(8,128)(2,1)}), bf16[128,32,128]{2,1,0:T(8,128)(2,1)}, u32[]{:S(2)}, u32[]{:S(2)}) %all-to-all-start.3) | async-done | bytes 1048608 | tf_op jit(solution)/shard_map/all_to_all | solution.py:58
  253.6 2.7 collective-permute-start.4
  259.1 2.0 fusion.76
  261.0 1.7 broadcast_select_fusion.1
  266.2 5.0 %all-to-all-start.4 = ((f32[32,4,128]{2,1,0:T(4,128)}), f32[32,4,128]{2,1,0:T(4,128)S(1)}, u32[]{:S(2)}, u32[]{:S(2)}) async-start(f32[32,4,128]{2,1,0:T(4,128)} %broadcast_in_dim.39), calls=%async_computation.4 | async-start | bytes 131072 | tf_op jit(solution)/shard_map/all_to_all | solution.py:58
  271.2 2.2 fusion.35
  276.6 2.0 all-to-all-done.4
  279.3 3.3 %all-to-all-start.5 = ((f32[8,4,128]{2,1,0:T(4,128)}), f32[8,4,128]{2,1,0:T(4,128)S(1)}, u32[]{:S(2)}, u32[]{:S(2)}) async-start(f32[8,4,128]{2,1,0:T(4,128)} %broadcast_in_dim.40), calls=%async_computation.5 | async-start | bytes 32768 | tf_op jit(solution)/shard_map/all_to_all | solution.py:58
  282.6 1.7 fusion.26
  285.2 1.8 reshape.270
  287.0 2.2 all-to-all-done.5
  (116 shorter events, 31.0 us)
Async XLA Ops:
  0.6 87.3 %copy-start = (bf16[1,384,4096]{2,1,0:T(8,128)(2,1)S(1)}, bf16[1,384,4096]{2,1,0:T(8,128)(2,1)}, u32[]{:S(2)}) copy-start(bf16[1,384,4096]{2,1,0:T(8,128)(2,1)} %param.28) | copy-start | bytes 9437188
  84.2 9.3 %collective-permute-start = (bf16[512,2048]{1,0:T(8,128)(2,1)}, bf16[512,2048]{1,0:T(8,128)(2,1)}, u32[]{:S(2)}, u32[]{:S(2)}) collective-permute-start(bf16[512,2048]{1,0:T(8,128)(2,1)} %reshape.273), channel_id=1, source_target_pairs={{0,1},{1,0},{2,3},{3,2},{4,5},{5,4},{6,7},{7,6},{8,9},{9,8},{10,11... | collective-permute-start | bytes 6291464 | tf_op jit(solution)/shard_map/ppermute | solution.py:53
  88.0 1.6 copy-start.2
  88.1 4.2 %copy-start.14 = (bf16[1,4096,384]{2,1,0:T(8,128)(2,1)S(1)}, bf16[1,4096,384]{2,1,0:T(8,128)(2,1)}, u32[]{:S(2)}) copy-start(bf16[1,4096,384]{2,1,0:T(8,128)(2,1)} %param.27) | copy-start | bytes 9437188
  88.1 13.3 %collective-permute-start.2 = (bf16[384,2048]{1,0:T(8,128)(2,1)S(1)}, bf16[384,2048]{1,0:T(8,128)(2,1)S(1)}, u32[]{:S(2)}, u32[]{:S(2)}) collective-permute-start(bf16[384,2048]{1,0:T(8,128)(2,1)S(1)} %dynamic-slice_bitcast_fusion), channel_id=1, source_target_pairs={{0,1},{1,0},{2,3},{3,2},{4,5},{5,4},{6,7},{7,6},{8,9},{9,8},{10,11... | collective-permute-start | bytes 4718600 | tf_op jit(solution)/shard_map/ppermute | solution.py:53
  92.2 1.9 copy-start.13
  100.0 1.8 collective-permute-start.1
  108.5 8.0 %copy-start.11 = (f32[32,8]{0,1:T(8,128)S(1)}, f32[32,8]{0,1:T(8,128)}, u32[]{:S(2)}) copy-start(f32[32,8]{0,1:T(8,128)} %param.25) | copy-start | bytes 3076
  108.5 57.1 %all-to-all-start.1 = ((bf16[128,4,2048]{2,1,0:T(4,128)(2,1)}), bf16[128,4,2048]{2,1,0:T(4,128)(2,1)}, u32[]{:S(2)}, u32[]{:S(2)}) async-start(bf16[128,4,2048]{2,1,0:T(4,128)(2,1)} %reshape.274), calls=%async_computation.1 | async-start | bytes 4194304 | tf_op jit(solution)/shard_map/all_to_all | solution.py:139
  169.6 7.5 %copy-start.5 = (bf16[32,2048]{1,0:T(8,128)(2,1)S(1)}, bf16[32,2048]{1,0:T(8,128)(2,1)}, u32[]{:S(2)}) copy-start(bf16[32,2048]{1,0:T(8,128)(2,1)} %param.22) | copy-start | bytes 393220
  174.8 34.6 %copy-start.12 = (f32[4096]{0:T(1024)S(1)}, f32[4096]{0:T(1024)}, u32[]{:S(2)}) copy-start(f32[4096]{0:T(1024)} %param.30) | copy-start | bytes 49156
  177.1 0.7 copy-start.7
  204.3 0.8 copy-start.1
  206.0 5.5 %collective-permute-start.3 = (bf16[128,2048]{1,0:T(8,128)(2,1)}, bf16[128,2048]{1,0:T(8,128)(2,1)}, u32[]{:S(2)}, u32[]{:S(2)}) collective-permute-start(bf16[128,2048]{1,0:T(8,128)(2,1)} %bitcast.133), channel_id=1, source_target_pairs={{0,1},{1,0},{2,3},{3,2},{4,5},{5,4},{6,7},{7,6},{8,9},{9,8},{10,11... | collective-permute-start | bytes 1572872 | tf_op jit(solution)/shard_map/ppermute | solution.py:53
  209.4 6.1 %copy-start.16 = (f32[2,16]{1,0:T(2,128)S(1)}, f32[2,16]{1,0:T(2,128)}, u32[]{:S(2)}) copy-start(f32[2,16]{1,0:T(2,128)} %param.32) | copy-start | bytes 388
  214.4 0.8 copy-start.3
  214.4 1.0 copy-start.4
  217.3 9.2 %copy-start.17 = (s32[1,32]{1,0:T(1,128)S(1)}, s32[1,32]{1,0:T(1,128)}, u32[]{:S(2)}) copy-start(s32[1,32]{1,0:T(1,128)} %param.21) | copy-start | bytes 388
  217.3 9.4 %copy-start.9 = (bf16[2,1,32,256]{3,2,1,0:T(8,128)(2,1)S(1)}, bf16[2,1,32,256]{3,2,1,0:T(8,128)(2,1)}, u32[]{:S(2)}) copy-start(bf16[2,1,32,256]{3,2,1,0:T(8,128)(2,1)} %param.18) | copy-start | bytes 98308
  217.3 40.5 %copy-start.6 = (bf16[1,32,4096]{2,1,0:T(8,128)(2,1)S(1)}, bf16[1,32,4096]{2,1,0:T(8,128)(2,1)}, u32[]{:S(2)}) copy-start(bf16[1,32,4096]{2,1,0:T(8,128)(2,1)} %param.17) | copy-start | bytes 786436
  218.5 35.0 %all-to-all-start.3 = ((bf16[128,32,128]{2,1,0:T(8,128)(2,1)}), bf16[128,32,128]{2,1,0:T(8,128)(2,1)}, u32[]{:S(2)}, u32[]{:S(2)}) async-start(bf16[128,32,128]{2,1,0:T(8,128)(2,1)} %broadcast_in_dim.38), calls=%async_computation.3 | async-start | bytes 2097152 | tf_op jit(solution)/shard_map/all_to_all | solution.py:58
  253.6 7.5 %collective-permute-start.4 = (bf16[128,32,128]{2,1,0:T(8,128)(2,1)}, bf16[128,32,128]{2,1,0:T(8,128)(2,1)}, u32[]{:S(2)}, u32[]{:S(2)}) collective-permute-start(bf16[128,32,128]{2,1,0:T(8,128)(2,1)} %all-to-all-done.3), channel_id=1, source_target_pairs={{0,1},{1,0},{2,3},{3,2},{4,5},{5,4},{6,7},{7,6},{8,9},{9,8},{10,11... | collective-permute-start | bytes 3145736 | tf_op jit(solution)/shard_map/ppermute | solution.py:53
  262.9 1.7 copy-start.15
  264.6 6.6 %copy-start.10 = (f32[2,16,32]{2,1,0:T(8,128)S(1)}, f32[2,16,32]{2,1,0:T(8,128)}, u32[]{:S(2)}) copy-start(f32[2,16,32]{2,1,0:T(8,128)} %get-tuple-element.15) | copy-start | bytes 12292
  264.6 11.9 %copy-start.8 = (bf16[1,1,32,256]{3,2,1,0:T(8,128)(2,1)S(1)}, bf16[1,1,32,256]{3,2,1,0:T(8,128)(2,1)}, u32[]{:S(2)}) copy-start(bf16[1,1,32,256]{3,2,1,0:T(8,128)(2,1)} %get-tuple-element.9) | copy-start | bytes 49156
  266.2 12.4 %all-to-all-start.4 = ((f32[32,4,128]{2,1,0:T(4,128)}), f32[32,4,128]{2,1,0:T(4,128)S(1)}, u32[]{:S(2)}, u32[]{:S(2)}) async-start(f32[32,4,128]{2,1,0:T(4,128)} %broadcast_in_dim.39), calls=%async_computation.4 | async-start | bytes 131072 | tf_op jit(solution)/shard_map/all_to_all | solution.py:58
  279.3 9.9 %all-to-all-start.5 = ((f32[8,4,128]{2,1,0:T(4,128)}), f32[8,4,128]{2,1,0:T(4,128)S(1)}, u32[]{:S(2)}, u32[]{:S(2)}) async-start(f32[8,4,128]{2,1,0:T(4,128)} %broadcast_in_dim.40), calls=%async_computation.5 | async-start | bytes 32768 | tf_op jit(solution)/shard_map/all_to_all | solution.py:58

commit v2 on v1

v2 whole, which is shorter than its diff:
```python
import jax
import jax.numpy as jnp
from jax import lax
from jax.experimental import pallas as pl
from jax.experimental.pallas import tpu as pltpu
from jax.sharding import Mesh, PartitionSpec as P

HD = 128
TOPK = 8
NODES = 32
CAP = 4
EXPERTS = 128
D = 4096
HALF = D // 2

eps_norm = 1e-06
EP = ("x", "z", "y")
TP = "c"
ALL = ("x", "z", "y", "c")
PLANE = ("x", "y")
NZ = 8
NY = 4
NPLANE = 16
LANES = 128
BLOCK = 512
VMEM_LIMIT = 40 << 20
SWAP = [(0, 1), (1, 0)]


def swap(value):
    return lax.ppermute(value, TP, SWAP)


def around(count, step):
    return [(chip, (chip + step) % count) for chip in range(count)]


def exchange(value, axes):
    return lax.all_to_all(value, axes, 0, 0, tiled=True)


def dot32(left, right):
    return jnp.dot(left, right, preferred_element_type=jnp.float32)


def last_dot(left, right):
    return lax.dot_general(
        left, right, (((1,), (1,)), ((), ())), preferred_element_type=jnp.float32
    )


def first_dot(left, right):
    return lax.dot_general(
        left, right, (((0,), (0,)), ((), ())), preferred_element_type=jnp.float32
    )


def iota(shape, dim):
    return lax.broadcasted_iota(jnp.int32, shape, dim)


def as_bf16(mask):
    return mask.astype(jnp.float32).astype(jnp.bfloat16)


def as_column(row):
    count = row.shape[1]
    here = iota((count, count), 0) == iota((count, count), 1)
    return jnp.sum(jnp.where(here, row, 0.0), 1, keepdims=True)


def silu(value):
    return value / (1.0 + jnp.exp(-value))


SMEM = pl.BlockSpec(memory_space=pltpu.SMEM)
ANY = pl.BlockSpec(memory_space=pl.ANY)


def whole(array):
    return pl.BlockSpec(array.shape, lambda *_: (0,) * len(array.shape))


def in_hbm(array):
    return pltpu.with_memory_space_constraint(array, pltpu.HBM)


def like(shape, dtype):
    return jax.ShapeDtypeStruct(shape, dtype)


def call(kernel, scalars, arrays, out_shape, flops=0, moved=1 << 20, unused=(), scratch=()):
    outs = out_shape if isinstance(out_shape, (list, tuple)) else [out_shape]
    count = len(scalars)

    def body(*refs):
        rest = refs[count + len(arrays) + len(unused) :]
        kernel(*refs[: count + len(arrays)], *rest)

    result = pl.pallas_call(
        body,
        out_shape=list(outs),
        in_specs=[SMEM] * count + [whole(a) for a in arrays] + [ANY] * len(unused),
        out_specs=[whole(o) for o in outs],
        scratch_shapes=list(scratch),
        compiler_params=pltpu.CompilerParams(vmem_limit_bytes=VMEM_LIMIT),
        cost_estimate=pl.CostEstimate(flops=flops, bytes_accessed=moved, transcendentals=0),
    )(*scalars, *arrays, *unused)
    return result if isinstance(out_shape, (list, tuple)) else result[0]


def attention_kernel(length, query, new_kv, cache, parents, attended):
    nodes = query.shape[1]
    heads = query.shape[2] // HD
    kv_heads = cache.shape[3] // HD
    group = heads // kv_heads
    shape = (nodes, nodes)
    parent = as_column(parents[...].astype(jnp.float32))
    column = iota(shape, 1).astype(jnp.float32)
    reach = ((column == parent) | (iota(shape, 0) == iota(shape, 1))).astype(jnp.float32)
    for _ in range(5):
        reach = jnp.minimum(dot32(reach.astype(jnp.bfloat16), reach.astype(jnp.bfloat16)), 1.0)
    reach = jnp.concatenate([reach] * group, 0)
    for kv in range(kv_heads):
        here = pl.ds(kv * HD, HD)
        first = kv * group
        rows = [query[0, :, (first + h) * HD : (first + h + 1) * HD] for h in range(group)]
        rows = jnp.concatenate(rows, 0)
        old = last_dot(rows, cache[0, 0, :, here]) * HD ** (-0.5)
        new = last_dot(rows, new_kv[0, 0, :, here]) * HD ** (-0.5)
        old = jnp.where(iota(old.shape, 1) < length[0], old, -jnp.inf)
        new = jnp.where(reach > 0.5, new, -jnp.inf)
        top = jnp.maximum(jnp.max(old, -1, keepdims=True), jnp.max(new, -1, keepdims=True))
        old, new = jnp.exp(old - top), jnp.exp(new - top)
        total = jnp.sum(old, -1, keepdims=True) + jnp.sum(new, -1, keepdims=True)
        mixed = dot32((old / total).astype(jnp.bfloat16), cache[1, 0, :, here])
        mixed = mixed + dot32((new / total).astype(jnp.bfloat16), new_kv[1, 0, :, here])
        mixed = mixed.astype(jnp.bfloat16)
        for h in range(group):
            attended[0, :, (first + h) * HD : (first + h + 1) * HD] = mixed[
                h * nodes : (h + 1) * nodes
            ]


def begin_kernel(accept, hidden, routes, gates, weights, bias, squares, notes, wide):
    rows = hidden[...].astype(jnp.float32)
    squares[...] = jnp.broadcast_to(jnp.sum(rows * rows, -1, keepdims=True), squares.shape)
    share = gates[...] / jnp.sum(gates[...], 0, keepdims=True)
    share_hi = share.astype(jnp.bfloat16).astype(jnp.float32)
    flag = (iota((TOPK, NODES), 1) == accept[0]).astype(jnp.float32)
    stack = [routes[...].astype(jnp.float32), share_hi, share - share_hi, flag]
    stack = jnp.concatenate(stack, 0).astype(jnp.bfloat16)
    places = as_bf16(iota((NODES, LANES), 0) == iota((NODES, LANES), 1))
    notes[...] = first_dot(stack, places).astype(jnp.bfloat16)
    block = weights.shape[1]
    lane = iota((block, LANES), 1)
    for head in range(2):
        wide[head, :, :D] = weights[head]
        value = as_column(bias[head : head + 1, :])
        extra = jnp.zeros((block, LANES), jnp.float32)
        for place in range(3):
            part = value.astype(jnp.bfloat16).astype(jnp.float32)
            extra = jnp.where(lane == place, part, extra)
            value = value - part
        wide[head, :, D:] = extra.astype(jnp.bfloat16)


def assemble_kernel(core, my_y, *refs):
    own, other, weights = refs[:NY], refs[NY], refs[NY + 1]
    block = own[0].shape[1]
    for step in range(NY):
        place = lax.rem(my_y[0] - step + NY, NY) * 2
        for head in range(2):
            here = pl.ds(pl.multiple_of((place + core[0]) * block, block), block)
            weights[head, here, :] = own[step][head]
            here = pl.ds(pl.multiple_of((place + 1 - core[0]) * block, block), block)
            weights[head, here, :] = other[step, head]


def pack_kernel(core, hidden, squares, gain, notes, packet):
    factor = lax.rsqrt(squares[...][:, :1] / D + eps_norm)
    own_gain = jnp.where(core[0] == 0, gain[:HALF], gain[HALF:]).reshape(1, HALF)
    normed = (hidden[...].astype(jnp.float32) * factor * own_gain).astype(jnp.bfloat16)
    for chip in range(NZ):
        packet[chip, :, :HALF] = normed
        packet[chip, :, HALF:] = notes[...]


def route_kernel(my_z, column, outgoing, mix_hi, mix_lo, accepted_mix):
    count = NZ * NODES
    slots = NZ * CAP
    tokens = column[...].reshape(count, HALF + LANES)
    turn = as_bf16(iota((NODES, LANES), 0) == iota((NODES, LANES), 1))
    notes = last_dot(turn, tokens[:, HALF:])
    expert = iota((NPLANE, 1), 0)
    expert = (((expert // 4) * NZ + my_z[0]) * 4 + expert % 4).astype(jnp.float32)
    member = jnp.zeros((NPLANE, count), jnp.float32)
    share_hi, share_lo = member, member
    for pick in range(TOPK):
        match = (notes[pick : pick + 1] == expert).astype(jnp.float32)
        member = member + match
        share_hi = share_hi + match * notes[TOPK + pick : TOPK + pick + 1]
        share_lo = share_lo + match * notes[2 * TOPK + pick : 2 * TOPK + pick + 1]
    first, second = iota((count, count), 0), iota((count, count), 1)
    earlier = (first < second) & (first // NODES == second // NODES)
    rank = dot32(member.astype(jnp.bfloat16), as_bf16(earlier))
    source = iota((1, count), 1) // NODES
    slot = jnp.where(member > 0.5, (source * CAP).astype(jnp.float32) + rank, -1.0)
    wanted = iota((slots, 1), 0).astype(jnp.float32)
    chosen = []
    for place in range(NPLANE):
        one = (slot[place : place + 1] == wanted).astype(jnp.float32)
        here = pl.ds(place * slots, slots)
        mix_hi[here, :] = (one * share_hi[place : place + 1]).astype(jnp.bfloat16)
        mix_lo[here, :] = (one * share_lo[place : place + 1]).astype(jnp.bfloat16)
        chosen.append(one.astype(jnp.bfloat16))
    chosen = jnp.concatenate(chosen, 0)
    for piece in range(HALF // BLOCK):
        here = slice(piece * BLOCK, (piece + 1) * BLOCK)
        part = dot32(chosen, tokens[:, here]).astype(jnp.bfloat16)
        outgoing[:, :, here] = part.reshape(NPLANE, slots, BLOCK)
    flag = notes[3 * TOPK : 3 * TOPK + 1]
    accepted = jnp.where(source == iota((NZ, 1), 0), flag, 0.0).astype(jnp.bfloat16)
    accepted_mix[:NZ] = last_dot(accepted, mix_hi[...]).astype(jnp.bfloat16)
    accepted_mix[NZ:] = last_dot(accepted, mix_lo[...]).astype(jnp.bfloat16)


def half_sums(core, rows, w_gate, w_up):
    here = pl.ds(pl.multiple_of(core * HALF, HALF), HALF)
    rows = rows[...].reshape(-1, HALF)
    return dot32(rows, w_gate[0, here, :]), dot32(rows, w_up[0, here, :])


def first_half_kernel(core, rows, w_gate, w_up, gate, up):
    gate[...], up[...] = half_sums(core[0], rows, w_gate, w_up)


def second_half_kernel(core, rows, w_gate, w_up, gate, up, activation):
    gate_part, up_part = half_sums(1 - core[0], rows, w_gate, w_up)
    activation[...] = (silu(gate[...] + gate_part) * (up[...] + up_part)).astype(jnp.bfloat16)


def down_kernel(core, own, other, down, other_down, finished):
    del core
    rows = jnp.concatenate([own[...], other[...]], 1)
    part = dot32(rows, jnp.concatenate([down[0], other_down[...]], 0))
    finished[...] = part.astype(jnp.bfloat16).reshape(finished.shape)


def down(core, own, other, w_down, other_down, out_shape):
    rows, units = own.shape
    steps = HALF // BLOCK
    column = lambda i, core: (0, i)
    return pl.pallas_call(
        down_kernel,
        out_shape=out_shape,
        grid_spec=pltpu.PrefetchScalarGridSpec(
            num_scalar_prefetch=1,
            grid=(steps,),
            in_specs=[
                pl.BlockSpec((rows, units), lambda i, core: (0, 0)),
                pl.BlockSpec((rows, units), lambda i, core: (0, 0)),
                pl.BlockSpec((1, units, BLOCK), lambda i, core: (0, 0, core[0] * steps + i)),
                pl.BlockSpec((units, BLOCK), column),
            ],
            out_specs=pl.BlockSpec((NPLANE, NZ * CAP, BLOCK), lambda i, core: (0, 0, i)),
        ),
        compiler_params=pltpu.CompilerParams(vmem_limit_bytes=VMEM_LIMIT),
        cost_estimate=pl.CostEstimate(
            flops=4 * rows * HALF * units, bytes_accessed=6 << 20, transcendentals=0
        ),
    )(core, own, other, w_down, other_down)


def accepted_kernel(accept, my_z, mix, returned, hidden, parts):
    part = dot32(mix[...], returned[...].reshape(-1, HALF))
    part = part[:NZ] + part[NZ:]
    here = iota((NODES, 1), 0) == accept[0]
    own = jnp.sum(jnp.where(here, hidden[...].astype(jnp.float32), 0.0), 0, keepdims=True)
    part = part + jnp.where(iota((NZ, 1), 0) == my_z[0], own, 0.0)
    part = part.astype(jnp.bfloat16)
    for place in range(2 * NZ):
        parts[place] = part


def mixture_kernel(my_z, mix_hi, mix_lo, returned, *refs):
    outs, partial = refs[:NZ], refs[NZ]
    rows = returned[...].reshape(-1, HALF)
    partial[...] = first_dot(mix_hi[...], rows) + first_dot(mix_lo[...], rows)
    for step in range(NZ):
        place = lax.rem(my_z[0] + step, NZ)
        block = partial[pl.ds(pl.multiple_of(place * NODES, NODES), NODES), :]
        outs[step][...] = block.astype(outs[step].dtype)


def final_kernel(parts, gain, copies):
    chosen = jnp.sum(parts[...].reshape(NZ, 2, NZ, HALF).astype(jnp.float32), 0)
    chosen = chosen.astype(jnp.bfloat16).astype(jnp.float32)
    squares = jnp.sum(chosen * chosen, -1, keepdims=True)
    factor = lax.rsqrt((squares[0] + squares[1]) / D + eps_norm)
    for half in range(2):
        final = (chosen[half] * factor * gain[half * HALF : (half + 1) * HALF].reshape(1, HALF)).astype(jnp.bfloat16)
        for chip in range(copies.shape[0]):
            copies[chip, :, half * HALF : (half + 1) * HALF] = final


def medusa_kernel(core, tile, final, weights, copies):
    count = 4 * NZ
    shape = (count // 2, count)
    row = iota(shape, 0)
    pick = as_bf16(iota(shape, 1) == row // 4 * NZ + core[0] * 4 + row % 4)
    rows = dot32(pick, final[...].reshape(count, D)).astype(jnp.bfloat16)
    here = pl.ds(pl.multiple_of(tile[0] * LANES, LANES), LANES)
    own = dot32(pick, final[:, :, here].reshape(count, LANES))
    ones = as_bf16(iota((count // 2, LANES), 1) < 3)
    rows = jnp.concatenate([rows, ones], 1)
    heads = [own + silu(last_dot(rows, weights[head])) for head in range(2)]
    heads = jnp.concatenate(heads, 0).astype(jnp.bfloat16)
    for chip in range(NZ):
        copies[chip] = heads


def copy_kernel(heads, copies):
    for chip in range(NPLANE):
        copies[chip] = heads[...]


def head_sums(heads, lm):
    tiles = []
    for x in range(4):
        for z in range(NZ):
            tiles.append(jnp.concatenate([heads[x * NY + y, z] for y in range(NY)], 0))
    return last_dot(lm[...], jnp.concatenate(tiles, 1))


def first_logits_kernel(heads, lm, total):
    total[...] = head_sums(heads, lm)


def logits_kernel(core, heads, lm, before, logits, stats):
    both = jnp.concatenate([before[...], head_sums(heads, lm)], 1)
    shape = (2 * EXPERTS, 2 * EXPERTS)
    lane = iota(shape, 0)
    z = jnp.where(lane < EXPERTS, core[0], 1 - core[0]) * 4 + lane % 4
    wanted = lane // 16 % 2 * EXPERTS + lane // 4 % 4 * 32 + z * 4 + lane // 32 % 4
    order = as_bf16(wanted == iota(shape, 1))
    total = jnp.zeros(both.shape, jnp.float32)
    for _ in range(3):
        part = both.astype(jnp.bfloat16)
        total = total + dot32(part, order)
        both = both - part.astype(jnp.float32)
    top = jnp.max(total, 0, keepdims=True)
    sums = jnp.sum(jnp.exp(total - top), 0, keepdims=True)
    for head in range(2):
        here = slice(head * EXPERTS, (head + 1) * EXPERTS)
        logits[head] = total[:, here]
        for place in range(stats.shape[0]):
            stats[place, head : head + 1, :] = top[:, here]
            stats[place, 2 + head : 3 + head, :] = sums[:, here]


def merged(stats):
    tops, sums = stats[:, :2], stats[:, 2:]
    top = jnp.max(tops, 0)
    return top, jnp.sum(sums * jnp.exp(tops - top[None]), 0)


def merge_kernel(stats, copies):
    top, sums = merged(stats[...])
    for chip in range(NZ):
        copies[chip, :2, :] = top
        copies[chip, 2:, :] = sums


def finish_kernel(stats, logits, logprob):
    top, sums = merged(stats[...])
    shift = top + jnp.log(sums)
    for head in range(2):
        logprob[head] = logits[head] - shift[head : head + 1, :]


def on_device(
    query,
    new_kv,
    cache,
    cache_len,
    parents,
    hidden,
    moe_gain,
    routes,
    gates,
    w_gate,
    w_up,
    w_down,
    accept,
    final_gain,
    medusa_w,
    medusa_b,
    lm_head,
):
    bf16, f32 = jnp.bfloat16, jnp.float32
    core, my_z = lax.axis_index(TP), lax.axis_index("z")
    core_at, z_at, y_at = core.reshape(1), my_z.reshape(1), lax.axis_index("y").reshape(1)
    tile_at = (lax.axis_index("x") * NZ + my_z).reshape(1)
    slots = NPLANE * NZ * CAP
    units = w_gate.shape[2]
    vocab = lm_head.shape[0]

    squares, notes, wide_w = call(
        begin_kernel,
        [accept],
        [in_hbm(array) for array in (hidden, routes.T, gates.T, medusa_w, medusa_b)],
        [
            like((NODES, LANES), f32),
            like((NODES, LANES), bf16),
            like(medusa_w.shape[:2] + (D + LANES,), bf16),
        ],
    )

    packet = call(
        pack_kernel,
        [core_at],
        [in_hbm(hidden), lax.psum(squares, TP), in_hbm(moe_gain), notes],
        pltpu.HBM((NZ, NODES, HALF + LANES), bf16),
    )
    column = exchange(packet, "z")

    attended = call(
        attention_kernel,
        [cache_len],
        [query, new_kv, cache, parents],
        like(query.shape, bf16),
        flops=4 << 24,
        moved=4 << 20,
    )
    wide = [wide_w] + [lax.ppermute(wide_w, "y", around(NY, step)) for step in range(1, NY)]
    block_w = call(
        assemble_kernel,
        [core_at, y_at],
        wide + [swap(jnp.stack(wide))],
        pltpu.HBM((2, LANES, D + LANES), bf16),
        moved=4 << 20,
    )
    other_down = swap(lax.dynamic_slice_in_dim(w_down[0], (1 - core) * HALF, HALF, 1))

    outgoing, mix_hi, mix_lo, accepted_mix = call(
        route_kernel,
        [z_at],
        [column],
        [
            pltpu.VMEM((NPLANE, NZ * CAP, HALF), bf16),
            like((slots, NZ * NODES), bf16),
            like((slots, NZ * NODES), bf16),
            like((2 * NZ, slots), bf16),
        ],
        flops=2 * slots * NZ * NODES * HALF,
        moved=4 << 20,
        unused=[attended, in_hbm(block_w), in_hbm(other_down)],
    )
    arrived = exchange(outgoing, PLANE)
    sums = call(
        first_half_kernel,
        [core_at],
        [arrived, w_gate, w_up],
        [like((slots, units), f32)] * 2,
        flops=4 * slots * HALF * units,
        moved=8 << 20,
    )
    activation = call(
        second_half_kernel,
        [core_at],
        [swap(arrived), w_gate, w_up, *sums],
        like((slots, units), bf16),
        flops=4 * slots * HALF * units,
        moved=8 << 20,
    )
    finished = down(
        core_at,
        activation,
        swap(activation),
        w_down,
        other_down,
        pltpu.VMEM((NPLANE, NZ * CAP, HALF), bf16),
    )
    returned = exchange(finished, PLANE)

    parts = call(
        accepted_kernel,
        [accept, z_at],
        [accepted_mix, returned, hidden],
        pltpu.HBM((2 * NZ, NZ, HALF), bf16),
        flops=4 * NZ * slots * HALF,
        moved=3 << 20,
    )
    parts = exchange(parts, ("z", "c"))
    own, *others = call(
        mixture_kernel,
        [z_at],
        [mix_hi, mix_lo, returned],
        [like((NODES, HALF), f32)] + [like((NODES, HALF), bf16)] * (NZ - 1),
        flops=4 * slots * NZ * NODES * HALF,
        moved=6 << 20,
        scratch=[pltpu.VMEM((NZ * NODES, HALF), f32)],
    )
    sent = {}
    for step, other in enumerate(others, 1):
        sent[step] = lax.ppermute(other, "z", around(NZ, step))

    final = call(
        final_kernel,
        [],
        [parts, in_hbm(final_gain)],
        pltpu.HBM((4, NZ, D), bf16),
        unused=[own],
    )
    final = exchange(final, "x")
    heads = call(
        medusa_kernel,
        [core_at, tile_at],
        [final, block_w],
        pltpu.HBM((NZ, 32, LANES), bf16),
        flops=2 * 16 * D * 256,
        moved=3 << 20,
        unused=[sent[step] for step in (1, 7, 2)],
    )
    heads = exchange(heads, "z")
    heads = call(
        copy_kernel,
        [],
        [heads],
        pltpu.HBM((NPLANE, NZ, 32, LANES), bf16),
        unused=[sent[step] for step in (6, 3, 5, 4)],
    )
    heads = exchange(heads, PLANE)
    total = call(
        first_logits_kernel,
        [],
        [heads, lm_head],
        like((vocab, EXPERTS), f32),
        flops=2 * EXPERTS * D * vocab,
        moved=4 << 20,
    )
    logits, stats = call(
        logits_kernel,
        [core_at],
        [swap(heads), lm_head, total],
        [like((2, vocab, EXPERTS), f32), pltpu.HBM((32, 4, EXPERTS), f32)],
        flops=2 * EXPERTS * D * vocab,
        moved=4 << 20,
    )
    mixture = own
    for other in sent.values():
        mixture = mixture + other.astype(f32)
    layer_out = (hidden.astype(f32) + mixture).astype(bf16)
    stats = exchange(stats, ("x", "y", "c"))
    stats = call(merge_kernel, [], [stats], pltpu.HBM((NZ, 4, EXPERTS), f32))
    stats = exchange(stats, "z")
    logprob = call(finish_kernel, [], [stats, logits], like((2, vocab, EXPERTS), f32))
    return (attended, layer_out, jnp.transpose(logprob, (0, 2, 1)))


def solution(mesh):
    fine = Mesh(mesh.devices.reshape(4, 8, 4, 2), ALL)
    in_specs = (
        P(EP, None, TP),
        P(None, EP, None, TP),
        P(None, EP, None, TP),
        P(EP),
        P(EP, None),
        P(EP, TP),
        P(),
        P(EP, None),
        P(EP, None),
        P(EP, None, TP),
        P(EP, None, TP),
        P(EP, TP, None),
        P(EP),
        P(),
        P(None, ALL, None),
        P(None, ALL),
        P(ALL, None),
    )
    out_specs = (P(EP, None, TP), P(EP, TP), P(None, None, ALL))
    return jax.shard_map(
        on_device, mesh=fine, in_specs=in_specs, out_specs=out_specs, check_vma=False
    )
```

time: 292 us -> 247 us (0.85)
  Pallas kernels: 0 us -> 32.3 us
  waiting for transfers between devices: 77.5 us -> 46.3 us
  local copies, waits for them, and re-layouts: 42.8 us -> 13.5 us
  matrix products: 23.7 us -> 0 us
  starting transfers between devices: 33.7 us -> 45.4 us
  other arithmetic: 14.7 us -> 4.05 us
  blocking collectives: 95.1 us -> 102 us
    all_to_all x4 -> x5, waiting for transfers between devices: 77.1 us -> 22.6 us  [exchange(): return lax.all_to_all(value, axes, 0, 0, tiled=True)]
    pallas_call x0 -> x17, Pallas kernels: none -> 32.3 us  [the longest x16 28.3 us: call(): pl.pallas_call(body, out_shape=list(outs), in_specs=[SMEM] * count + [who...]
    dot_general x16 -> x0, matrix products: 23.7 us -> none  [the longest x7 16.6 us: dot32(): return jnp.dot(left, right, preferred_element_type=jnp.float32)]
    ppermute x0 -> x10, waiting for transfers between devices: none -> 19.4 us  [the longest x7 11 us: on_device(): sent[step] = lax.ppermute(other, 'z', around(NZ, step))]
    reshape x5 -> x0, local copies, waits for them, and re-layouts: 17.9 us -> none  [the longest x1 4.12 us: on_device(): finished = finished.astype(jnp.bfloat16).reshape(EXPERTS, CAP, HALF)]
    ppermute x0 -> x10, starting transfers between devices: none -> 14.6 us  [the longest x7 9.63 us: on_device(): sent[step] = lax.ppermute(other, 'z', around(NZ, step))]
    reduce_sum x10 -> x0, other arithmetic: 9.11 us -> none  [the longest x1 2.21 us: tree_attention(): weight = (expo / jnp.sum(expo, -1, keepdims=True)).astype(jnp.bfloat16)]
    all_to_all x2 -> x4, blocking collectives: 89.8 us -> 95.8 us  [exchange(): return lax.all_to_all(value, axes, 0, 0, tiled=True)]
  transfers between devices with their start and end apart: 9 -> 20, of which waited for: 5 -> 13; matrix products, arithmetic and copies ran while one was open for 10% -> 2% of each run, Pallas kernels for 0% -> 5%
where the time goes in v2:
time: 247 us; the launch traced here: 246 us
  blocking collectives  102 us (41%)
  waiting for transfers between devices  46.3 us (19%)
  starting transfers between devices  45.4 us (18%)
  Pallas kernels  32.3 us (13%)
  local copies, waits for them, and re-layouts  13.5 us (5%)
  other arithmetic  4.05 us (2%)
    all_to_all x4, blocking collectives, exchange(): return lax.all_to_all(value, axes, 0, 0, tiled=True)  95.8 us
    pallas_call x16, Pallas kernels, call(): pl.pallas_call(body, out_shape=list(outs), in_specs=[SMEM] * count + [who...  28.3 us
    all_to_all x5, starting transfers between devices, exchange(): return lax.all_to_all(value, axes, 0, 0, tiled=True)  22.6 us
    all_to_all x5, waiting for transfers between devices, exchange(): return lax.all_to_all(value, axes, 0, 0, tiled=True)  22.6 us
    unnamed x50, local copies, waits for them, and re-layouts  12.2 us
    ppermute x7, waiting for transfers between devices, on_device(): sent[step] = lax.ppermute(other, 'z', around(NZ, step))  11 us
    ppermute x7, starting transfers between devices, on_device(): sent[step] = lax.ppermute(other, 'z', around(NZ, step))  9.63 us
    ppermute x3, waiting for transfers between devices, on_device(): lax.ppermute(wide_w, 'y', around(NY, step))  8.38 us
  transfers between devices with their start and end apart: 20, of which 13 were waited for; matrix products, arithmetic and copies ran while one was open for 2% of the time, Pallas kernels for 5%

profile of v2, /device:TPU:1, one launch (start us, length us, event | category | flops | bytes accessed | tf_op | source)
XLA Modules:
  0.0 245.9 jit_solution(15943029360405310461)
XLA Ops:
  2.5 6.4 %psum.7.refs_2_ = f32[32,128]{1,0:T(8,128)S(1)} all-reduce(f32[32,128]{1,0:T(8,128)S(1)} %get-tuple-element.22), channel_id=1, replica_groups=mesh['x'=4,'z'=8,'y'=4,'c'=2] {'c'}, use_global_device_ids=true, to_apply=%region_0.0 | all-reduce | flops 4096 | bytes 32768 | tf_op jit(solution)/shard_map/psum | solution.py:423
  8.9 2.2 shard_map.186
  11.1 6.4 %all-to-all-start = ((bf16[8,32,2176]{2,1,0:T(8,128)(2,1)}), bf16[8,32,2176]{2,1,0:T(8,128)(2,1)}, u32[]{:S(2)}, u32[]{:S(2)}) async-start(bf16[8,32,2176]{2,1,0:T(8,128)(2,1)} %shard_map.186), calls=%async_computation | async-start | bytes 2228224 | tf_op jit(solution)/shard_map/all_to_all | solution.py:39
  18.9 2.6 %collective-permute-start.1 = (bf16[2,16,4224]{2,1,0:T(8,128)(2,1)S(1)}, bf16[2,16,4224]{2,1,0:T(8,128)(2,1)}, u32[]{:S(2)}, u32[]{:S(2)}) collective-permute-start(bf16[2,16,4224]{2,1,0:T(8,128)(2,1)S(1)} %get-tuple-element.24.refs_2_), channel_id=1, source_target_pairs={{0,4},{2,6},{4,0},{6,2},{1,5},{3,7},{5,1},{7,3},{8,12},{10,14},{12... | collective-permute-start | bytes 811016 | tf_op jit(solution)/shard_map/ppermute | solution.py:436
  26.6 6.9 %collective-permute-done.1.refs_4_ = bf16[2,16,4224]{2,1,0:T(8,128)(2,1)} collective-permute-done((bf16[2,16,4224]{2,1,0:T(8,128)(2,1)S(1)}, bf16[2,16,4224]{2,1,0:T(8,128)(2,1)}, u32[]{:S(2)}, u32[]{:S(2)}) %collective-permute-start.1) | collective-permute-done | bytes 270368 | tf_op jit(solution)/shard_map/ppermute | solution.py:436
  33.5 2.3 pad_maximum_fusion
  39.5 2.1 shard_map.184.refs_2_
  41.7 3.0 %shard_map.187.refs_3_ = bf16[2,128,4224]{2,1,0:T(8,128)(2,1)} custom-call(s32[1]{0:T(128)} %bitcast.1.refs_0_.core, s32[1]{0:T(128)} %bitcast.4.refs_1_, bf16[2,16,4224]{2,1,0:T(8,128)(2,1)S(1)} %get-tuple-element.24.refs_2_, bf16[2,16,4224]{2,1,0:T(8,128)(2,1)} %collective-permute-done.refs_3_, bf16[2,16,4224]{2,1,0:T(8,128)(2,1)} %collective-permute-done.1.refs_4_, ...), custom_call_target="tpu_custom_call" | custom-call | bytes 4194304 | tf_op jit(solution)/shard_map/pallas_call | solution.py:100
  44.7 3.7 %all-to-all-done.refs_1_ = bf16[8,32,2176]{2,1,0:T(8,128)(2,1)} async-done(((bf16[8,32,2176]{2,1,0:T(8,128)(2,1)}), bf16[8,32,2176]{2,1,0:T(8,128)(2,1)}, u32[]{:S(2)}, u32[]{:S(2)}) %all-to-all-start) | async-done | bytes 1114144 | tf_op jit(solution)/shard_map/all_to_all | solution.py:39
  49.3 2.5 %shard_map.188 = (bf16[16,32,2048]{2,1,0:T(8,128)(2,1)S(1)}, bf16[512,256]{1,0:T(8,128)(2,1)S(1)}, bf16[512,256]{1,0:T(8,128)(2,1)S(1)}, bf16[16,512]{1,0:T(8,128)(2,1)S(1)}) custom-call(s32[1]{0:T(128)} %bitcast.refs_0_.refs_1_, bf16[8,32,2176]{2,1,0:T(8,128)(2,1)} %all-to-all-done.refs_1_, bf16[1,32,4096]{2,1,0:T(8,128)(2,1)S(1)} %copy-done.8, ...), custom_call_target="tpu_custom_call" | custom-call | flops 536870912 | bytes 4194304 | tf_op jit(solution)/shard_map/pallas_call | solution.py:100
  53.2 34.0 %all_to_all.45.refs_1_ = bf16[16,32,2048]{2,1,0:T(8,128)(2,1)S(1)} all-to-all(bf16[16,32,2048]{2,1,0:T(8,128)(2,1)S(1)} %get-tuple-element.27), channel_id=1, replica_groups=mesh['x'=4,'z'=8,'y'=4,'c'=2] {'x','y'}, dimensions={0} | all-to-all | bytes 4194304 | tf_op jit(solution)/shard_map/all_to_all | solution.py:39
  87.2 2.0 collective-permute-start.5
  89.3 2.3 shard_map.189
  93.0 2.4 shard_map.190.own
  97.2 3.9 %shard_map.191 = bf16[16,32,2048]{2,1,0:T(8,128)(2,1)S(1)} custom-call(s32[1]{0:T(128)} %bitcast.1.refs_0_.core, bf16[512,384]{1,0:T(8,128)(2,1)S(1)} %shard_map.190.own, bf16[512,384]{1,0:T(8,128)(2,1)S(1)} %collective-permute-done.6.other, bf16[1,384,4096]{2,1,0:T(8,128)(2,1)S(1)} %copy-done.6, bf16[384,2048]{1,0:T(8,128)(2,1)} %collective-permute-done.4.refs_4_.other_down), custom_call_target="tpu_custom_call" | custom-call | flops 1610612736 | bytes 6291456 | tf_op jit(solution)/shard_map/pallas_call | solution.py:254
  101.2 30.7 %all_to_all.46.refs_3_ = bf16[16,32,2048]{2,1,0:T(8,128)(2,1)S(1)} all-to-all(bf16[16,32,2048]{2,1,0:T(8,128)(2,1)S(1)} %shard_map.191), channel_id=1, replica_groups=mesh['x'=4,'z'=8,'y'=4,'c'=2] {'x','y'}, dimensions={0} | all-to-all | bytes 4194304 | tf_op jit(solution)/shard_map/all_to_all | solution.py:39
  134.4 5.4 %all-to-all-start.3 = ((bf16[16,8,2048]{2,1,0:T(8,128)(2,1)}), bf16[16,8,2048]{2,1,0:T(8,128)(2,1)S(1)}, u32[]{:S(2)}, u32[]{:S(2)}) async-start(bf16[16,8,2048]{2,1,0:T(8,128)(2,1)} %shard_map.193), calls=%async_computation.3 | async-start | bytes 1048576 | tf_op jit(solution)/shard_map/all_to_all | solution.py:39
  142.4 2.1 shard_map.192
  146.5 10.7 %all-to-all-done.3.refs_0_ = bf16[16,8,2048]{2,1,0:T(8,128)(2,1)S(1)} async-done(((bf16[16,8,2048]{2,1,0:T(8,128)(2,1)}), bf16[16,8,2048]{2,1,0:T(8,128)(2,1)S(1)}, u32[]{:S(2)}, u32[]{:S(2)}) %all-to-all-start.3) | async-done | bytes 524320 | tf_op jit(solution)/shard_map/all_to_all | solution.py:39
  158.9 3.4 %all-to-all-start.4 = ((bf16[4,8,4096]{2,1,0:T(8,128)(2,1)}), bf16[4,8,4096]{2,1,0:T(8,128)(2,1)S(1)}, u32[]{:S(2)}, u32[]{:S(2)}) async-start(bf16[4,8,4096]{2,1,0:T(8,128)(2,1)} %shard_map.194), calls=%async_computation.4 | async-start | bytes 524288 | tf_op jit(solution)/shard_map/all_to_all | solution.py:39
  163.9 3.6 %collective-permute-start.12 = (bf16[32,2048]{1,0:T(8,128)(2,1)}, bf16[32,2048]{1,0:T(8,128)(2,1)S(1)}, u32[]{:S(2)}, u32[]{:S(2)}) collective-permute-start(bf16[32,2048]{1,0:T(8,128)(2,1)} %get-tuple-element.36), channel_id=1, source_target_pairs={{0,48},{8,56},{16,0},{24,8},{32,16},{40,24},{48,32},{56,40},{1,49}... | collective-permute-start | bytes 393224 | tf_op jit(solution)/shard_map/ppermute | solution.py:507
  168.3 3.3 %collective-permute-start.10 = (bf16[32,2048]{1,0:T(8,128)(2,1)}, bf16[32,2048]{1,0:T(8,128)(2,1)S(1)}, u32[]{:S(2)}, u32[]{:S(2)}) collective-permute-start(bf16[32,2048]{1,0:T(8,128)(2,1)} %copy-done.22), channel_id=1, source_target_pairs={{0,32},{8,40},{16,48},{24,56},{32,0},{40,8},{48,16},{56,24},{1,33}... | collective-permute-start | bytes 393224 | tf_op jit(solution)/shard_map/ppermute | solution.py:507
  173.4 5.6 %collective-permute-done.7.refs_4_ = bf16[32,2048]{1,0:T(8,128)(2,1)} collective-permute-done((bf16[32,2048]{1,0:T(8,128)(2,1)}, bf16[32,2048]{1,0:T(8,128)(2,1)}, u32[]{:S(2)}, u32[]{:S(2)}) %collective-permute-start.7) | collective-permute-done | bytes 131104 | tf_op jit(solution)/shard_map/ppermute | solution.py:507
  181.3 4.0 %all-to-all-start.5 = ((bf16[8,32,128]{2,1,0:T(8,128)(2,1)}), bf16[8,32,128]{2,1,0:T(8,128)(2,1)}, u32[]{:S(2)}, u32[]{:S(2)}) async-start(bf16[8,32,128]{2,1,0:T(8,128)(2,1)} %shard_map.195), calls=%async_computation.5 | async-start | bytes 131072 | tf_op jit(solution)/shard_map/all_to_all | solution.py:39
  185.3 2.6 %collective-permute-done.11.refs_3_ = bf16[32,2048]{1,0:T(8,128)(2,1)S(1)} collective-permute-done((bf16[32,2048]{1,0:T(8,128)(2,1)}, bf16[32,2048]{1,0:T(8,128)(2,1)S(1)}, u32[]{:S(2)}, u32[]{:S(2)}) %collective-permute-start.11) | collective-permute-done | bytes 131104 | tf_op jit(solution)/shard_map/ppermute | solution.py:507
  188.0 2.1 collective-permute-done.9.refs_2_
  190.0 3.3 %all-to-all-done.5.refs_0_ = bf16[8,32,128]{2,1,0:T(8,128)(2,1)} async-done(((bf16[8,32,128]{2,1,0:T(8,128)(2,1)}), bf16[8,32,128]{2,1,0:T(8,128)(2,1)}, u32[]{:S(2)}, u32[]{:S(2)}) %all-to-all-start.5) | async-done | bytes 65568 | tf_op jit(solution)/shard_map/all_to_all | solution.py:39
  195.3 19.7 %all_to_all.47.refs_0_ = bf16[16,8,32,128]{3,2,1,0:T(8,128)(2,1)S(1)} all-to-all(bf16[16,8,32,128]{3,2,1,0:T(8,128)(2,1)} %shard_map.196), channel_id=1, replica_groups=mesh['x'=4,'z'=8,'y'=4,'c'=2] {'x','y'}, dimensions={0} | all-to-all | bytes 2097152 | tf_op jit(solution)/shard_map/all_to_all | solution.py:39
  215.0 3.2 %collective-permute-start.14 = (bf16[16,8,32,128]{3,2,1,0:T(8,128)(2,1)S(1)}, bf16[16,8,32,128]{3,2,1,0:T(8,128)(2,1)S(1)}, u32[]{:S(2)}, u32[]{:S(2)}) collective-permute-start(bf16[16,8,32,128]{3,2,1,0:T(8,128)(2,1)S(1)} %all_to_all.47.refs_0_), channel_id=1, source_target_pairs={{0,1},{1,0},{2,3},{3,2},{4,5},{5,4},{6,7},{7,6},{8,9},{9,8},{10,11... | collective-permute-start | bytes 3145736 | tf_op jit(solution)/shard_map/ppermute | solution.py:31
  223.1 11.5 %all_to_all.48.refs_0_ = f32[32,4,128]{2,1,0:T(4,128)S(1)} all-to-all(f32[32,4,128]{2,1,0:T(4,128)} %get-tuple-element.39), channel_id=1, replica_groups=mesh['x'=4,'z'=8,'y'=4,'c'=2] {'x','y','c'}, dimensions={0} | all-to-all | bytes 131072 | tf_op jit(solution)/shard_map/all_to_all | solution.py:39
  235.3 3.3 %all-to-all-start.8 = ((f32[8,4,128]{2,1,0:T(4,128)}), f32[8,4,128]{2,1,0:T(4,128)S(1)}, u32[]{:S(2)}, u32[]{:S(2)}) async-start(f32[8,4,128]{2,1,0:T(4,128)} %shard_map.199), calls=%async_computation.8 | async-start | bytes 32768 | tf_op jit(solution)/shard_map/all_to_all | solution.py:39
  240.4 4.8 %all-to-all-done.8.refs_0_ = f32[8,4,128]{2,1,0:T(4,128)S(1)} async-done(((f32[8,4,128]{2,1,0:T(4,128)}), f32[8,4,128]{2,1,0:T(4,128)S(1)}, u32[]{:S(2)}, u32[]{:S(2)}) %all-to-all-start.8) | async-done | bytes 16416 | tf_op jit(solution)/shard_map/all_to_all | solution.py:39
  (83 shorter events, 41.7 us)
Async XLA Ops:
  8.9 13.7 %copy-start.6 = (bf16[1,384,4096]{2,1,0:T(8,128)(2,1)S(1)}, bf16[1,384,4096]{2,1,0:T(8,128)(2,1)}, u32[]{:S(2)}) copy-start(bf16[1,384,4096]{2,1,0:T(8,128)(2,1)} %down.1) | copy-start | bytes 9437188
  11.1 37.3 %all-to-all-start = ((bf16[8,32,2176]{2,1,0:T(8,128)(2,1)}), bf16[8,32,2176]{2,1,0:T(8,128)(2,1)}, u32[]{:S(2)}, u32[]{:S(2)}) async-start(bf16[8,32,2176]{2,1,0:T(8,128)(2,1)} %shard_map.186), calls=%async_computation | async-start | bytes 2228224 | tf_op jit(solution)/shard_map/all_to_all | solution.py:39
  17.6 9.0 %collective-permute-start = (bf16[2,16,4224]{2,1,0:T(8,128)(2,1)S(1)}, bf16[2,16,4224]{2,1,0:T(8,128)(2,1)}, u32[]{:S(2)}, u32[]{:S(2)}) collective-permute-start(bf16[2,16,4224]{2,1,0:T(8,128)(2,1)S(1)} %get-tuple-element.24.refs_2_), channel_id=1, source_target_pairs={{0,2},{2,4},{4,6},{6,0},{1,3},{3,5},{5,7},{7,1},{8,10},{10,12},{12... | collective-permute-start | bytes 811016 | tf_op jit(solution)/shard_map/ppermute | solution.py:436
  18.9 14.7 %collective-permute-start.1 = (bf16[2,16,4224]{2,1,0:T(8,128)(2,1)S(1)}, bf16[2,16,4224]{2,1,0:T(8,128)(2,1)}, u32[]{:S(2)}, u32[]{:S(2)}) collective-permute-start(bf16[2,16,4224]{2,1,0:T(8,128)(2,1)S(1)} %get-tuple-element.24.refs_2_), channel_id=1, source_target_pairs={{0,4},{2,6},{4,0},{6,2},{1,5},{3,7},{5,1},{7,3},{8,12},{10,14},{12... | collective-permute-start | bytes 811016 | tf_op jit(solution)/shard_map/ppermute | solution.py:436
  21.5 12.0 %collective-permute-start.2 = (bf16[2,16,4224]{2,1,0:T(8,128)(2,1)S(1)}, bf16[2,16,4224]{2,1,0:T(8,128)(2,1)}, u32[]{:S(2)}, u32[]{:S(2)}) collective-permute-start(bf16[2,16,4224]{2,1,0:T(8,128)(2,1)S(1)} %get-tuple-element.24.refs_2_), channel_id=1, source_target_pairs={{0,6},{2,0},{4,2},{6,4},{1,7},{3,1},{5,3},{7,5},{8,14},{10,8},{12,... | collective-permute-start | bytes 811016 | tf_op jit(solution)/shard_map/ppermute | solution.py:436
  23.9 13.9 %copy-start.14 = (bf16[2,1,128,256]{3,2,1,0:T(8,128)(2,1)S(1)}, bf16[2,1,128,256]{3,2,1,0:T(8,128)(2,1)}, u32[]{:S(2)}) copy-start(bf16[2,1,128,256]{3,2,1,0:T(8,128)(2,1)} %refs_3_.4) | copy-start | bytes 393220
  23.9 13.9 %copy-start.16 = (s32[1,32]{1,0:T(1,128)S(1)}, s32[1,32]{1,0:T(1,128)}, u32[]{:S(2)}) copy-start(s32[1,32]{1,0:T(1,128)} %refs_4_.3) | copy-start | bytes 388
  23.9 20.8 %collective-permute-start.4 = (bf16[384,2048]{1,0:T(8,128)(2,1)}, bf16[384,2048]{1,0:T(8,128)(2,1)}, u32[]{:S(2)}, u32[]{:S(2)}) collective-permute-start(bf16[384,2048]{1,0:T(8,128)(2,1)} %dynamic-slice_bitcast_fusion), channel_id=1, source_target_pairs={{0,1},{1,0},{2,3},{3,2},{4,5},{5,4},{6,7},{7,6},{8,9},{9,8},{10,11... | collective-permute-start | bytes 4718600 | tf_op jit(solution)/shard_map/ppermute | solution.py:31
  35.8 5.8 %collective-permute-start.3 = (bf16[4,2,16,4224]{3,2,1,0:T(8,128)(2,1)}, bf16[4,2,16,4224]{3,2,1,0:T(8,128)(2,1)}, u32[]{:S(2)}, u32[]{:S(2)}) collective-permute-start(bf16[4,2,16,4224]{3,2,1,0:T(8,128)(2,1)} %pad_maximum_fusion), channel_id=1, source_target_pairs={{0,1},{1,0},{2,3},{3,2},{4,5},{5,4},{6,7},{7,6},{8,9},{9,8},{10,11... | collective-permute-start | bytes 3244040 | tf_op jit(solution)/shard_map/ppermute | solution.py:31
  49.3 39.9 %copy-start.2 = (bf16[1,4096,384]{2,1,0:T(8,128)(2,1)S(1)}, bf16[1,4096,384]{2,1,0:T(8,128)(2,1)}, u32[]{:S(2)}) copy-start(bf16[1,4096,384]{2,1,0:T(8,128)(2,1)} %refs_3_.7) | copy-start | bytes 9437188
  53.2 36.0 %copy-start.1 = (bf16[1,4096,384]{2,1,0:T(8,128)(2,1)S(1)}, bf16[1,4096,384]{2,1,0:T(8,128)(2,1)}, u32[]{:S(2)}) copy-start(bf16[1,4096,384]{2,1,0:T(8,128)(2,1)} %refs_2_.6) | copy-start | bytes 9437188
  87.2 5.8 %collective-permute-start.5 = (bf16[16,32,2048]{2,1,0:T(8,128)(2,1)S(1)}, bf16[16,32,2048]{2,1,0:T(8,128)(2,1)S(1)}, u32[]{:S(2)}, u32[]{:S(2)}) collective-permute-start(bf16[16,32,2048]{2,1,0:T(8,128)(2,1)S(1)} %all_to_all.45.refs_1_), channel_id=1, source_target_pairs={{0,1},{1,0},{2,3},{3,2},{4,5},{5,4},{6,7},{7,6},{8,9},{9,8},{10,11... | collective-permute-start | bytes 6291464 | tf_op jit(solution)/shard_map/ppermute | solution.py:31
  95.4 1.8 collective-permute-start.6
  101.2 30.7 %copy-start.7 = (bf16[32,2048]{1,0:T(8,128)(2,1)S(1)}, bf16[32,2048]{1,0:T(8,128)(2,1)}, u32[]{:S(2)}) copy-start(bf16[32,2048]{1,0:T(8,128)(2,1)} %refs_4_.5) | copy-start | bytes 393220
  131.9 8.0 %copy-start.18 = (bf16[512,256]{1,0:T(8,128)(2,1)S(1)}, bf16[512,256]{1,0:T(8,128)(2,1)}, u32[]{:S(2)}) copy-start(bf16[512,256]{1,0:T(8,128)(2,1)} %copy-done.17) | copy-start | bytes 786436
  134.4 22.8 %all-to-all-start.3 = ((bf16[16,8,2048]{2,1,0:T(8,128)(2,1)}), bf16[16,8,2048]{2,1,0:T(8,128)(2,1)S(1)}, u32[]{:S(2)}, u32[]{:S(2)}) async-start(bf16[16,8,2048]{2,1,0:T(8,128)(2,1)} %shard_map.193), calls=%async_computation.3 | async-start | bytes 1048576 | tf_op jit(solution)/shard_map/all_to_all | solution.py:39
  139.9 1.6 copy-start.5
  142.4 36.5 %copy-start = (bf16[2,128,4224]{2,1,0:T(8,128)(2,1)S(1)}, bf16[2,128,4224]{2,1,0:T(8,128)(2,1)}, u32[]{:S(2)}) copy-start(bf16[2,128,4224]{2,1,0:T(8,128)(2,1)} %shard_map.187.refs_3_) | copy-start | bytes 6488068
  157.2 5.1 %copy-start.24 = (bf16[32,2048]{1,0:T(8,128)(2,1)S(1)}, bf16[32,2048]{1,0:T(8,128)(2,1)}, u32[]{:S(2)}) copy-start(bf16[32,2048]{1,0:T(8,128)(2,1)} %copy-done.23) | copy-start | bytes 393220
  158.9 20.1 %all-to-all-start.4 = ((bf16[4,8,4096]{2,1,0:T(8,128)(2,1)}), bf16[4,8,4096]{2,1,0:T(8,128)(2,1)S(1)}, u32[]{:S(2)}, u32[]{:S(2)}) async-start(bf16[4,8,4096]{2,1,0:T(8,128)(2,1)} %shard_map.194), calls=%async_computation.4 | async-start | bytes 524288 | tf_op jit(solution)/shard_map/all_to_all | solution.py:39
  162.3 6.0 %collective-permute-start.13 = (bf16[32,2048]{1,0:T(8,128)(2,1)S(1)}, bf16[32,2048]{1,0:T(8,128)(2,1)S(1)}, u32[]{:S(2)}, u32[]{:S(2)}) collective-permute-start(bf16[32,2048]{1,0:T(8,128)(2,1)S(1)} %copy-done.24), channel_id=1, source_target_pairs={{0,56},{8,0},{16,8},{24,16},{32,24},{40,32},{48,40},{56,48},{1,57}... | collective-permute-start | bytes 393224 | tf_op jit(solution)/shard_map/ppermute | solution.py:507
  162.4 10.0 %collective-permute-start.8 = (bf16[32,2048]{1,0:T(8,128)(2,1)}, bf16[32,2048]{1,0:T(8,128)(2,1)S(1)}, u32[]{:S(2)}, u32[]{:S(2)}) collective-permute-start(bf16[32,2048]{1,0:T(8,128)(2,1)} %get-tuple-element.32), channel_id=1, source_target_pairs={{0,16},{8,24},{16,32},{24,40},{32,48},{40,56},{48,0},{56,8},{1,17}... | collective-permute-start | bytes 393224 | tf_op jit(solution)/shard_map/ppermute | solution.py:507
  162.5 16.5 %collective-permute-start.7 = (bf16[32,2048]{1,0:T(8,128)(2,1)}, bf16[32,2048]{1,0:T(8,128)(2,1)}, u32[]{:S(2)}, u32[]{:S(2)}) collective-permute-start(bf16[32,2048]{1,0:T(8,128)(2,1)} %get-tuple-element.31), channel_id=1, source_target_pairs={{0,8},{8,16},{16,24},{24,32},{32,40},{40,48},{48,56},{56,0},{1,9},... | collective-permute-start | bytes 393224 | tf_op jit(solution)/shard_map/ppermute | solution.py:507
  163.9 21.4 %collective-permute-start.12 = (bf16[32,2048]{1,0:T(8,128)(2,1)}, bf16[32,2048]{1,0:T(8,128)(2,1)S(1)}, u32[]{:S(2)}, u32[]{:S(2)}) collective-permute-start(bf16[32,2048]{1,0:T(8,128)(2,1)} %get-tuple-element.36), channel_id=1, source_target_pairs={{0,48},{8,56},{16,0},{24,8},{32,16},{40,24},{48,32},{56,40},{1,49}... | collective-permute-start | bytes 393224 | tf_op jit(solution)/shard_map/ppermute | solution.py:507
  167.4 20.5 %collective-permute-start.11 = (bf16[32,2048]{1,0:T(8,128)(2,1)}, bf16[32,2048]{1,0:T(8,128)(2,1)S(1)}, u32[]{:S(2)}, u32[]{:S(2)}) collective-permute-start(bf16[32,2048]{1,0:T(8,128)(2,1)} %get-tuple-element.35), channel_id=1, source_target_pairs={{0,40},{8,48},{16,56},{24,0},{32,8},{40,16},{48,24},{56,32},{1,41}... | collective-permute-start | bytes 393224 | tf_op jit(solution)/shard_map/ppermute | solution.py:507
  168.3 19.6 %collective-permute-start.10 = (bf16[32,2048]{1,0:T(8,128)(2,1)}, bf16[32,2048]{1,0:T(8,128)(2,1)S(1)}, u32[]{:S(2)}, u32[]{:S(2)}) collective-permute-start(bf16[32,2048]{1,0:T(8,128)(2,1)} %copy-done.22), channel_id=1, source_target_pairs={{0,32},{8,40},{16,48},{24,56},{32,0},{40,8},{48,16},{56,24},{1,33}... | collective-permute-start | bytes 393224 | tf_op jit(solution)/shard_map/ppermute | solution.py:507
  173.0 17.0 %collective-permute-start.9 = (bf16[32,2048]{1,0:T(8,128)(2,1)}, bf16[32,2048]{1,0:T(8,128)(2,1)S(1)}, u32[]{:S(2)}, u32[]{:S(2)}) collective-permute-start(bf16[32,2048]{1,0:T(8,128)(2,1)} %copy-done.21), channel_id=1, source_target_pairs={{0,24},{8,32},{16,40},{24,48},{32,56},{40,0},{48,8},{56,16},{1,25}... | collective-permute-start | bytes 393224 | tf_op jit(solution)/shard_map/ppermute | solution.py:507
  181.3 12.0 %all-to-all-start.5 = ((bf16[8,32,128]{2,1,0:T(8,128)(2,1)}), bf16[8,32,128]{2,1,0:T(8,128)(2,1)}, u32[]{:S(2)}, u32[]{:S(2)}) async-start(bf16[8,32,128]{2,1,0:T(8,128)(2,1)} %shard_map.195), calls=%async_computation.5 | async-start | bytes 131072 | tf_op jit(solution)/shard_map/all_to_all | solution.py:39
  185.3 32.9 %copy-start.3 = (bf16[304,4096]{1,0:T(8,128)(2,1)S(1)}, bf16[304,4096]{1,0:T(8,128)(2,1)}, u32[]{:S(2)}) copy-start(bf16[304,4096]{1,0:T(8,128)(2,1)} %refs_2_.7) | copy-start | bytes 7471108
  215.0 5.4 %collective-permute-start.14 = (bf16[16,8,32,128]{3,2,1,0:T(8,128)(2,1)S(1)}, bf16[16,8,32,128]{3,2,1,0:T(8,128)(2,1)S(1)}, u32[]{:S(2)}, u32[]{:S(2)}) collective-permute-start(bf16[16,8,32,128]{3,2,1,0:T(8,128)(2,1)S(1)} %all_to_all.47.refs_0_), channel_id=1, source_target_pairs={{0,1},{1,0},{2,3},{3,2},{4,5},{5,4},{6,7},{7,6},{8,9},{9,8},{10,11... | collective-permute-start | bytes 3145736 | tf_op jit(solution)/shard_map/ppermute | solution.py:31
  223.1 22.0 %copy-start.12 = (f32[2,304,128]{2,1,0:T(8,128)S(1)}, f32[2,304,128]{2,1,0:T(8,128)}, u32[]{:S(2)}) copy-start(f32[2,304,128]{2,1,0:T(8,128)} %copy-done.11) | copy-start | bytes 933892
  235.3 9.9 %all-to-all-start.8 = ((f32[8,4,128]{2,1,0:T(4,128)}), f32[8,4,128]{2,1,0:T(4,128)S(1)}, u32[]{:S(2)}, u32[]{:S(2)}) async-start(f32[8,4,128]{2,1,0:T(4,128)} %shard_map.199), calls=%async_computation.8 | async-start | bytes 32768 | tf_op jit(solution)/shard_map/all_to_all | solution.py:39
  (13 other events, 10.6 us)

commit v3 on v2

--- a/solution.py
+++ b/solution.py
@@ -83,6 +83,10 @@
 
 def in_hbm(array):
     return pltpu.with_memory_space_constraint(array, pltpu.HBM)
+
+
+def in_vmem(array):
+    return pltpu.with_memory_space_constraint(array, pltpu.VMEM)
 
 
 def like(shape, dtype):
@@ -272,48 +276,57 @@
     )(core, own, other, w_down, other_down)
 
 
-def accepted_kernel(accept, my_z, mix, returned, hidden, parts):
-    part = dot32(mix[...], returned[...].reshape(-1, HALF))
+def combine_kernel(accept, my_z, mix, mix_hi, mix_lo, returned, hidden, parts, *refs):
+    outs, partial = refs[:NZ], refs[NZ]
+    rows = returned[...].reshape(-1, HALF)
+    part = dot32(mix[...], rows)
     part = part[:NZ] + part[NZ:]
     here = iota((NODES, 1), 0) == accept[0]
     own = jnp.sum(jnp.where(here, hidden[...].astype(jnp.float32), 0.0), 0, keepdims=True)
     part = part + jnp.where(iota((NZ, 1), 0) == my_z[0], own, 0.0)
-    part = part.astype(jnp.bfloat16)
-    for place in range(2 * NZ):
-        parts[place] = part
-
-
-def mixture_kernel(my_z, mix_hi, mix_lo, returned, *refs):
-    outs, partial = refs[:NZ], refs[NZ]
-    rows = returned[...].reshape(-1, HALF)
+    quarter = HALF // 2
+    for core in range(2):
+        four = part[core * 4 : core * 4 + 4]
+        four = jnp.concatenate([four[:, :quarter], four[:, quarter:]], 0).astype(jnp.bfloat16)
+        for chip in range(NZ):
+            parts[chip * 2 + core] = four
     partial[...] = first_dot(mix_hi[...], rows) + first_dot(mix_lo[...], rows)
-    for step in range(NZ):
+    for step, out in enumerate(outs):
         place = lax.rem(my_z[0] + step, NZ)
         block = partial[pl.ds(pl.multiple_of(place * NODES, NODES), NODES), :]
-        outs[step][...] = block.astype(outs[step].dtype)
+        out[...] = block.astype(out.dtype)
 
 
 def final_kernel(parts, gain, copies):
-    chosen = jnp.sum(parts[...].reshape(NZ, 2, NZ, HALF).astype(jnp.float32), 0)
+    quarter = parts.shape[2]
+    chosen = jnp.sum(parts[...].reshape(NZ, 2, 8, quarter).astype(jnp.float32), 0)
     chosen = chosen.astype(jnp.bfloat16).astype(jnp.float32)
-    squares = jnp.sum(chosen * chosen, -1, keepdims=True)
-    factor = lax.rsqrt((squares[0] + squares[1]) / D + eps_norm)
-    for half in range(2):
-        final = (chosen[half] * factor * gain[half * HALF : (half + 1) * HALF].reshape(1, HALF)).astype(jnp.bfloat16)
+    squares = jnp.sum(jnp.sum(chosen * chosen, -1, keepdims=True), 0)
+    squares = squares + jnp.concatenate([squares[4:], squares[:4]], 0)
+    factor = lax.rsqrt(squares / D + eps_norm)
+    first = iota((8, 1), 0) < 4
+    for core in range(2):
+        low = gain[core * HALF : core * HALF + quarter].reshape(1, quarter)
+        high = gain[core * HALF + quarter : (core + 1) * HALF].reshape(1, quarter)
+        final = (chosen[core] * factor * jnp.where(first, low, high)).astype(jnp.bfloat16)
         for chip in range(copies.shape[0]):
-            copies[chip, :, half * HALF : (half + 1) * HALF] = final
-
-
-def medusa_kernel(core, tile, final, weights, copies):
-    count = 4 * NZ
-    shape = (count // 2, count)
+            copies[chip, core * 8 : (core + 1) * 8, :] = final
+
+
+def medusa_kernel(tile, final, weights, copies):
+    count, quarter = final.shape[0] * final.shape[1], final.shape[2]
+    shape = (count // 4, count)
     row = iota(shape, 0)
-    pick = as_bf16(iota(shape, 1) == row // 4 * NZ + core[0] * 4 + row % 4)
-    rows = dot32(pick, final[...].reshape(count, D)).astype(jnp.bfloat16)
-    here = pl.ds(pl.multiple_of(tile[0] * LANES, LANES), LANES)
-    own = dot32(pick, final[:, :, here].reshape(count, LANES))
-    ones = as_bf16(iota((count // 2, LANES), 1) < 3)
-    rows = jnp.concatenate([rows, ones], 1)
+
+    def pick(part):
+        return as_bf16(iota(shape, 1) == row // 4 * 16 + part * 4 + row % 4)
+
+    pieces = final[...].reshape(count, quarter)
+    rows = [dot32(pick(part), pieces).astype(jnp.bfloat16) for part in range(4)]
+    here = pl.ds(pl.multiple_of(tile[0] % NZ * LANES, LANES), LANES)
+    own = dot32(pick(tile[0] // NZ), final[:, :, here].reshape(count, LANES))
+    rows.append(as_bf16(iota((count // 4, LANES), 1) < 3))
+    rows = jnp.concatenate(rows, 1)
     heads = [own + silu(last_dot(rows, weights[head])) for head in range(2)]
     heads = jnp.concatenate(heads, 0).astype(jnp.bfloat16)
     for chip in range(NZ):
@@ -333,12 +346,12 @@
     return last_dot(lm[...], jnp.concatenate(tiles, 1))
 
 
-def first_logits_kernel(heads, lm, total):
+def sums_kernel(heads, lm, total):
     total[...] = head_sums(heads, lm)
 
 
-def logits_kernel(core, heads, lm, before, logits, stats):
-    both = jnp.concatenate([before[...], head_sums(heads, lm)], 1)
+def logits_kernel(core, own, other, logits, stats):
+    both = jnp.concatenate([own[...], other[...]], 1)
     shape = (2 * EXPERTS, 2 * EXPERTS)
     lane = iota(shape, 0)
     z = jnp.where(lane < EXPERTS, core[0], 1 - core[0]) * 4 + lane % 4
@@ -443,19 +456,21 @@
     )
     other_down = swap(lax.dynamic_slice_in_dim(w_down[0], (1 - core) * HALF, HALF, 1))
 
+    other_lm = swap(lm_head)
+
     outgoing, mix_hi, mix_lo, accepted_mix = call(
         route_kernel,
         [z_at],
         [column],
         [
             pltpu.VMEM((NPLANE, NZ * CAP, HALF), bf16),
-            like((slots, NZ * NODES), bf16),
-            like((slots, NZ * NODES), bf16),
+            pltpu.HBM((slots, NZ * NODES), bf16),
+            pltpu.HBM((slots, NZ * NODES), bf16),
             like((2 * NZ, slots), bf16),
         ],
         flops=2 * slots * NZ * NODES * HALF,
         moved=4 << 20,
-        unused=[attended, in_hbm(block_w), in_hbm(other_down)],
+        unused=[in_hbm(attended), in_hbm(block_w), in_hbm(other_down), other_lm],
     )
     arrived = exchange(outgoing, PLANE)
     sums = call(
@@ -484,24 +499,17 @@
     )
     returned = exchange(finished, PLANE)
 
-    parts = call(
-        accepted_kernel,
+    parts, own, *others = call(
+        combine_kernel,
         [accept, z_at],
-        [accepted_mix, returned, hidden],
-        pltpu.HBM((2 * NZ, NZ, HALF), bf16),
-        flops=4 * NZ * slots * HALF,
-        moved=3 << 20,
-    )
-    parts = exchange(parts, ("z", "c"))
-    own, *others = call(
-        mixture_kernel,
-        [z_at],
-        [mix_hi, mix_lo, returned],
-        [like((NODES, HALF), f32)] + [like((NODES, HALF), bf16)] * (NZ - 1),
+        [accepted_mix, in_hbm(mix_hi), in_hbm(mix_lo), returned, hidden],
+        [pltpu.HBM((2 * NZ, NZ, HALF // 2), bf16), pltpu.HBM((NODES, HALF), f32)]
+        + [pltpu.HBM((NODES, HALF), bf16)] * (NZ - 1),
         flops=4 * slots * NZ * NODES * HALF,
         moved=6 << 20,
         scratch=[pltpu.VMEM((NZ * NODES, HALF), f32)],
     )
+    parts = exchange(parts, ("z", "c"))
     sent = {}
     for step, other in enumerate(others, 1):
         sent[step] = lax.ppermute(other, "z", around(NZ, step))
@@ -510,30 +518,38 @@
         final_kernel,
         [],
         [parts, in_hbm(final_gain)],
-        pltpu.HBM((4, NZ, D), bf16),
-        unused=[own],
+        pltpu.HBM((4, 16, HALF // 2), bf16),
+        unused=[in_hbm(sent[1]), in_hbm(sent[7])],
     )
     final = exchange(final, "x")
     heads = call(
         medusa_kernel,
-        [core_at, tile_at],
+        [tile_at],
         [final, block_w],
         pltpu.HBM((NZ, 32, LANES), bf16),
         flops=2 * 16 * D * 256,
         moved=3 << 20,
-        unused=[sent[step] for step in (1, 7, 2)],
     )
     heads = exchange(heads, "z")
     heads = call(
         copy_kernel,
         [],
         [heads],
-        pltpu.HBM((NPLANE, NZ, 32, LANES), bf16),
-        unused=[sent[step] for step in (6, 3, 5, 4)],
+        pltpu.VMEM((NPLANE, NZ, 32, LANES), bf16),
+        unused=[in_hbm(sent[2]), in_hbm(sent[6])],
     )
     heads = exchange(heads, PLANE)
-    total = call(
-        first_logits_kernel,
+    to_other = call(
+        sums_kernel,
+        [],
+        [heads, other_lm],
+        like((vocab, EXPERTS), f32),
+        flops=2 * EXPERTS * D * vocab,
+        moved=4 << 20,
+        unused=[in_hbm(sent[step]) for step in (3, 5, 4)],
+    )
+    to_own = call(
+        sums_kernel,
         [],
         [heads, lm_head],
         like((vocab, EXPERTS), f32),
@@ -543,19 +559,18 @@
     logits, stats = call(
         logits_kernel,
         [core_at],
-        [swap(heads), lm_head, total],
-        [like((2, vocab, EXPERTS), f32), pltpu.HBM((32, 4, EXPERTS), f32)],
-        flops=2 * EXPERTS * D * vocab,
-        moved=4 << 20,
+        [to_own, swap(to_other)],
+        [pltpu.HBM((2, vocab, EXPERTS), f32), pltpu.HBM((32, 4, EXPERTS), f32)],
+        moved=1 << 20,
     )
     mixture = own
-    for other in sent.values():
-        mixture = mixture + other.astype(f32)
+    for part in sent.values():
+        mixture = mixture + part.astype(f32)
     layer_out = (hidden.astype(f32) + mixture).astype(bf16)
     stats = exchange(stats, ("x", "y", "c"))
     stats = call(merge_kernel, [], [stats], pltpu.HBM((NZ, 4, EXPERTS), f32))
     stats = exchange(stats, "z")
-    logprob = call(finish_kernel, [], [stats, logits], like((2, vocab, EXPERTS), f32))
+    logprob = call(finish_kernel, [], [stats, in_hbm(logits)], like((2, vocab, EXPERTS), f32))
     return (attended, layer_out, jnp.transpose(logprob, (0, 2, 1)))
 
 

time: 247 us -> 236 us (0.955)
  blocking collectives: 102 us -> 83 us
  starting transfers between devices: 45.4 us -> 54.6 us
  local copies, waits for them, and re-layouts: 13.5 us -> 5.93 us
  waiting for transfers between devices: 46.3 us -> 52.9 us
    all_to_all x4 -> x3, blocking collectives: 95.8 us -> 79.5 us  [exchange(): return lax.all_to_all(value, axes, 0, 0, tiled=True)]
    ppermute x7, waiting for transfers between devices: 11 us -> 23.6 us  [on_device(): sent[step] = lax.ppermute(other, 'z', around(NZ, step))]
    unnamed x50 -> x54, local copies, waits for them, and re-layouts: 12.2 us -> 3.21 us
    all_to_all x5 -> x6, starting transfers between devices: 22.6 us -> 29.6 us  [exchange(): return lax.all_to_all(value, axes, 0, 0, tiled=True)]
    all_to_all x5 -> x6, waiting for transfers between devices: 22.6 us -> 19.4 us  [exchange(): return lax.all_to_all(value, axes, 0, 0, tiled=True)]
    psum x1, blocking collectives: 6.42 us -> 3.54 us  [on_device(): lax.psum(squares, TP)]
    ppermute x5 -> x6, starting transfers between devices: 8.23 us -> 10.3 us  [swap(): return lax.ppermute(value, TP, SWAP)]
  transfers between devices with their start and end apart: 20 -> 22, of which waited for: 13 -> 14; matrix products, arithmetic and copies ran while one was open for 2% -> 3% of each run, Pallas kernels for 5% -> 5%
where the time goes in v3:
time: 236 us; the launch traced here: 235 us
  blocking collectives  83 us (35%)
  starting transfers between devices  54.6 us (23%)
  waiting for transfers between devices  52.9 us (22%)
  Pallas kernels  32.9 us (14%)
  local copies, waits for them, and re-layouts  5.93 us (3%)
  other arithmetic  3.82 us (2%)
    all_to_all x3, blocking collectives, exchange(): return lax.all_to_all(value, axes, 0, 0, tiled=True)  79.5 us
    all_to_all x6, starting transfers between devices, exchange(): return lax.all_to_all(value, axes, 0, 0, tiled=True)  29.6 us
    pallas_call x16, Pallas kernels, call(): pl.pallas_call(body, out_shape=list(outs), in_specs=[SMEM] * count + [who...  28.9 us
    ppermute x7, waiting for transfers between devices, on_device(): sent[step] = lax.ppermute(other, 'z', around(NZ, step))  23.6 us
    all_to_all x6, waiting for transfers between devices, exchange(): return lax.all_to_all(value, axes, 0, 0, tiled=True)  19.4 us
    ppermute x6, starting transfers between devices, swap(): return lax.ppermute(value, TP, SWAP)  10.3 us
    ppermute x7, starting transfers between devices, on_device(): sent[step] = lax.ppermute(other, 'z', around(NZ, step))  9.68 us
    ppermute x3, waiting for transfers between devices, on_device(): lax.ppermute(wide_w, 'y', around(NY, step))  6.85 us
  transfers between devices with their start and end apart: 22, of which 14 were waited for; matrix products, arithmetic and copies ran while one was open for 3% of the time, Pallas kernels for 5%

profile of v3, /device:TPU:1, one launch (start us, length us, event | category | flops | bytes accessed | tf_op | source)
XLA Modules:
  0.0 235.3 jit_solution(2936316614727103243)
XLA Ops:
  0.6 3.3 %collective-permute-start.5 = (bf16[304,4096]{1,0:T(8,128)(2,1)}, bf16[304,4096]{1,0:T(8,128)(2,1)S(1)}, u32[]{:S(2)}, u32[]{:S(2)}) collective-permute-start(bf16[304,4096]{1,0:T(8,128)(2,1)} %refs_1_.9), channel_id=1, source_target_pairs={{0,1},{1,0},{2,3},{3,2},{4,5},{5,4},{6,7},{7,6},{8,9},{9,8},{10,11... | collective-permute-start | bytes 7471112 | tf_op jit(solution)/shard_map/ppermute | solution.py:31
  5.8 3.5 %psum.7.refs_2_ = f32[32,128]{1,0:T(8,128)S(1)} all-reduce(f32[32,128]{1,0:T(8,128)S(1)} %get-tuple-element.23), channel_id=1, replica_groups=mesh['x'=4,'z'=8,'y'=4,'c'=2] {'c'}, use_global_device_ids=true, to_apply=%region_0.0 | all-reduce | flops 4096 | bytes 32768 | tf_op jit(solution)/shard_map/psum | solution.py:436
  9.4 2.1 shard_map.186
  11.5 6.5 %all-to-all-start = ((bf16[8,32,2176]{2,1,0:T(8,128)(2,1)}), bf16[8,32,2176]{2,1,0:T(8,128)(2,1)}, u32[]{:S(2)}, u32[]{:S(2)}) async-start(bf16[8,32,2176]{2,1,0:T(8,128)(2,1)} %shard_map.186), calls=%async_computation | async-start | bytes 2228224 | tf_op jit(solution)/shard_map/all_to_all | solution.py:39
  19.2 2.6 %collective-permute-start.1 = (bf16[2,16,4224]{2,1,0:T(8,128)(2,1)S(1)}, bf16[2,16,4224]{2,1,0:T(8,128)(2,1)S(1)}, u32[]{:S(2)}, u32[]{:S(2)}) collective-permute-start(bf16[2,16,4224]{2,1,0:T(8,128)(2,1)S(1)} %get-tuple-element.25.refs_2_), channel_id=1, source_target_pairs={{0,4},{2,6},{4,0},{6,2},{1,5},{3,7},{5,1},{7,3},{8,12},{10,14},{12... | collective-permute-start | bytes 811016 | tf_op jit(solution)/shard_map/ppermute | solution.py:449
  22.9 2.7 %dynamic-slice_bitcast_fusion = bf16[384,2048]{1,0:T(8,128)(2,1)} fusion(bf16[1,384,4096]{2,1,0:T(8,128)(2,1)} %down.1, s32[]{:T(128)S(6)} %select_n.3), kind=kLoop, calls=%fused_computation | loop fusion | bytes 3145732 | tf_op jit(solution)/shard_map/dynamic_slice | solution.py:457
  27.0 6.8 %collective-permute-done.1.refs_4_ = bf16[2,16,4224]{2,1,0:T(8,128)(2,1)S(1)} collective-permute-done((bf16[2,16,4224]{2,1,0:T(8,128)(2,1)S(1)}, bf16[2,16,4224]{2,1,0:T(8,128)(2,1)S(1)}, u32[]{:S(2)}, u32[]{:S(2)}) %collective-permute-start.1) | collective-permute-done | bytes 270368 | tf_op jit(solution)/shard_map/ppermute | solution.py:449
  33.8 2.1 pad_maximum_fusion
  38.8 2.1 shard_map.184.refs_2_
  41.0 2.8 %shard_map.187.refs_3_.refs_2_ = bf16[2,128,4224]{2,1,0:T(8,128)(2,1)} custom-call(s32[1]{0:T(128)} %bitcast.1.refs_0_.core, s32[1]{0:T(128)} %bitcast.4.refs_1_, bf16[2,16,4224]{2,1,0:T(8,128)(2,1)S(1)} %get-tuple-element.25.refs_2_, bf16[2,16,4224]{2,1,0:T(8,128)(2,1)S(1)} %collective-permute-done.refs_3_, ...), custom_call_target="tpu_custom_call" | custom-call | bytes 4194304 | tf_op jit(solution)/shard_map/pallas_call | solution.py:104
  43.8 4.9 %all-to-all-done.refs_1_ = bf16[8,32,2176]{2,1,0:T(8,128)(2,1)} async-done(((bf16[8,32,2176]{2,1,0:T(8,128)(2,1)}), bf16[8,32,2176]{2,1,0:T(8,128)(2,1)}, u32[]{:S(2)}, u32[]{:S(2)}) %all-to-all-start) | async-done | bytes 1114144 | tf_op jit(solution)/shard_map/all_to_all | solution.py:39
  48.7 3.9 %shard_map.188 = (bf16[16,32,2048]{2,1,0:T(8,128)(2,1)S(1)}, bf16[512,256]{1,0:T(8,128)(2,1)}, bf16[512,256]{1,0:T(8,128)(2,1)}, bf16[16,512]{1,0:T(8,128)(2,1)S(1)}) custom-call(s32[1]{0:T(128)} %bitcast.refs_0_.refs_1_, bf16[8,32,2176]{2,1,0:T(8,128)(2,1)} %all-to-all-done.refs_1_, bf16[1,32,4096]{2,1,0:T(8,128)(2,1)} %shard_map.184.refs_2_, ...), custom_call_target="tpu_custom_call" | custom-call | flops 536870912 | bytes 4194304 | tf_op jit(solution)/shard_map/pallas_call | solution.py:104
  52.7 34.0 %all_to_all.45.refs_1_ = bf16[16,32,2048]{2,1,0:T(8,128)(2,1)S(1)} all-to-all(bf16[16,32,2048]{2,1,0:T(8,128)(2,1)S(1)} %get-tuple-element.29), channel_id=1, replica_groups=mesh['x'=4,'z'=8,'y'=4,'c'=2] {'x','y'}, dimensions={0} | all-to-all | bytes 4194304 | tf_op jit(solution)/shard_map/all_to_all | solution.py:39
  88.7 2.3 shard_map.189
  92.5 2.4 %shard_map.190.own = bf16[512,384]{1,0:T(8,128)(2,1)S(1)} custom-call(s32[1]{0:T(128)} %bitcast.1.refs_0_.core, bf16[16,32,2048]{2,1,0:T(8,128)(2,1)S(1)} %collective-permute-done.6.refs_1_, bf16[1,4096,384]{2,1,0:T(8,128)(2,1)S(1)} %copy-done.1, bf16[1,4096,384]{2,1,0:T(8,128)(2,1)S(1)} %copy-done.2, f32[512,384]{1,0:T(8,128)S(1)} %get-tuple-element.30.refs_4_, ...), custom_call_target="tpu_custom_call" | custom-call | flops 1610612736 | bytes 8388608 | tf_op jit(solution)/shard_map/pallas_call | solution.py:104
  96.8 3.9 %shard_map.191 = bf16[16,32,2048]{2,1,0:T(8,128)(2,1)S(1)} custom-call(s32[1]{0:T(128)} %bitcast.1.refs_0_.core, bf16[512,384]{1,0:T(8,128)(2,1)S(1)} %shard_map.190.own, bf16[512,384]{1,0:T(8,128)(2,1)S(1)} %collective-permute-done.7.other, bf16[1,384,4096]{2,1,0:T(8,128)(2,1)S(1)} %copy-done.5, bf16[384,2048]{1,0:T(8,128)(2,1)} %collective-permute-done.4.refs_4_.other_down), custom_call_target="tpu_custom_call" | custom-call | flops 1610612736 | bytes 6291456 | tf_op jit(solution)/shard_map/pallas_call | solution.py:258
  100.8 30.7 %all_to_all.46.refs_5_ = bf16[16,32,2048]{2,1,0:T(8,128)(2,1)S(1)} all-to-all(bf16[16,32,2048]{2,1,0:T(8,128)(2,1)S(1)} %shard_map.191), channel_id=1, replica_groups=mesh['x'=4,'z'=8,'y'=4,'c'=2] {'x','y'}, dimensions={0} | all-to-all | bytes 4194304 | tf_op jit(solution)/shard_map/all_to_all | solution.py:39
  131.5 3.7 %shard_map.192 = (bf16[16,8,1024]{2,1,0:T(8,128)(2,1)}, f32[32,2048]{1,0:T(8,128)}, bf16[32,2048]{1,0:T(8,128)(2,1)}, bf16[32,2048]{1,0:T(8,128)(2,1)}, bf16[32,...) custom-call(s32[1]{0:T(128)S(6)} %copy.21.refs_0_, ...), custom_call_target="tpu_custom_call" | custom-call | flops 1073741824 | bytes 6291456 | tf_op jit(solution)/shard_map/pallas_call | solution.py:104
  135.3 5.4 %all-to-all-start.3 = ((bf16[16,8,1024]{2,1,0:T(8,128)(2,1)}), bf16[16,8,1024]{2,1,0:T(8,128)(2,1)S(1)}, u32[]{:S(2)}, u32[]{:S(2)}) async-start(bf16[16,8,1024]{2,1,0:T(8,128)(2,1)} %get-tuple-element.40), calls=%async_computation.3 | async-start | bytes 524288 | tf_op jit(solution)/shard_map/all_to_all | solution.py:39
  140.7 2.7 %collective-permute-start.14 = (bf16[32,2048]{1,0:T(8,128)(2,1)}, bf16[32,2048]{1,0:T(8,128)(2,1)S(1)}, u32[]{:S(2)}, u32[]{:S(2)}) collective-permute-start(bf16[32,2048]{1,0:T(8,128)(2,1)} %get-tuple-element.39), channel_id=1, source_target_pairs={{0,56},{8,0},{16,8},{24,16},{32,24},{40,32},{48,40},{56,48},{1,57}... | collective-permute-start | bytes 393224 | tf_op jit(solution)/shard_map/ppermute | solution.py:515
  143.3 8.1 %collective-permute-done.14.refs_3_ = bf16[32,2048]{1,0:T(8,128)(2,1)S(1)} collective-permute-done((bf16[32,2048]{1,0:T(8,128)(2,1)}, bf16[32,2048]{1,0:T(8,128)(2,1)S(1)}, u32[]{:S(2)}, u32[]{:S(2)}) %collective-permute-start.14) | collective-permute-done | bytes 131104 | tf_op jit(solution)/shard_map/ppermute | solution.py:515
  154.9 3.3 %all-to-all-start.4 = ((bf16[4,16,1024]{2,1,0:T(8,128)(2,1)}), bf16[4,16,1024]{2,1,0:T(8,128)(2,1)S(1)}, u32[]{:S(2)}, u32[]{:S(2)}) async-start(bf16[4,16,1024]{2,1,0:T(8,128)(2,1)} %shard_map.193), calls=%async_computation.4 | async-start | bytes 262144 | tf_op jit(solution)/shard_map/all_to_all | solution.py:39
  158.2 2.2 collective-permute-start.13
  160.7 2.3 all-to-all-done.4.refs_1_
  164.4 4.7 %all-to-all-start.5 = ((bf16[8,32,128]{2,1,0:T(8,128)(2,1)}), bf16[8,32,128]{2,1,0:T(8,128)(2,1)S(1)}, u32[]{:S(2)}, u32[]{:S(2)}) async-start(bf16[8,32,128]{2,1,0:T(8,128)(2,1)} %shard_map.194), calls=%async_computation.5 | async-start | bytes 131072 | tf_op jit(solution)/shard_map/all_to_all | solution.py:39
  169.2 7.2 %all-to-all-done.5.refs_0_ = bf16[8,32,128]{2,1,0:T(8,128)(2,1)S(1)} async-done(((bf16[8,32,128]{2,1,0:T(8,128)(2,1)}), bf16[8,32,128]{2,1,0:T(8,128)(2,1)S(1)}, u32[]{:S(2)}, u32[]{:S(2)}) %all-to-all-start.5) | async-done | bytes 65568 | tf_op jit(solution)/shard_map/all_to_all | solution.py:39
  177.5 3.7 %all-to-all-start.6 = ((bf16[16,8,32,128]{3,2,1,0:T(8,128)(2,1)}), bf16[16,8,32,128]{3,2,1,0:T(8,128)(2,1)S(1)}, u32[]{:S(2)}, u32[]{:S(2)}) async-start(bf16[16,8,32,128]{3,2,1,0:T(8,128)(2,1)} %copy-done.6), calls=%async_computation.6 | async-start | bytes 2097152 | tf_op jit(solution)/shard_map/all_to_all | solution.py:39
  181.7 4.0 %collective-permute-start.11 = (bf16[32,2048]{1,0:T(8,128)(2,1)}, bf16[32,2048]{1,0:T(8,128)(2,1)S(1)}, u32[]{:S(2)}, u32[]{:S(2)}) collective-permute-start(bf16[32,2048]{1,0:T(8,128)(2,1)} %get-tuple-element.36), channel_id=1, source_target_pairs={{0,32},{8,40},{16,48},{24,56},{32,0},{40,8},{48,16},{56,24},{1,33}... | collective-permute-start | bytes 393224 | tf_op jit(solution)/shard_map/ppermute | solution.py:515
  190.4 10.3 %collective-permute-done.10.refs_2_ = bf16[32,2048]{1,0:T(8,128)(2,1)} collective-permute-done((bf16[32,2048]{1,0:T(8,128)(2,1)}, bf16[32,2048]{1,0:T(8,128)(2,1)}, u32[]{:S(2)}, u32[]{:S(2)}) %collective-permute-start.10) | collective-permute-done | bytes 131104 | tf_op jit(solution)/shard_map/ppermute | solution.py:515
  205.5 14.8 %all_to_all.47.refs_0_ = f32[32,4,128]{2,1,0:T(4,128)S(1)} all-to-all(f32[32,4,128]{2,1,0:T(4,128)} %get-tuple-element.41), channel_id=1, replica_groups=mesh['x'=4,'z'=8,'y'=4,'c'=2] {'x','y','c'}, dimensions={0} | all-to-all | bytes 131072 | tf_op jit(solution)/shard_map/all_to_all | solution.py:39
  220.9 6.0 %all-to-all-start.8 = ((f32[8,4,128]{2,1,0:T(4,128)}), f32[8,4,128]{2,1,0:T(4,128)S(1)}, u32[]{:S(2)}, u32[]{:S(2)}) async-start(f32[8,4,128]{2,1,0:T(4,128)} %shard_map.199), calls=%async_computation.8 | async-start | bytes 32768 | tf_op jit(solution)/shard_map/all_to_all | solution.py:39
  228.7 4.8 %all-to-all-done.8.refs_0_ = f32[8,4,128]{2,1,0:T(4,128)S(1)} async-done(((f32[8,4,128]{2,1,0:T(4,128)}), f32[8,4,128]{2,1,0:T(4,128)S(1)}, u32[]{:S(2)}, u32[]{:S(2)}) %all-to-all-start.8) | async-done | bytes 16416 | tf_op jit(solution)/shard_map/all_to_all | solution.py:39
  (90 shorter events, 32.9 us)
Async XLA Ops:
  0.6 48.1 %collective-permute-start.5 = (bf16[304,4096]{1,0:T(8,128)(2,1)}, bf16[304,4096]{1,0:T(8,128)(2,1)S(1)}, u32[]{:S(2)}, u32[]{:S(2)}) collective-permute-start(bf16[304,4096]{1,0:T(8,128)(2,1)} %refs_1_.9), channel_id=1, source_target_pairs={{0,1},{1,0},{2,3},{3,2},{4,5},{5,4},{6,7},{7,6},{8,9},{9,8},{10,11... | collective-permute-start | bytes 7471112 | tf_op jit(solution)/shard_map/ppermute | solution.py:31
  11.5 37.3 %all-to-all-start = ((bf16[8,32,2176]{2,1,0:T(8,128)(2,1)}), bf16[8,32,2176]{2,1,0:T(8,128)(2,1)}, u32[]{:S(2)}, u32[]{:S(2)}) async-start(bf16[8,32,2176]{2,1,0:T(8,128)(2,1)} %shard_map.186), calls=%async_computation | async-start | bytes 2228224 | tf_op jit(solution)/shard_map/all_to_all | solution.py:39
  17.9 9.1 %collective-permute-start = (bf16[2,16,4224]{2,1,0:T(8,128)(2,1)S(1)}, bf16[2,16,4224]{2,1,0:T(8,128)(2,1)S(1)}, u32[]{:S(2)}, u32[]{:S(2)}) collective-permute-start(bf16[2,16,4224]{2,1,0:T(8,128)(2,1)S(1)} %get-tuple-element.25.refs_2_), channel_id=1, source_target_pairs={{0,2},{2,4},{4,6},{6,0},{1,3},{3,5},{5,7},{7,1},{8,10},{10,12},{12... | collective-permute-start | bytes 811016 | tf_op jit(solution)/shard_map/ppermute | solution.py:449
  19.2 14.6 %collective-permute-start.1 = (bf16[2,16,4224]{2,1,0:T(8,128)(2,1)S(1)}, bf16[2,16,4224]{2,1,0:T(8,128)(2,1)S(1)}, u32[]{:S(2)}, u32[]{:S(2)}) collective-permute-start(bf16[2,16,4224]{2,1,0:T(8,128)(2,1)S(1)} %get-tuple-element.25.refs_2_), channel_id=1, source_target_pairs={{0,4},{2,6},{4,0},{6,2},{1,5},{3,7},{5,1},{7,3},{8,12},{10,14},{12... | collective-permute-start | bytes 811016 | tf_op jit(solution)/shard_map/ppermute | solution.py:449
  21.9 11.9 %collective-permute-start.2 = (bf16[2,16,4224]{2,1,0:T(8,128)(2,1)S(1)}, bf16[2,16,4224]{2,1,0:T(8,128)(2,1)}, u32[]{:S(2)}, u32[]{:S(2)}) collective-permute-start(bf16[2,16,4224]{2,1,0:T(8,128)(2,1)S(1)} %get-tuple-element.25.refs_2_), channel_id=1, source_target_pairs={{0,6},{2,0},{4,2},{6,4},{1,7},{3,1},{5,3},{7,5},{8,14},{10,8},{12,... | collective-permute-start | bytes 811016 | tf_op jit(solution)/shard_map/ppermute | solution.py:449
  25.7 18.2 %collective-permute-start.4 = (bf16[384,2048]{1,0:T(8,128)(2,1)}, bf16[384,2048]{1,0:T(8,128)(2,1)}, u32[]{:S(2)}, u32[]{:S(2)}) collective-permute-start(bf16[384,2048]{1,0:T(8,128)(2,1)} %dynamic-slice_bitcast_fusion), channel_id=1, source_target_pairs={{0,1},{1,0},{2,3},{3,2},{4,5},{5,4},{6,7},{7,6},{8,9},{9,8},{10,11... | collective-permute-start | bytes 4718600 | tf_op jit(solution)/shard_map/ppermute | solution.py:31
  35.9 5.1 %collective-permute-start.3 = (bf16[4,2,16,4224]{3,2,1,0:T(8,128)(2,1)}, bf16[4,2,16,4224]{3,2,1,0:T(8,128)(2,1)}, u32[]{:S(2)}, u32[]{:S(2)}) collective-permute-start(bf16[4,2,16,4224]{3,2,1,0:T(8,128)(2,1)} %pad_maximum_fusion), channel_id=1, source_target_pairs={{0,1},{1,0},{2,3},{3,2},{4,5},{5,4},{6,7},{7,6},{8,9},{9,8},{10,11... | collective-permute-start | bytes 3244040 | tf_op jit(solution)/shard_map/ppermute | solution.py:31
  48.7 39.9 %copy-start.2 = (bf16[1,4096,384]{2,1,0:T(8,128)(2,1)S(1)}, bf16[1,4096,384]{2,1,0:T(8,128)(2,1)}, u32[]{:S(2)}) copy-start(bf16[1,4096,384]{2,1,0:T(8,128)(2,1)} %refs_3_.7) | copy-start | bytes 9437188
  52.7 36.0 %copy-start.1 = (bf16[1,4096,384]{2,1,0:T(8,128)(2,1)S(1)}, bf16[1,4096,384]{2,1,0:T(8,128)(2,1)}, u32[]{:S(2)}) copy-start(bf16[1,4096,384]{2,1,0:T(8,128)(2,1)} %refs_2_.5) | copy-start | bytes 9437188
  86.6 5.8 %collective-permute-start.6 = (bf16[16,32,2048]{2,1,0:T(8,128)(2,1)S(1)}, bf16[16,32,2048]{2,1,0:T(8,128)(2,1)S(1)}, u32[]{:S(2)}, u32[]{:S(2)}) collective-permute-start(bf16[16,32,2048]{2,1,0:T(8,128)(2,1)S(1)} %all_to_all.45.refs_1_), channel_id=1, source_target_pairs={{0,1},{1,0},{2,3},{3,2},{4,5},{5,4},{6,7},{7,6},{8,9},{9,8},{10,11... | collective-permute-start | bytes 6291464 | tf_op jit(solution)/shard_map/ppermute | solution.py:31
  94.8 2.0 collective-permute-start.7
  100.8 30.7 %copy-start.8 = (bf16[32,2048]{1,0:T(8,128)(2,1)S(1)}, bf16[32,2048]{1,0:T(8,128)(2,1)}, u32[]{:S(2)}) copy-start(bf16[32,2048]{1,0:T(8,128)(2,1)} %refs_6_.1) | copy-start | bytes 393220
  131.5 31.5 %copy-start = (bf16[2,128,4224]{2,1,0:T(8,128)(2,1)S(1)}, bf16[2,128,4224]{2,1,0:T(8,128)(2,1)}, u32[]{:S(2)}) copy-start(bf16[2,128,4224]{2,1,0:T(8,128)(2,1)} %shard_map.187.refs_3_.refs_2_) | copy-start | bytes 6488068
  135.3 17.5 %all-to-all-start.3 = ((bf16[16,8,1024]{2,1,0:T(8,128)(2,1)}), bf16[16,8,1024]{2,1,0:T(8,128)(2,1)S(1)}, u32[]{:S(2)}, u32[]{:S(2)}) async-start(bf16[16,8,1024]{2,1,0:T(8,128)(2,1)} %get-tuple-element.40), calls=%async_computation.3 | async-start | bytes 524288 | tf_op jit(solution)/shard_map/all_to_all | solution.py:39
  140.7 10.8 %collective-permute-start.14 = (bf16[32,2048]{1,0:T(8,128)(2,1)}, bf16[32,2048]{1,0:T(8,128)(2,1)S(1)}, u32[]{:S(2)}, u32[]{:S(2)}) collective-permute-start(bf16[32,2048]{1,0:T(8,128)(2,1)} %get-tuple-element.39), channel_id=1, source_target_pairs={{0,56},{8,0},{16,8},{24,16},{32,24},{40,32},{48,40},{56,48},{1,57}... | collective-permute-start | bytes 393224 | tf_op jit(solution)/shard_map/ppermute | solution.py:515
  143.3 9.3 %collective-permute-start.8 = (bf16[32,2048]{1,0:T(8,128)(2,1)}, bf16[32,2048]{1,0:T(8,128)(2,1)S(1)}, u32[]{:S(2)}, u32[]{:S(2)}) collective-permute-start(bf16[32,2048]{1,0:T(8,128)(2,1)} %get-tuple-element.33), channel_id=1, source_target_pairs={{0,8},{8,16},{16,24},{24,32},{32,40},{40,48},{48,56},{56,0},{1,9},... | collective-permute-start | bytes 393224 | tf_op jit(solution)/shard_map/ppermute | solution.py:515
  154.9 8.1 %all-to-all-start.4 = ((bf16[4,16,1024]{2,1,0:T(8,128)(2,1)}), bf16[4,16,1024]{2,1,0:T(8,128)(2,1)S(1)}, u32[]{:S(2)}, u32[]{:S(2)}) async-start(bf16[4,16,1024]{2,1,0:T(8,128)(2,1)} %shard_map.193), calls=%async_computation.4 | async-start | bytes 262144 | tf_op jit(solution)/shard_map/all_to_all | solution.py:39
  158.2 11.0 %collective-permute-start.13 = (bf16[32,2048]{1,0:T(8,128)(2,1)}, bf16[32,2048]{1,0:T(8,128)(2,1)S(1)}, u32[]{:S(2)}, u32[]{:S(2)}) collective-permute-start(bf16[32,2048]{1,0:T(8,128)(2,1)} %get-tuple-element.38), channel_id=1, source_target_pairs={{0,48},{8,56},{16,0},{24,8},{32,16},{40,24},{48,32},{56,40},{1,49}... | collective-permute-start | bytes 393224 | tf_op jit(solution)/shard_map/ppermute | solution.py:515
  160.5 8.7 %collective-permute-start.9 = (bf16[32,2048]{1,0:T(8,128)(2,1)}, bf16[32,2048]{1,0:T(8,128)(2,1)S(1)}, u32[]{:S(2)}, u32[]{:S(2)}) collective-permute-start(bf16[32,2048]{1,0:T(8,128)(2,1)} %get-tuple-element.34), channel_id=1, source_target_pairs={{0,16},{8,24},{16,32},{24,40},{32,48},{40,56},{48,0},{56,8},{1,17}... | collective-permute-start | bytes 393224 | tf_op jit(solution)/shard_map/ppermute | solution.py:515
  164.4 12.0 %all-to-all-start.5 = ((bf16[8,32,128]{2,1,0:T(8,128)(2,1)}), bf16[8,32,128]{2,1,0:T(8,128)(2,1)S(1)}, u32[]{:S(2)}, u32[]{:S(2)}) async-start(bf16[8,32,128]{2,1,0:T(8,128)(2,1)} %shard_map.194), calls=%async_computation.5 | async-start | bytes 131072 | tf_op jit(solution)/shard_map/all_to_all | solution.py:39
  169.2 31.5 %copy-start.4 = (bf16[304,4096]{1,0:T(8,128)(2,1)S(1)}, bf16[304,4096]{1,0:T(8,128)(2,1)}, u32[]{:S(2)}) copy-start(bf16[304,4096]{1,0:T(8,128)(2,1)} %copy-done.3) | copy-start | bytes 7471108
  177.5 23.2 %all-to-all-start.6 = ((bf16[16,8,32,128]{3,2,1,0:T(8,128)(2,1)}), bf16[16,8,32,128]{3,2,1,0:T(8,128)(2,1)S(1)}, u32[]{:S(2)}, u32[]{:S(2)}) async-start(bf16[16,8,32,128]{3,2,1,0:T(8,128)(2,1)} %copy-done.6), calls=%async_computation.6 | async-start | bytes 2097152 | tf_op jit(solution)/shard_map/all_to_all | solution.py:39
  181.2 6.6 %collective-permute-start.12 = (bf16[32,2048]{1,0:T(8,128)(2,1)}, bf16[32,2048]{1,0:T(8,128)(2,1)S(1)}, u32[]{:S(2)}, u32[]{:S(2)}) collective-permute-start(bf16[32,2048]{1,0:T(8,128)(2,1)} %get-tuple-element.37), channel_id=1, source_target_pairs={{0,40},{8,48},{16,56},{24,0},{32,8},{40,16},{48,24},{56,32},{1,41}... | collective-permute-start | bytes 393224 | tf_op jit(solution)/shard_map/ppermute | solution.py:515
  181.7 8.1 %collective-permute-start.11 = (bf16[32,2048]{1,0:T(8,128)(2,1)}, bf16[32,2048]{1,0:T(8,128)(2,1)S(1)}, u32[]{:S(2)}, u32[]{:S(2)}) collective-permute-start(bf16[32,2048]{1,0:T(8,128)(2,1)} %get-tuple-element.36), channel_id=1, source_target_pairs={{0,32},{8,40},{16,48},{24,56},{32,0},{40,8},{48,16},{56,24},{1,33}... | collective-permute-start | bytes 393224 | tf_op jit(solution)/shard_map/ppermute | solution.py:515
  185.7 15.0 %collective-permute-start.10 = (bf16[32,2048]{1,0:T(8,128)(2,1)}, bf16[32,2048]{1,0:T(8,128)(2,1)}, u32[]{:S(2)}, u32[]{:S(2)}) collective-permute-start(bf16[32,2048]{1,0:T(8,128)(2,1)} %get-tuple-element.35), channel_id=1, source_target_pairs={{0,24},{8,32},{16,40},{24,48},{32,56},{40,0},{48,8},{56,16},{1,25}... | collective-permute-start | bytes 393224 | tf_op jit(solution)/shard_map/ppermute | solution.py:515
  201.5 25.4 %copy-start.9 = (bf16[32,2048]{1,0:T(8,128)(2,1)S(1)}, bf16[32,2048]{1,0:T(8,128)(2,1)}, u32[]{:S(2)}) copy-start(bf16[32,2048]{1,0:T(8,128)(2,1)} %refs_6_.1) | copy-start | bytes 393220
  201.5 25.4 %copy-start.15 = (bf16[32,2048]{1,0:T(8,128)(2,1)S(1)}, bf16[32,2048]{1,0:T(8,128)(2,1)}, u32[]{:S(2)}) copy-start(bf16[32,2048]{1,0:T(8,128)(2,1)} %copy-done.14) | copy-start | bytes 393220
  201.5 25.4 %copy-start.17 = (bf16[32,2048]{1,0:T(8,128)(2,1)S(1)}, bf16[32,2048]{1,0:T(8,128)(2,1)}, u32[]{:S(2)}) copy-start(bf16[32,2048]{1,0:T(8,128)(2,1)} %copy-done.16) | copy-start | bytes 393220
  201.6 25.4 %copy-start.19 = (bf16[32,2048]{1,0:T(8,128)(2,1)S(1)}, bf16[32,2048]{1,0:T(8,128)(2,1)}, u32[]{:S(2)}) copy-start(bf16[32,2048]{1,0:T(8,128)(2,1)} %copy-done.18) | copy-start | bytes 393220
  201.6 25.4 %copy-start.21 = (bf16[32,2048]{1,0:T(8,128)(2,1)S(1)}, bf16[32,2048]{1,0:T(8,128)(2,1)}, u32[]{:S(2)}) copy-start(bf16[32,2048]{1,0:T(8,128)(2,1)} %copy-done.20) | copy-start | bytes 393220
  201.6 2.8 %collective-permute-start.15 = (f32[304,128]{1,0:T(8,128)S(1)}, f32[304,128]{1,0:T(8,128)S(1)}, u32[]{:S(2)}, u32[]{:S(2)}) collective-permute-start(f32[304,128]{1,0:T(8,128)S(1)} %shard_map.197), channel_id=1, source_target_pairs={{0,1},{1,0},{2,3},{3,2},{4,5},{5,4},{6,7},{7,6},{8,9},{9,8},{10,11... | collective-permute-start | bytes 466952 | tf_op jit(solution)/shard_map/ppermute | solution.py:31
  220.9 12.6 %all-to-all-start.8 = ((f32[8,4,128]{2,1,0:T(4,128)}), f32[8,4,128]{2,1,0:T(4,128)S(1)}, u32[]{:S(2)}, u32[]{:S(2)}) async-start(f32[8,4,128]{2,1,0:T(4,128)} %shard_map.199), calls=%async_computation.8 | async-start | bytes 32768 | tf_op jit(solution)/shard_map/all_to_all | solution.py:39
  (17 other events, 144.7 us)

commit v4 on v3

--- a/solution.py
+++ b/solution.py
@@ -22,6 +22,7 @@
 NY = 4
 NPLANE = 16
 LANES = 128
+NEAR = (1, 2, -1, -2)
 BLOCK = 512
 VMEM_LIMIT = 40 << 20
 SWAP = [(0, 1), (1, 0)]
@@ -146,16 +147,20 @@
             ]
 
 
-def begin_kernel(accept, hidden, routes, gates, weights, bias, squares, notes, wide):
+def begin_kernel(accept, hidden, routes, gates, squares, notes):
     rows = hidden[...].astype(jnp.float32)
-    squares[...] = jnp.broadcast_to(jnp.sum(rows * rows, -1, keepdims=True), squares.shape)
+    here = iota((NODES, LANES), 0) == iota((NODES, LANES), 1)
+    sums = jnp.sum(rows * rows, -1, keepdims=True)
+    squares[...] = jnp.sum(jnp.where(here, sums, 0.0), 0, keepdims=True)
     share = gates[...] / jnp.sum(gates[...], 0, keepdims=True)
     share_hi = share.astype(jnp.bfloat16).astype(jnp.float32)
     flag = (iota((TOPK, NODES), 1) == accept[0]).astype(jnp.float32)
     stack = [routes[...].astype(jnp.float32), share_hi, share - share_hi, flag]
     stack = jnp.concatenate(stack, 0).astype(jnp.bfloat16)
-    places = as_bf16(iota((NODES, LANES), 0) == iota((NODES, LANES), 1))
-    notes[...] = first_dot(stack, places).astype(jnp.bfloat16)
+    notes[...] = first_dot(stack, as_bf16(here)).astype(jnp.bfloat16)
+
+
+def widen_kernel(weights, bias, wide):
     block = weights.shape[1]
     lane = iota((block, LANES), 1)
     for head in range(2):
@@ -182,11 +187,18 @@
 
 
 def pack_kernel(core, hidden, squares, gain, notes, packet):
-    factor = lax.rsqrt(squares[...][:, :1] / D + eps_norm)
-    own_gain = jnp.where(core[0] == 0, gain[:HALF], gain[HALF:]).reshape(1, HALF)
-    normed = (hidden[...].astype(jnp.float32) * factor * own_gain).astype(jnp.bfloat16)
+    here = iota((NODES, LANES), 0) == iota((NODES, LANES), 1)
+    sums = jnp.sum(jnp.where(here, squares[...], 0.0), 1, keepdims=True)
+    factor = lax.rsqrt(sums / D + eps_norm)
+    tiles = HALF // LANES
+    for tile in range(tiles):
+        own_gain = gain[pl.ds(core[0] * tiles + tile, 1), :]
+        here = slice(tile * LANES, (tile + 1) * LANES)
+        normed = hidden[:, here].astype(jnp.float32) * factor * own_gain
+        normed = normed.astype(jnp.bfloat16)
+        for chip in range(NZ):
+            packet[chip, :, here] = normed
     for chip in range(NZ):
-        packet[chip, :, :HALF] = normed
         packet[chip, :, HALF:] = notes[...]
 
 
@@ -245,56 +257,54 @@
 
 
 def down_kernel(core, own, other, down, other_down, finished):
-    del core
     rows = jnp.concatenate([own[...], other[...]], 1)
-    part = dot32(rows, jnp.concatenate([down[0], other_down[...]], 0))
-    finished[...] = part.astype(jnp.bfloat16).reshape(finished.shape)
-
-
-def down(core, own, other, w_down, other_down, out_shape):
-    rows, units = own.shape
-    steps = HALF // BLOCK
-    column = lambda i, core: (0, i)
-    return pl.pallas_call(
-        down_kernel,
-        out_shape=out_shape,
-        grid_spec=pltpu.PrefetchScalarGridSpec(
-            num_scalar_prefetch=1,
-            grid=(steps,),
-            in_specs=[
-                pl.BlockSpec((rows, units), lambda i, core: (0, 0)),
-                pl.BlockSpec((rows, units), lambda i, core: (0, 0)),
-                pl.BlockSpec((1, units, BLOCK), lambda i, core: (0, 0, core[0] * steps + i)),
-                pl.BlockSpec((units, BLOCK), column),
-            ],
-            out_specs=pl.BlockSpec((NPLANE, NZ * CAP, BLOCK), lambda i, core: (0, 0, i)),
-        ),
-        compiler_params=pltpu.CompilerParams(vmem_limit_bytes=VMEM_LIMIT),
-        cost_estimate=pl.CostEstimate(
-            flops=4 * rows * HALF * units, bytes_accessed=6 << 20, transcendentals=0
-        ),
-    )(core, own, other, w_down, other_down)
-
-
-def combine_kernel(accept, my_z, mix, mix_hi, mix_lo, returned, hidden, parts, *refs):
-    outs, partial = refs[:NZ], refs[NZ]
+    columns = pl.ds(pl.multiple_of(core[0] * HALF, HALF), HALF)
+    weights = jnp.concatenate([down[0, :, columns], other_down[...]], 0)
+    for piece in range(HALF // BLOCK):
+        here = slice(piece * BLOCK, (piece + 1) * BLOCK)
+        part = dot32(rows, weights[:, here]).astype(jnp.bfloat16)
+        finished[:, :, here] = part.reshape(NPLANE, NZ * CAP, BLOCK)
+
+
+def combine_kernel(
+    accept, my_z, mix, mix_hi, mix_lo, returned, hidden, parts, own, far_up, far_down, near, total
+):
     rows = returned[...].reshape(-1, HALF)
     part = dot32(mix[...], rows)
     part = part[:NZ] + part[NZ:]
     here = iota((NODES, 1), 0) == accept[0]
-    own = jnp.sum(jnp.where(here, hidden[...].astype(jnp.float32), 0.0), 0, keepdims=True)
-    part = part + jnp.where(iota((NZ, 1), 0) == my_z[0], own, 0.0)
+    row = jnp.sum(jnp.where(here, hidden[...].astype(jnp.float32), 0.0), 0, keepdims=True)
+    part = part + jnp.where(iota((NZ, 1), 0) == my_z[0], row, 0.0)
     quarter = HALF // 2
     for core in range(2):
         four = part[core * 4 : core * 4 + 4]
         four = jnp.concatenate([four[:, :quarter], four[:, quarter:]], 0).astype(jnp.bfloat16)
         for chip in range(NZ):
             parts[chip * 2 + core] = four
-    partial[...] = first_dot(mix_hi[...], rows) + first_dot(mix_lo[...], rows)
-    for step, out in enumerate(outs):
-        place = lax.rem(my_z[0] + step, NZ)
-        block = partial[pl.ds(pl.multiple_of(place * NODES, NODES), NODES), :]
-        out[...] = block.astype(out.dtype)
+    total[...] = first_dot(mix_hi[...], rows) + first_dot(mix_lo[...], rows)
+
+    def block(step, first=0, count=NODES):
+        place = lax.rem(my_z[0] + step + NZ, NZ)
+        return total[pl.ds(pl.multiple_of(place * NODES + first, 16), count), :]
+
+    own[...] = block(0)
+    far_up[:NODES, :] = block(3).astype(jnp.bfloat16)
+    far_up[NODES:, :] = block(4, 0, NODES // 2).astype(jnp.bfloat16)
+    far_down[:NODES, :] = block(-3).astype(jnp.bfloat16)
+    far_down[NODES:, :] = block(4, NODES // 2, NODES // 2).astype(jnp.bfloat16)
+    for place, step in enumerate(NEAR):
+        near[place] = block(step)
+
+
+def relay_kernel(near, from_below, from_above, up1, up2, down1, down2):
+    half = NODES // 2
+    below, above = from_below[...].astype(jnp.float32), from_above[...].astype(jnp.float32)
+    up1[...] = (near[0] + below[:NODES]).astype(jnp.bfloat16)
+    up2[:half, :] = (near[1, :half] + below[NODES:]).astype(jnp.bfloat16)
+    up2[half:, :] = near[1, half:].astype(jnp.bfloat16)
+    down1[...] = (near[2] + above[:NODES]).astype(jnp.bfloat16)
+    down2[:half, :] = near[3, :half].astype(jnp.bfloat16)
+    down2[half:, :] = (near[3, half:] + above[NODES:]).astype(jnp.bfloat16)
 
 
 def final_kernel(parts, gain, copies):
@@ -305,12 +315,15 @@
     squares = squares + jnp.concatenate([squares[4:], squares[:4]], 0)
     factor = lax.rsqrt(squares / D + eps_norm)
     first = iota((8, 1), 0) < 4
+    tiles = quarter // LANES
     for core in range(2):
-        low = gain[core * HALF : core * HALF + quarter].reshape(1, quarter)
-        high = gain[core * HALF + quarter : (core + 1) * HALF].reshape(1, quarter)
-        final = (chosen[core] * factor * jnp.where(first, low, high)).astype(jnp.bfloat16)
-        for chip in range(copies.shape[0]):
-            copies[chip, core * 8 : (core + 1) * 8, :] = final
+        for tile in range(tiles):
+            low = core * 2 * tiles + tile
+            own_gain = jnp.where(first, gain[low : low + 1], gain[low + tiles : low + tiles + 1])
+            here = slice(tile * LANES, (tile + 1) * LANES)
+            final = (chosen[core, :, here] * factor * own_gain).astype(jnp.bfloat16)
+            for chip in range(copies.shape[0]):
+                copies[chip, core * 8 : (core + 1) * 8, here] = final
 
 
 def medusa_kernel(tile, final, weights, copies):
@@ -419,21 +432,17 @@
     units = w_gate.shape[2]
     vocab = lm_head.shape[0]
 
-    squares, notes, wide_w = call(
+    squares, notes = call(
         begin_kernel,
         [accept],
-        [in_hbm(array) for array in (hidden, routes.T, gates.T, medusa_w, medusa_b)],
-        [
-            like((NODES, LANES), f32),
-            like((NODES, LANES), bf16),
-            like(medusa_w.shape[:2] + (D + LANES,), bf16),
-        ],
+        [in_hbm(hidden), in_hbm(routes.T), in_hbm(gates.T)],
+        [like((1, LANES), f32), like((NODES, LANES), bf16)],
     )
 
     packet = call(
         pack_kernel,
         [core_at],
-        [in_hbm(hidden), lax.psum(squares, TP), in_hbm(moe_gain), notes],
+        [in_hbm(hidden), lax.psum(squares, TP), in_hbm(moe_gain.reshape(-1, LANES)), notes],
         pltpu.HBM((NZ, NODES, HALF + LANES), bf16),
     )
     column = exchange(packet, "z")
@@ -445,6 +454,12 @@
         like(query.shape, bf16),
         flops=4 << 24,
         moved=4 << 20,
+    )
+    wide_w = call(
+        widen_kernel,
+        [],
+        [in_hbm(medusa_w), in_hbm(medusa_b)],
+        like(medusa_w.shape[:2] + (D + LANES,), bf16),
     )
     wide = [wide_w] + [lax.ppermute(wide_w, "y", around(NY, step)) for step in range(1, NY)]
     block_w = call(
@@ -489,37 +504,50 @@
         flops=4 * slots * HALF * units,
         moved=8 << 20,
     )
-    finished = down(
-        core_at,
-        activation,
-        swap(activation),
-        w_down,
-        other_down,
+    finished = call(
+        down_kernel,
+        [core_at],
+        [activation, swap(activation), w_down, other_down],
         pltpu.VMEM((NPLANE, NZ * CAP, HALF), bf16),
+        flops=4 * slots * HALF * units,
+        moved=6 << 20,
     )
     returned = exchange(finished, PLANE)
 
-    parts, own, *others = call(
+    parts, own, far_up, far_down, near = call(
         combine_kernel,
         [accept, z_at],
         [accepted_mix, in_hbm(mix_hi), in_hbm(mix_lo), returned, hidden],
-        [pltpu.HBM((2 * NZ, NZ, HALF // 2), bf16), pltpu.HBM((NODES, HALF), f32)]
-        + [pltpu.HBM((NODES, HALF), bf16)] * (NZ - 1),
+        [
+            pltpu.HBM((2 * NZ, NZ, HALF // 2), bf16),
+            pltpu.HBM((NODES, HALF), f32),
+            pltpu.HBM((NODES * 3 // 2, HALF), bf16),
+            pltpu.HBM((NODES * 3 // 2, HALF), bf16),
+            pltpu.HBM((len(NEAR), NODES, HALF), f32),
+        ],
         flops=4 * slots * NZ * NODES * HALF,
         moved=6 << 20,
         scratch=[pltpu.VMEM((NZ * NODES, HALF), f32)],
     )
     parts = exchange(parts, ("z", "c"))
-    sent = {}
-    for step, other in enumerate(others, 1):
-        sent[step] = lax.ppermute(other, "z", around(NZ, step))
+    from_below = in_hbm(lax.ppermute(far_up, "z", around(NZ, 2)))
+    from_above = in_hbm(lax.ppermute(far_down, "z", around(NZ, -2)))
+    relayed = call(
+        relay_kernel,
+        [],
+        [in_hbm(near), from_below, from_above],
+        [pltpu.HBM((NODES, HALF), bf16)] * len(NEAR),
+        moved=2 << 20,
+    )
+    sent = [
+        lax.ppermute(part, "z", around(NZ, step)) for step, part in zip(NEAR, relayed)
+    ]
 
     final = call(
         final_kernel,
         [],
-        [parts, in_hbm(final_gain)],
+        [parts, in_hbm(final_gain.reshape(-1, LANES))],
         pltpu.HBM((4, 16, HALF // 2), bf16),
-        unused=[in_hbm(sent[1]), in_hbm(sent[7])],
     )
     final = exchange(final, "x")
     heads = call(
@@ -535,8 +563,8 @@
         copy_kernel,
         [],
         [heads],
-        pltpu.VMEM((NPLANE, NZ, 32, LANES), bf16),
-        unused=[in_hbm(sent[2]), in_hbm(sent[6])],
+        pltpu.HBM((NPLANE, NZ, 32, LANES), bf16),
+        unused=[from_below, from_above],
     )
     heads = exchange(heads, PLANE)
     to_other = call(
@@ -546,7 +574,7 @@
         like((vocab, EXPERTS), f32),
         flops=2 * EXPERTS * D * vocab,
         moved=4 << 20,
-        unused=[in_hbm(sent[step]) for step in (3, 5, 4)],
+        unused=[in_hbm(part) for part in sent],
     )
     to_own = call(
         sums_kernel,
@@ -564,7 +592,7 @@
         moved=1 << 20,
     )
     mixture = own
-    for part in sent.values():
+    for part in sent:
         mixture = mixture + part.astype(f32)
     layer_out = (hidden.astype(f32) + mixture).astype(bf16)
     stats = exchange(stats, ("x", "y", "c"))

time: 236 us -> 229 us (0.970)
  waiting for transfers between devices: 52.9 us -> 35.6 us
  blocking collectives: 83 us -> 99 us
  starting transfers between devices: 54.6 us -> 46.3 us
  Pallas kernels: 32.9 us -> 36.4 us
    all_to_all x3 -> x4, blocking collectives: 79.5 us -> 96.4 us  [exchange(): return lax.all_to_all(value, axes, 0, 0, tiled=True)]
    ppermute x7 -> x6, waiting for transfers between devices: 23.6 us -> 10.1 us  [the longest x4 8.34 us: on_device(): lax.ppermute(part, 'z', around(NZ, step))]
    all_to_all x6 -> x5, starting transfers between devices: 29.6 us -> 22.1 us  [exchange(): return lax.all_to_all(value, axes, 0, 0, tiled=True)]
    pallas_call x16 -> x19, Pallas kernels: 28.9 us -> 36.4 us  [call(): pl.pallas_call(body, out_shape=list(outs), in_specs=[SMEM] * count + [who...]
    pallas_call x1 -> x0, Pallas kernels: 3.94 us -> none  [down(): pl.pallas_call(down_kernel, out_shape=out_shape, grid_spec=pltpu.Prefetch...]
    all_to_all x6 -> x5, waiting for transfers between devices: 19.4 us -> 15.9 us  [exchange(): return lax.all_to_all(value, axes, 0, 0, tiled=True)]
    ppermute x7 -> x6, starting transfers between devices: 9.68 us -> 7.48 us  [the longest x4 3.83 us: on_device(): lax.ppermute(part, 'z', around(NZ, step))]
  transfers between devices with their start and end apart: 22 -> 20, of which waited for: 14 -> 13; matrix products, arithmetic and copies ran while one was open for 3% -> 3% of each run, Pallas kernels for 5% -> 7%
where the time goes in v4:
time: 229 us; the launch traced here: 228 us
  blocking collectives  99 us (43%)
  starting transfers between devices  46.3 us (20%)
  Pallas kernels  36.4 us (16%)
  waiting for transfers between devices  35.6 us (16%)
  local copies, waits for them, and re-layouts  5.02 us (2%)
  other arithmetic  3.74 us (2%)
    all_to_all x4, blocking collectives, exchange(): return lax.all_to_all(value, axes, 0, 0, tiled=True)  96.4 us
    pallas_call x19, Pallas kernels, call(): pl.pallas_call(body, out_shape=list(outs), in_specs=[SMEM] * count + [who...  36.4 us
    all_to_all x5, starting transfers between devices, exchange(): return lax.all_to_all(value, axes, 0, 0, tiled=True)  22.1 us
    all_to_all x5, waiting for transfers between devices, exchange(): return lax.all_to_all(value, axes, 0, 0, tiled=True)  15.9 us
    ppermute x6, starting transfers between devices, swap(): return lax.ppermute(value, TP, SWAP)  11.7 us
    ppermute x4, waiting for transfers between devices, on_device(): lax.ppermute(part, 'z', around(NZ, step))  8.34 us
    ppermute x3, waiting for transfers between devices, on_device(): lax.ppermute(wide_w, 'y', around(NY, step))  6.52 us
    ppermute x3, starting transfers between devices, on_device(): lax.ppermute(wide_w, 'y', around(NY, step))  5.04 us
  transfers between devices with their start and end apart: 20, of which 13 were waited for; matrix products, arithmetic and copies ran while one was open for 3% of the time, Pallas kernels for 7%

profile of v4, /device:TPU:1, one launch (start us, length us, event | category | flops | bytes accessed | tf_op | source)
XLA Modules:
  0.0 228.2 jit_solution(6554999847969024313)
XLA Ops:
  0.6 3.3 %collective-permute-start.5 = (bf16[304,4096]{1,0:T(8,128)(2,1)}, bf16[304,4096]{1,0:T(8,128)(2,1)S(1)}, u32[]{:S(2)}, u32[]{:S(2)}) collective-permute-start(bf16[304,4096]{1,0:T(8,128)(2,1)} %refs_1_.9), channel_id=1, source_target_pairs={{0,1},{1,0},{2,3},{3,2},{4,5},{5,4},{6,7},{7,6},{8,9},{9,8},{10,11... | collective-permute-start | bytes 7471112 | tf_op jit(solution)/shard_map/ppermute | solution.py:32
  5.7 2.6 %psum.7.refs_2_ = f32[1,128]{1,0:T(1,128)S(1)} all-reduce(f32[1,128]{1,0:T(1,128)S(1)} %get-tuple-element.22), channel_id=1, replica_groups=mesh['x'=4,'z'=8,'y'=4,'c'=2] {'c'}, use_global_device_ids=true, to_apply=%region_0.0 | all-reduce | flops 128 | bytes 1024 | tf_op jit(solution)/shard_map/psum | solution.py:445
  8.3 2.2 shard_map.186
  10.5 6.5 %all-to-all-start = ((bf16[8,32,2176]{2,1,0:T(8,128)(2,1)}), bf16[8,32,2176]{2,1,0:T(8,128)(2,1)}, u32[]{:S(2)}, u32[]{:S(2)}) async-start(bf16[8,32,2176]{2,1,0:T(8,128)(2,1)} %shard_map.186), calls=%async_computation | async-start | bytes 2228224 | tf_op jit(solution)/shard_map/all_to_all | solution.py:40
  19.3 2.6 %collective-permute-start.1 = (bf16[2,16,4224]{2,1,0:T(8,128)(2,1)S(1)}, bf16[2,16,4224]{2,1,0:T(8,128)(2,1)S(1)}, u32[]{:S(2)}, u32[]{:S(2)}) collective-permute-start(bf16[2,16,4224]{2,1,0:T(8,128)(2,1)S(1)} %shard_map.187.refs_2_), channel_id=1, source_target_pairs={{0,4},{2,6},{4,0},{6,2},{1,5},{3,7},{5,1},{7,3},{8,12},{10,14},{12... | collective-permute-start | bytes 811016 | tf_op jit(solution)/shard_map/ppermute | solution.py:464
  23.0 2.7 %dynamic-slice_bitcast_fusion = bf16[384,2048]{1,0:T(8,128)(2,1)} fusion(bf16[1,384,4096]{2,1,0:T(8,128)(2,1)} %refs_3_.7, s32[]{:T(128)S(6)} %select_n.3), kind=kLoop, calls=%fused_computation | loop fusion | bytes 3145732 | tf_op jit(solution)/shard_map/dynamic_slice | solution.py:472
  27.2 6.5 %collective-permute-done.1.refs_4_ = bf16[2,16,4224]{2,1,0:T(8,128)(2,1)S(1)} collective-permute-done((bf16[2,16,4224]{2,1,0:T(8,128)(2,1)S(1)}, bf16[2,16,4224]{2,1,0:T(8,128)(2,1)S(1)}, u32[]{:S(2)}, u32[]{:S(2)}) %collective-permute-start.1) | collective-permute-done | bytes 270368 | tf_op jit(solution)/shard_map/ppermute | solution.py:464
  33.8 2.1 pad_maximum_fusion
  38.9 2.1 shard_map.184.refs_2_
  41.1 2.9 %shard_map.188.refs_3_.refs_2_ = bf16[2,128,4224]{2,1,0:T(8,128)(2,1)} custom-call(s32[1]{0:T(128)} %bitcast.1.refs_0_, s32[1]{0:T(128)} %bitcast.5.refs_1_, bf16[2,16,4224]{2,1,0:T(8,128)(2,1)S(1)} %shard_map.187.refs_2_, bf16[2,16,4224]{2,1,0:T(8,128)(2,1)S(1)} %collective-permute-done.refs_3_, bf16[2,16,4224]{2,1,0:T(8,128)(2,1)S(1)} %collective-permute-done.1.refs_4_, ...), custom_call_target="tpu_custom_call" | custom-call | bytes 4194304 | tf_op jit(solution)/shard_map/pallas_call | solution.py:105
  43.9 3.8 %all-to-all-done.refs_1_ = bf16[8,32,2176]{2,1,0:T(8,128)(2,1)} async-done(((bf16[8,32,2176]{2,1,0:T(8,128)(2,1)}), bf16[8,32,2176]{2,1,0:T(8,128)(2,1)}, u32[]{:S(2)}, u32[]{:S(2)}) %all-to-all-start) | async-done | bytes 1114144 | tf_op jit(solution)/shard_map/all_to_all | solution.py:40
  47.7 3.9 %shard_map.189 = (bf16[16,32,2048]{2,1,0:T(8,128)(2,1)S(1)}, bf16[512,256]{1,0:T(8,128)(2,1)}, bf16[512,256]{1,0:T(8,128)(2,1)}, bf16[16,512]{1,0:T(8,128)(2,1)S(1)}) custom-call(s32[1]{0:T(128)} %bitcast.refs_0_.refs_1_, bf16[8,32,2176]{2,1,0:T(8,128)(2,1)} %all-to-all-done.refs_1_, bf16[1,32,4096]{2,1,0:T(8,128)(2,1)} %shard_map.184.refs_2_, ...), custom_call_target="tpu_custom_call" | custom-call | flops 536870912 | bytes 4194304 | tf_op jit(solution)/shard_map/pallas_call | solution.py:105
  51.6 34.0 %all_to_all.45.refs_1_ = bf16[16,32,2048]{2,1,0:T(8,128)(2,1)S(1)} all-to-all(bf16[16,32,2048]{2,1,0:T(8,128)(2,1)S(1)} %get-tuple-element.27), channel_id=1, replica_groups=mesh['x'=4,'z'=8,'y'=4,'c'=2] {'x','y'}, dimensions={0} | all-to-all | bytes 4194304 | tf_op jit(solution)/shard_map/all_to_all | solution.py:40
  85.6 2.0 collective-permute-start.6
  87.6 2.3 %shard_map.190 = (f32[512,384]{1,0:T(8,128)S(1)}, f32[512,384]{1,0:T(8,128)S(1)}) custom-call(s32[1]{0:T(128)} %bitcast.1.refs_0_, bf16[16,32,2048]{2,1,0:T(8,128)(2,1)S(1)} %all_to_all.45.refs_1_, bf16[1,4096,384]{2,1,0:T(8,128)(2,1)S(1)} %copy-done.1, bf16[1,4096,384]{2,1,0:T(8,128)(2,1)S(1)} %copy-done.2), custom_call_target="tpu_custom_call" | custom-call | flops 1610612736 | bytes 8388608 | tf_op jit(solution)/shard_map/pallas_call | solution.py:105
  91.4 2.4 %shard_map.191.refs_1_ = bf16[512,384]{1,0:T(8,128)(2,1)S(1)} custom-call(s32[1]{0:T(128)} %bitcast.1.refs_0_, bf16[16,32,2048]{2,1,0:T(8,128)(2,1)S(1)} %collective-permute-done.6.refs_1_, bf16[1,4096,384]{2,1,0:T(8,128)(2,1)S(1)} %copy-done.1, bf16[1,4096,384]{2,1,0:T(8,128)(2,1)S(1)} %copy-done.2, f32[512,384]{1,0:T(8,128)S(1)} %get-tuple-element.28.refs_4_, ...), custom_call_target="tpu_custom_call" | custom-call | flops 1610612736 | bytes 8388608 | tf_op jit(solution)/shard_map/pallas_call | solution.py:105
  95.8 3.2 %shard_map.192 = bf16[16,32,2048]{2,1,0:T(8,128)(2,1)S(1)} custom-call(s32[1]{0:T(128)} %bitcast.1.refs_0_, bf16[512,384]{1,0:T(8,128)(2,1)S(1)} %shard_map.191.refs_1_, bf16[512,384]{1,0:T(8,128)(2,1)S(1)} %collective-permute-done.7.refs_2_, bf16[1,384,4096]{2,1,0:T(8,128)(2,1)S(1)} %copy-done.5, bf16[384,2048]{1,0:T(8,128)(2,1)} %collective-permute-done.4.refs_4_), custom_call_target="tpu_custom_call" | custom-call | flops 1610612736 | bytes 6291456 | tf_op jit(solution)/shard_map/pallas_call | solution.py:105
  99.0 30.7 %all_to_all.46.refs_5_ = bf16[16,32,2048]{2,1,0:T(8,128)(2,1)S(1)} all-to-all(bf16[16,32,2048]{2,1,0:T(8,128)(2,1)S(1)} %shard_map.192), channel_id=1, replica_groups=mesh['x'=4,'z'=8,'y'=4,'c'=2] {'x','y'}, dimensions={0} | all-to-all | bytes 4194304 | tf_op jit(solution)/shard_map/all_to_all | solution.py:40
  129.7 3.9 %shard_map.193 = (bf16[16,8,1024]{2,1,0:T(8,128)(2,1)}, f32[32,2048]{1,0:T(8,128)}, bf16[48,2048]{1,0:T(8,128)(2,1)}, bf16[48,2048]{1,0:T(8,128)(2,1)}, f32[4,32,2048]{2,1,0:T(8,128)}) custom-call(s32[1]{0:T(128)S(6)} %copy.21.refs_0_, s32[1]{0:T(128)} %bitcast.refs_0_.refs_1_, bf16[16,512]{1,0:T(8,128)(2,1)S(1)} %get-tuple-element.24.refs_2_, ...), custom_call_target="tpu_custom_call" | custom-call | flops 1073741824 | bytes 6291456 | tf_op jit(solution)/shard_map/pallas_call | solution.py:105
  133.6 17.2 %all_to_all.47.refs_0_ = bf16[16,8,1024]{2,1,0:T(8,128)(2,1)S(1)} all-to-all(bf16[16,8,1024]{2,1,0:T(8,128)(2,1)} %get-tuple-element.38), channel_id=1, replica_groups=mesh['x'=4,'z'=8,'y'=4,'c'=2] {'z','c'}, dimensions={0} | all-to-all | bytes 524288 | tf_op jit(solution)/shard_map/all_to_all | solution.py:40
  152.5 3.3 %all-to-all-start.4 = ((bf16[4,16,1024]{2,1,0:T(8,128)(2,1)}), bf16[4,16,1024]{2,1,0:T(8,128)(2,1)S(1)}, u32[]{:S(2)}, u32[]{:S(2)}) async-start(bf16[4,16,1024]{2,1,0:T(8,128)(2,1)} %shard_map.195), calls=%async_computation.4 | async-start | bytes 262144 | tf_op jit(solution)/shard_map/all_to_all | solution.py:40
  156.1 3.4 %collective-permute-start.9 = (bf16[48,2048]{1,0:T(8,128)(2,1)}, bf16[48,2048]{1,0:T(8,128)(2,1)S(1)}, u32[]{:S(2)}, u32[]{:S(2)}) collective-permute-start(bf16[48,2048]{1,0:T(8,128)(2,1)} %get-tuple-element.33), channel_id=1, source_target_pairs={{0,48},{8,56},{16,0},{24,8},{32,16},{40,24},{48,32},{56,40},{1,49}... | collective-permute-start | bytes 589832 | tf_op jit(solution)/shard_map/ppermute | solution.py:534
  159.5 2.0 all-to-all-done.4.refs_1_
  162.9 3.4 %all-to-all-start.5 = ((bf16[8,32,128]{2,1,0:T(8,128)(2,1)}), bf16[8,32,128]{2,1,0:T(8,128)(2,1)S(1)}, u32[]{:S(2)}, u32[]{:S(2)}) async-start(bf16[8,32,128]{2,1,0:T(8,128)(2,1)} %shard_map.196), calls=%async_computation.5 | async-start | bytes 131072 | tf_op jit(solution)/shard_map/all_to_all | solution.py:40
  168.0 5.2 %all-to-all-done.5.refs_0_ = bf16[8,32,128]{2,1,0:T(8,128)(2,1)S(1)} async-done(((bf16[8,32,128]{2,1,0:T(8,128)(2,1)}), bf16[8,32,128]{2,1,0:T(8,128)(2,1)S(1)}, u32[]{:S(2)}, u32[]{:S(2)}) %all-to-all-start.5) | async-done | bytes 65568 | tf_op jit(solution)/shard_map/all_to_all | solution.py:40
  174.4 3.8 %all-to-all-start.6 = ((bf16[16,8,32,128]{3,2,1,0:T(8,128)(2,1)}), bf16[16,8,32,128]{3,2,1,0:T(8,128)(2,1)S(1)}, u32[]{:S(2)}, u32[]{:S(2)}) async-start(bf16[16,8,32,128]{3,2,1,0:T(8,128)(2,1)} %shard_map.197), calls=%async_computation.6 | async-start | bytes 2097152 | tf_op jit(solution)/shard_map/all_to_all | solution.py:40
  178.2 2.1 shard_map.194
  185.9 6.3 %collective-permute-done.12.refs_4_ = bf16[32,2048]{1,0:T(8,128)(2,1)S(1)} collective-permute-done((bf16[32,2048]{1,0:T(8,128)(2,1)}, bf16[32,2048]{1,0:T(8,128)(2,1)S(1)}, u32[]{:S(2)}, u32[]{:S(2)}) %collective-permute-start.12) | collective-permute-done | bytes 131104 | tf_op jit(solution)/shard_map/ppermute | solution.py:543
  194.7 2.8 %collective-permute-start.14 = (f32[304,128]{1,0:T(8,128)S(1)}, f32[304,128]{1,0:T(8,128)S(1)}, u32[]{:S(2)}, u32[]{:S(2)}) collective-permute-start(f32[304,128]{1,0:T(8,128)S(1)} %shard_map.199), channel_id=1, source_target_pairs={{0,1},{1,0},{2,3},{3,2},{4,5},{5,4},{6,7},{7,6},{8,9},{9,8},{10,11... | collective-permute-start | bytes 466952 | tf_op jit(solution)/shard_map/ppermute | solution.py:32
  199.6 14.4 %all_to_all.48.refs_0_ = f32[32,4,128]{2,1,0:T(4,128)S(1)} all-to-all(f32[32,4,128]{2,1,0:T(4,128)} %get-tuple-element.39), channel_id=1, replica_groups=mesh['x'=4,'z'=8,'y'=4,'c'=2] {'x','y','c'}, dimensions={0} | all-to-all | bytes 131072 | tf_op jit(solution)/shard_map/all_to_all | solution.py:40
  214.6 5.2 %all-to-all-start.8 = ((f32[8,4,128]{2,1,0:T(4,128)}), f32[8,4,128]{2,1,0:T(4,128)S(1)}, u32[]{:S(2)}, u32[]{:S(2)}) async-start(f32[8,4,128]{2,1,0:T(4,128)} %shard_map.201), calls=%async_computation.8 | async-start | bytes 32768 | tf_op jit(solution)/shard_map/all_to_all | solution.py:40
  221.5 4.9 %all-to-all-done.8.refs_0_ = f32[8,4,128]{2,1,0:T(4,128)S(1)} async-done(((f32[8,4,128]{2,1,0:T(4,128)}), f32[8,4,128]{2,1,0:T(4,128)S(1)}, u32[]{:S(2)}, u32[]{:S(2)}) %all-to-all-start.8) | async-done | bytes 16416 | tf_op jit(solution)/shard_map/all_to_all | solution.py:40
  (79 shorter events, 32.3 us)
Async XLA Ops:
  0.6 47.0 %collective-permute-start.5 = (bf16[304,4096]{1,0:T(8,128)(2,1)}, bf16[304,4096]{1,0:T(8,128)(2,1)S(1)}, u32[]{:S(2)}, u32[]{:S(2)}) collective-permute-start(bf16[304,4096]{1,0:T(8,128)(2,1)} %refs_1_.9), channel_id=1, source_target_pairs={{0,1},{1,0},{2,3},{3,2},{4,5},{5,4},{6,7},{7,6},{8,9},{9,8},{10,11... | collective-permute-start | bytes 7471112 | tf_op jit(solution)/shard_map/ppermute | solution.py:32
  10.5 37.2 %all-to-all-start = ((bf16[8,32,2176]{2,1,0:T(8,128)(2,1)}), bf16[8,32,2176]{2,1,0:T(8,128)(2,1)}, u32[]{:S(2)}, u32[]{:S(2)}) async-start(bf16[8,32,2176]{2,1,0:T(8,128)(2,1)} %shard_map.186), calls=%async_computation | async-start | bytes 2228224 | tf_op jit(solution)/shard_map/all_to_all | solution.py:40
  18.0 9.3 %collective-permute-start = (bf16[2,16,4224]{2,1,0:T(8,128)(2,1)S(1)}, bf16[2,16,4224]{2,1,0:T(8,128)(2,1)S(1)}, u32[]{:S(2)}, u32[]{:S(2)}) collective-permute-start(bf16[2,16,4224]{2,1,0:T(8,128)(2,1)S(1)} %shard_map.187.refs_2_), channel_id=1, source_target_pairs={{0,2},{2,4},{4,6},{6,0},{1,3},{3,5},{5,7},{7,1},{8,10},{10,12},{12... | collective-permute-start | bytes 811016 | tf_op jit(solution)/shard_map/ppermute | solution.py:464
  19.3 14.4 %collective-permute-start.1 = (bf16[2,16,4224]{2,1,0:T(8,128)(2,1)S(1)}, bf16[2,16,4224]{2,1,0:T(8,128)(2,1)S(1)}, u32[]{:S(2)}, u32[]{:S(2)}) collective-permute-start(bf16[2,16,4224]{2,1,0:T(8,128)(2,1)S(1)} %shard_map.187.refs_2_), channel_id=1, source_target_pairs={{0,4},{2,6},{4,0},{6,2},{1,5},{3,7},{5,1},{7,3},{8,12},{10,14},{12... | collective-permute-start | bytes 811016 | tf_op jit(solution)/shard_map/ppermute | solution.py:464
  22.0 11.8 %collective-permute-start.2 = (bf16[2,16,4224]{2,1,0:T(8,128)(2,1)S(1)}, bf16[2,16,4224]{2,1,0:T(8,128)(2,1)}, u32[]{:S(2)}, u32[]{:S(2)}) collective-permute-start(bf16[2,16,4224]{2,1,0:T(8,128)(2,1)S(1)} %shard_map.187.refs_2_), channel_id=1, source_target_pairs={{0,6},{2,0},{4,2},{6,4},{1,7},{3,1},{5,3},{7,5},{8,14},{10,8},{12,... | collective-permute-start | bytes 811016 | tf_op jit(solution)/shard_map/ppermute | solution.py:464
  25.7 12.2 %copy-start.11 = (bf16[2,1,32,256]{3,2,1,0:T(8,128)(2,1)S(1)}, bf16[2,1,32,256]{3,2,1,0:T(8,128)(2,1)}, u32[]{:S(2)}) copy-start(bf16[2,1,32,256]{3,2,1,0:T(8,128)(2,1)} %refs_2_.3) | copy-start | bytes 98308
  25.7 12.2 %copy-start.12 = (s32[1,32]{1,0:T(1,128)S(1)}, s32[1,32]{1,0:T(1,128)}, u32[]{:S(2)}) copy-start(s32[1,32]{1,0:T(1,128)} %refs_4_.1) | copy-start | bytes 388
  25.7 18.2 %collective-permute-start.4 = (bf16[384,2048]{1,0:T(8,128)(2,1)}, bf16[384,2048]{1,0:T(8,128)(2,1)}, u32[]{:S(2)}, u32[]{:S(2)}) collective-permute-start(bf16[384,2048]{1,0:T(8,128)(2,1)} %dynamic-slice_bitcast_fusion), channel_id=1, source_target_pairs={{0,1},{1,0},{2,3},{3,2},{4,5},{5,4},{6,7},{7,6},{8,9},{9,8},{10,11... | collective-permute-start | bytes 4718600 | tf_op jit(solution)/shard_map/ppermute | solution.py:32
  35.9 5.2 %collective-permute-start.3 = (bf16[4,2,16,4224]{3,2,1,0:T(8,128)(2,1)}, bf16[4,2,16,4224]{3,2,1,0:T(8,128)(2,1)}, u32[]{:S(2)}, u32[]{:S(2)}) collective-permute-start(bf16[4,2,16,4224]{3,2,1,0:T(8,128)(2,1)} %pad_maximum_fusion), channel_id=1, source_target_pairs={{0,1},{1,0},{2,3},{3,2},{4,5},{5,4},{6,7},{7,6},{8,9},{9,8},{10,11... | collective-permute-start | bytes 3244040 | tf_op jit(solution)/shard_map/ppermute | solution.py:32
  47.7 39.9 %copy-start.2 = (bf16[1,4096,384]{2,1,0:T(8,128)(2,1)S(1)}, bf16[1,4096,384]{2,1,0:T(8,128)(2,1)}, u32[]{:S(2)}) copy-start(bf16[1,4096,384]{2,1,0:T(8,128)(2,1)} %refs_3_.6) | copy-start | bytes 9437188
  51.6 36.0 %copy-start.1 = (bf16[1,4096,384]{2,1,0:T(8,128)(2,1)S(1)}, bf16[1,4096,384]{2,1,0:T(8,128)(2,1)}, u32[]{:S(2)}) copy-start(bf16[1,4096,384]{2,1,0:T(8,128)(2,1)} %refs_2_.5) | copy-start | bytes 9437188
  85.6 5.8 %collective-permute-start.6 = (bf16[16,32,2048]{2,1,0:T(8,128)(2,1)S(1)}, bf16[16,32,2048]{2,1,0:T(8,128)(2,1)S(1)}, u32[]{:S(2)}, u32[]{:S(2)}) collective-permute-start(bf16[16,32,2048]{2,1,0:T(8,128)(2,1)S(1)} %all_to_all.45.refs_1_), channel_id=1, source_target_pairs={{0,1},{1,0},{2,3},{3,2},{4,5},{5,4},{6,7},{7,6},{8,9},{9,8},{10,11... | collective-permute-start | bytes 6291464 | tf_op jit(solution)/shard_map/ppermute | solution.py:32
  93.8 2.0 collective-permute-start.7
  99.0 30.7 %copy-start.7 = (bf16[32,2048]{1,0:T(8,128)(2,1)S(1)}, bf16[32,2048]{1,0:T(8,128)(2,1)}, u32[]{:S(2)}) copy-start(bf16[32,2048]{1,0:T(8,128)(2,1)} %refs_6_.1) | copy-start | bytes 393220
  129.7 31.7 %copy-start = (bf16[2,128,4224]{2,1,0:T(8,128)(2,1)S(1)}, bf16[2,128,4224]{2,1,0:T(8,128)(2,1)}, u32[]{:S(2)}) copy-start(bf16[2,128,4224]{2,1,0:T(8,128)(2,1)} %shard_map.188.refs_3_.refs_2_) | copy-start | bytes 6488068
  152.5 8.9 %all-to-all-start.4 = ((bf16[4,16,1024]{2,1,0:T(8,128)(2,1)}), bf16[4,16,1024]{2,1,0:T(8,128)(2,1)S(1)}, u32[]{:S(2)}, u32[]{:S(2)}) async-start(bf16[4,16,1024]{2,1,0:T(8,128)(2,1)} %shard_map.195), calls=%async_computation.4 | async-start | bytes 262144 | tf_op jit(solution)/shard_map/all_to_all | solution.py:40
  155.8 12.1 %collective-permute-start.8 = (bf16[48,2048]{1,0:T(8,128)(2,1)}, bf16[48,2048]{1,0:T(8,128)(2,1)S(1)}, u32[]{:S(2)}, u32[]{:S(2)}) collective-permute-start(bf16[48,2048]{1,0:T(8,128)(2,1)} %get-tuple-element.32), channel_id=1, source_target_pairs={{0,16},{8,24},{16,32},{24,40},{32,48},{40,56},{48,0},{56,8},{1,17}... | collective-permute-start | bytes 589832 | tf_op jit(solution)/shard_map/ppermute | solution.py:533
  156.1 12.0 %collective-permute-start.9 = (bf16[48,2048]{1,0:T(8,128)(2,1)}, bf16[48,2048]{1,0:T(8,128)(2,1)S(1)}, u32[]{:S(2)}, u32[]{:S(2)}) collective-permute-start(bf16[48,2048]{1,0:T(8,128)(2,1)} %get-tuple-element.33), channel_id=1, source_target_pairs={{0,48},{8,56},{16,0},{24,8},{32,16},{40,24},{48,32},{56,40},{1,49}... | collective-permute-start | bytes 589832 | tf_op jit(solution)/shard_map/ppermute | solution.py:534
  162.9 10.4 %all-to-all-start.5 = ((bf16[8,32,128]{2,1,0:T(8,128)(2,1)}), bf16[8,32,128]{2,1,0:T(8,128)(2,1)S(1)}, u32[]{:S(2)}, u32[]{:S(2)}) async-start(bf16[8,32,128]{2,1,0:T(8,128)(2,1)} %shard_map.196), calls=%async_computation.5 | async-start | bytes 131072 | tf_op jit(solution)/shard_map/all_to_all | solution.py:40
  174.4 19.4 %copy-start.4 = (bf16[304,4096]{1,0:T(8,128)(2,1)S(1)}, bf16[304,4096]{1,0:T(8,128)(2,1)}, u32[]{:S(2)}) copy-start(bf16[304,4096]{1,0:T(8,128)(2,1)} %copy-done.3) | copy-start | bytes 7471108
  174.4 19.4 %all-to-all-start.6 = ((bf16[16,8,32,128]{3,2,1,0:T(8,128)(2,1)}), bf16[16,8,32,128]{3,2,1,0:T(8,128)(2,1)S(1)}, u32[]{:S(2)}, u32[]{:S(2)}) async-start(bf16[16,8,32,128]{3,2,1,0:T(8,128)(2,1)} %shard_map.197), calls=%async_computation.6 | async-start | bytes 2097152 | tf_op jit(solution)/shard_map/all_to_all | solution.py:40
  180.3 5.5 %collective-permute-start.13 = (bf16[32,2048]{1,0:T(8,128)(2,1)}, bf16[32,2048]{1,0:T(8,128)(2,1)S(1)}, u32[]{:S(2)}, u32[]{:S(2)}) collective-permute-start(bf16[32,2048]{1,0:T(8,128)(2,1)} %get-tuple-element.37), channel_id=1, source_target_pairs={{0,48},{8,56},{16,0},{24,8},{32,16},{40,24},{48,32},{56,40},{1,49}... | collective-permute-start | bytes 393224 | tf_op jit(solution)/shard_map/ppermute | solution.py:543
  181.8 10.4 %collective-permute-start.12 = (bf16[32,2048]{1,0:T(8,128)(2,1)}, bf16[32,2048]{1,0:T(8,128)(2,1)S(1)}, u32[]{:S(2)}, u32[]{:S(2)}) collective-permute-start(bf16[32,2048]{1,0:T(8,128)(2,1)} %get-tuple-element.36), channel_id=1, source_target_pairs={{0,56},{8,0},{16,8},{24,16},{32,24},{40,32},{48,40},{56,48},{1,57}... | collective-permute-start | bytes 393224 | tf_op jit(solution)/shard_map/ppermute | solution.py:543
  182.8 9.4 %collective-permute-start.11 = (bf16[32,2048]{1,0:T(8,128)(2,1)}, bf16[32,2048]{1,0:T(8,128)(2,1)S(1)}, u32[]{:S(2)}, u32[]{:S(2)}) collective-permute-start(bf16[32,2048]{1,0:T(8,128)(2,1)} %get-tuple-element.35), channel_id=1, source_target_pairs={{0,16},{8,24},{16,32},{24,40},{32,48},{40,56},{48,0},{56,8},{1,17}... | collective-permute-start | bytes 393224 | tf_op jit(solution)/shard_map/ppermute | solution.py:543
  183.7 10.1 %collective-permute-start.10 = (bf16[32,2048]{1,0:T(8,128)(2,1)}, bf16[32,2048]{1,0:T(8,128)(2,1)}, u32[]{:S(2)}, u32[]{:S(2)}) collective-permute-start(bf16[32,2048]{1,0:T(8,128)(2,1)} %get-tuple-element.34), channel_id=1, source_target_pairs={{0,8},{8,16},{16,24},{24,32},{32,40},{40,48},{48,56},{56,0},{1,9},... | collective-permute-start | bytes 393224 | tf_op jit(solution)/shard_map/ppermute | solution.py:543
  194.6 25.2 %copy-start.8 = (bf16[32,2048]{1,0:T(8,128)(2,1)S(1)}, bf16[32,2048]{1,0:T(8,128)(2,1)}, u32[]{:S(2)}) copy-start(bf16[32,2048]{1,0:T(8,128)(2,1)} %refs_6_.1) | copy-start | bytes 393220
  194.6 25.2 %copy-start.16 = (bf16[32,2048]{1,0:T(8,128)(2,1)S(1)}, bf16[32,2048]{1,0:T(8,128)(2,1)}, u32[]{:S(2)}) copy-start(bf16[32,2048]{1,0:T(8,128)(2,1)} %copy-done.15) | copy-start | bytes 393220
  194.6 25.2 %copy-start.18 = (bf16[32,2048]{1,0:T(8,128)(2,1)S(1)}, bf16[32,2048]{1,0:T(8,128)(2,1)}, u32[]{:S(2)}) copy-start(bf16[32,2048]{1,0:T(8,128)(2,1)} %copy-done.17) | copy-start | bytes 393220
  194.6 25.2 %copy-start.20 = (bf16[32,2048]{1,0:T(8,128)(2,1)S(1)}, bf16[32,2048]{1,0:T(8,128)(2,1)}, u32[]{:S(2)}) copy-start(bf16[32,2048]{1,0:T(8,128)(2,1)} %copy-done.19) | copy-start | bytes 393220
  194.7 25.2 %copy-start.21 = (f32[32,2048]{1,0:T(8,128)S(1)}, f32[32,2048]{1,0:T(8,128)}, u32[]{:S(2)}) copy-start(f32[32,2048]{1,0:T(8,128)} %get-tuple-element.30) | copy-start | bytes 786436
  194.7 3.8 %collective-permute-start.14 = (f32[304,128]{1,0:T(8,128)S(1)}, f32[304,128]{1,0:T(8,128)S(1)}, u32[]{:S(2)}, u32[]{:S(2)}) collective-permute-start(f32[304,128]{1,0:T(8,128)S(1)} %shard_map.199), channel_id=1, source_target_pairs={{0,1},{1,0},{2,3},{3,2},{4,5},{5,4},{6,7},{7,6},{8,9},{9,8},{10,11... | collective-permute-start | bytes 466952 | tf_op jit(solution)/shard_map/ppermute | solution.py:32
  214.6 11.8 %all-to-all-start.8 = ((f32[8,4,128]{2,1,0:T(4,128)}), f32[8,4,128]{2,1,0:T(4,128)S(1)}, u32[]{:S(2)}, u32[]{:S(2)}) async-start(f32[8,4,128]{2,1,0:T(4,128)} %shard_map.201), calls=%async_computation.8 | async-start | bytes 32768 | tf_op jit(solution)/shard_map/all_to_all | solution.py:40
  (10 other events, 43.3 us)

commit v5 on v4

--- a/solution.py
+++ b/solution.py
@@ -24,7 +24,7 @@
 LANES = 128
 NEAR = (1, 2, -1, -2)
 BLOCK = 512
-VMEM_LIMIT = 40 << 20
+VMEM_LIMIT = 24 << 20
 SWAP = [(0, 1), (1, 0)]
 
 
@@ -147,17 +147,17 @@
             ]
 
 
-def begin_kernel(accept, hidden, routes, gates, squares, notes):
-    rows = hidden[...].astype(jnp.float32)
-    here = iota((NODES, LANES), 0) == iota((NODES, LANES), 1)
-    sums = jnp.sum(rows * rows, -1, keepdims=True)
-    squares[...] = jnp.sum(jnp.where(here, sums, 0.0), 0, keepdims=True)
+def begin_kernel(accept, hidden, routes, gates, packet):
     share = gates[...] / jnp.sum(gates[...], 0, keepdims=True)
     share_hi = share.astype(jnp.bfloat16).astype(jnp.float32)
     flag = (iota((TOPK, NODES), 1) == accept[0]).astype(jnp.float32)
     stack = [routes[...].astype(jnp.float32), share_hi, share - share_hi, flag]
     stack = jnp.concatenate(stack, 0).astype(jnp.bfloat16)
-    notes[...] = first_dot(stack, as_bf16(here)).astype(jnp.bfloat16)
+    here = iota((NODES, LANES), 0) == iota((NODES, LANES), 1)
+    notes = first_dot(stack, as_bf16(here)).astype(jnp.bfloat16)
+    for chip in range(NZ):
+        packet[chip, :, :HALF] = hidden[...]
+        packet[chip, :, HALF:] = notes
 
 
 def widen_kernel(weights, bias, wide):
@@ -184,22 +184,6 @@
             weights[head, here, :] = own[step][head]
             here = pl.ds(pl.multiple_of((place + 1 - core[0]) * block, block), block)
             weights[head, here, :] = other[step, head]
-
-
-def pack_kernel(core, hidden, squares, gain, notes, packet):
-    here = iota((NODES, LANES), 0) == iota((NODES, LANES), 1)
-    sums = jnp.sum(jnp.where(here, squares[...], 0.0), 1, keepdims=True)
-    factor = lax.rsqrt(sums / D + eps_norm)
-    tiles = HALF // LANES
-    for tile in range(tiles):
-        own_gain = gain[pl.ds(core[0] * tiles + tile, 1), :]
-        here = slice(tile * LANES, (tile + 1) * LANES)
-        normed = hidden[:, here].astype(jnp.float32) * factor * own_gain
-        normed = normed.astype(jnp.bfloat16)
-        for chip in range(NZ):
-            packet[chip, :, here] = normed
-    for chip in range(NZ):
-        packet[chip, :, HALF:] = notes[...]
 
 
 def route_kernel(my_z, column, outgoing, mix_hi, mix_lo, accepted_mix):
@@ -241,18 +225,43 @@
     accepted_mix[NZ:] = last_dot(accepted, mix_lo[...]).astype(jnp.bfloat16)
 
 
-def half_sums(core, rows, w_gate, w_up):
+def squares_kernel(arrived, squares):
+    count = squares.shape[0] * LANES
+    total = jnp.zeros((count, LANES), jnp.float32)
+    for tile in range(HALF // LANES):
+        here = slice(tile * LANES, (tile + 1) * LANES)
+        values = arrived[:, :, here].reshape(count, LANES).astype(jnp.float32)
+        total = total + values * values
+    total = jnp.sum(total, -1, keepdims=True)
+    here = iota((LANES, LANES), 0) == iota((LANES, LANES), 1)
+    for place in range(squares.shape[0]):
+        part = total[place * LANES : (place + 1) * LANES]
+        squares[place : place + 1, :] = jnp.sum(jnp.where(here, part, 0.0), 0, keepdims=True)
+
+
+def half_sums(core, arrived, own, other, gain, w_gate, w_up, rows):
+    count = rows.shape[0]
+    tiles = HALF // LANES
+    sums = own[...] + other[...]
+    sums = [as_column(sums[place : place + 1, :]) for place in range(count // LANES)]
+    factor = lax.rsqrt(jnp.concatenate(sums, 0) / D + eps_norm)
+    for tile in range(tiles):
+        here = slice(tile * LANES, (tile + 1) * LANES)
+        values = arrived[:, :, here].reshape(count, LANES).astype(jnp.float32)
+        values = values * factor * gain[pl.ds(core * tiles + tile, 1), :]
+        rows[:, here] = values.astype(jnp.bfloat16)
     here = pl.ds(pl.multiple_of(core * HALF, HALF), HALF)
-    rows = rows[...].reshape(-1, HALF)
-    return dot32(rows, w_gate[0, here, :]), dot32(rows, w_up[0, here, :])
-
-
-def first_half_kernel(core, rows, w_gate, w_up, gate, up):
-    gate[...], up[...] = half_sums(core[0], rows, w_gate, w_up)
-
-
-def second_half_kernel(core, rows, w_gate, w_up, gate, up, activation):
-    gate_part, up_part = half_sums(1 - core[0], rows, w_gate, w_up)
+    return dot32(rows[...], w_gate[0, here, :]), dot32(rows[...], w_up[0, here, :])
+
+
+def first_half_kernel(core, arrived, own, other, gain, w_gate, w_up, gate, up, rows):
+    gate[...], up[...] = half_sums(core[0], arrived, own, other, gain, w_gate, w_up, rows)
+
+
+def second_half_kernel(
+    core, arrived, own, other, gain, w_gate, w_up, gate, up, activation, rows
+):
+    gate_part, up_part = half_sums(1 - core[0], arrived, own, other, gain, w_gate, w_up, rows)
     activation[...] = (silu(gate[...] + gate_part) * (up[...] + up_part)).astype(jnp.bfloat16)
 
 
@@ -432,17 +441,10 @@
     units = w_gate.shape[2]
     vocab = lm_head.shape[0]
 
-    squares, notes = call(
+    packet = call(
         begin_kernel,
         [accept],
         [in_hbm(hidden), in_hbm(routes.T), in_hbm(gates.T)],
-        [like((1, LANES), f32), like((NODES, LANES), bf16)],
-    )
-
-    packet = call(
-        pack_kernel,
-        [core_at],
-        [in_hbm(hidden), lax.psum(squares, TP), in_hbm(moe_gain.reshape(-1, LANES)), notes],
         pltpu.HBM((NZ, NODES, HALF + LANES), bf16),
     )
     column = exchange(packet, "z")
@@ -488,21 +490,26 @@
         unused=[in_hbm(attended), in_hbm(block_w), in_hbm(other_down), other_lm],
     )
     arrived = exchange(outgoing, PLANE)
+    squares = call(squares_kernel, [], [arrived], like((slots // LANES, LANES), f32))
+    both = [squares, swap(squares)]
+    gain = moe_gain.reshape(-1, LANES)
     sums = call(
         first_half_kernel,
         [core_at],
-        [arrived, w_gate, w_up],
+        [arrived, *both, gain, w_gate, w_up],
         [like((slots, units), f32)] * 2,
         flops=4 * slots * HALF * units,
         moved=8 << 20,
+        scratch=[pltpu.VMEM((slots, HALF), bf16)],
     )
     activation = call(
         second_half_kernel,
         [core_at],
-        [swap(arrived), w_gate, w_up, *sums],
+        [swap(arrived), *both, gain, w_gate, w_up, *sums],
         like((slots, units), bf16),
         flops=4 * slots * HALF * units,
         moved=8 << 20,
+        scratch=[pltpu.VMEM((slots, HALF), bf16)],
     )
     finished = call(
         down_kernel,
@@ -564,7 +571,7 @@
         [],
         [heads],
         pltpu.HBM((NPLANE, NZ, 32, LANES), bf16),
-        unused=[from_below, from_above],
+        unused=[in_hbm(relayed[0])],
     )
     heads = exchange(heads, PLANE)
     to_other = call(

time: 229 us -> 227 us (level)
  blocking collectives: 99 us -> 96.3 us
  starting transfers between devices: 46.3 us -> 43.9 us
    all_to_all x5, waiting for transfers between devices: 15.9 us -> 13 us  [exchange(): return lax.all_to_all(value, axes, 0, 0, tiled=True)]
    psum x1 -> x0, blocking collectives: 2.6 us -> none  [on_device(): lax.psum(squares, TP)]
    ppermute x6 -> x7, starting transfers between devices: 11.7 us -> 9.83 us  [swap(): return lax.ppermute(value, TP, SWAP)]
    ppermute x6 -> x7, waiting for transfers between devices: 3.01 us -> 4.58 us  [swap(): return lax.ppermute(value, TP, SWAP)]
  transfers between devices with their start and end apart: 20 -> 21, of which waited for: 13 -> 14; matrix products, arithmetic and copies ran while one was open for 3% -> 3% of each run, Pallas kernels for 7% -> 7%
where the time goes in v5:
time: 227 us; the launch traced here: 225 us
  blocking collectives  96.3 us (42%)
  starting transfers between devices  43.9 us (19%)
  waiting for transfers between devices  37.1 us (16%)
  Pallas kernels  36.5 us (16%)
  local copies, waits for them, and re-layouts  5.66 us (2%)
  other arithmetic  3.75 us (2%)
    all_to_all x4, blocking collectives, exchange(): return lax.all_to_all(value, axes, 0, 0, tiled=True)  96.3 us
    pallas_call x19, Pallas kernels, call(): pl.pallas_call(body, out_shape=list(outs), in_specs=[SMEM] * count + [who...  36.5 us
    all_to_all x5, starting transfers between devices, exchange(): return lax.all_to_all(value, axes, 0, 0, tiled=True)  20.2 us
    all_to_all x5, waiting for transfers between devices, exchange(): return lax.all_to_all(value, axes, 0, 0, tiled=True)  13 us
    ppermute x4, waiting for transfers between devices, on_device(): lax.ppermute(part, 'z', around(NZ, step))  10.4 us
    ppermute x7, starting transfers between devices, swap(): return lax.ppermute(value, TP, SWAP)  9.83 us
    ppermute x3, waiting for transfers between devices, on_device(): lax.ppermute(wide_w, 'y', around(NY, step))  7.3 us
    ppermute x4, starting transfers between devices, on_device(): lax.ppermute(part, 'z', around(NZ, step))  5.15 us
  transfers between devices with their start and end apart: 21, of which 14 were waited for; matrix products, arithmetic and copies ran while one was open for 3% of the time, Pallas kernels for 7%

profile of v5, /device:TPU:1, one launch (start us, length us, event | category | flops | bytes accessed | tf_op | source)
XLA Modules:
  0.0 225.5 jit_solution(9088322604209898999)
XLA Ops:
  0.6 3.3 %collective-permute-start.5 = (bf16[304,4096]{1,0:T(8,128)(2,1)}, bf16[304,4096]{1,0:T(8,128)(2,1)S(1)}, u32[]{:S(2)}, u32[]{:S(2)}) collective-permute-start(bf16[304,4096]{1,0:T(8,128)(2,1)} %refs_1_.7), channel_id=1, source_target_pairs={{0,1},{1,0},{2,3},{3,2},{4,5},{5,4},{6,7},{7,6},{8,9},{9,8},{10,11... | collective-permute-start | bytes 7471112 | tf_op jit(solution)/shard_map/ppermute | solution.py:32
  4.6 2.2 shard_map.185
  6.8 6.5 %all-to-all-start = ((bf16[8,32,2176]{2,1,0:T(8,128)(2,1)}), bf16[8,32,2176]{2,1,0:T(8,128)(2,1)}, u32[]{:S(2)}, u32[]{:S(2)}) async-start(bf16[8,32,2176]{2,1,0:T(8,128)(2,1)} %shard_map.185), calls=%async_computation | async-start | bytes 2228224 | tf_op jit(solution)/shard_map/all_to_all | solution.py:40
  15.6 2.6 %collective-permute-start.1 = (bf16[2,16,4224]{2,1,0:T(8,128)(2,1)S(1)}, bf16[2,16,4224]{2,1,0:T(8,128)(2,1)S(1)}, u32[]{:S(2)}, u32[]{:S(2)}) collective-permute-start(bf16[2,16,4224]{2,1,0:T(8,128)(2,1)S(1)} %shard_map.186.refs_2_), channel_id=1, source_target_pairs={{0,4},{2,6},{4,0},{6,2},{1,5},{3,7},{5,1},{7,3},{8,12},{10,14},{12... | collective-permute-start | bytes 811016 | tf_op jit(solution)/shard_map/ppermute | solution.py:466
  19.3 2.7 %dynamic-slice_bitcast_fusion = bf16[384,2048]{1,0:T(8,128)(2,1)} fusion(bf16[1,384,4096]{2,1,0:T(8,128)(2,1)} %refs_3_.3, s32[]{:T(128)S(6)} %select_n.3), kind=kLoop, calls=%fused_computation | loop fusion | bytes 3145732 | tf_op jit(solution)/shard_map/dynamic_slice | solution.py:474
  23.6 6.9 %collective-permute-done.1.refs_4_ = bf16[2,16,4224]{2,1,0:T(8,128)(2,1)S(1)} collective-permute-done((bf16[2,16,4224]{2,1,0:T(8,128)(2,1)S(1)}, bf16[2,16,4224]{2,1,0:T(8,128)(2,1)S(1)}, u32[]{:S(2)}, u32[]{:S(2)}) %collective-permute-start.1) | collective-permute-done | bytes 270368 | tf_op jit(solution)/shard_map/ppermute | solution.py:466
  30.5 2.1 pad_maximum_fusion
  35.2 2.1 shard_map.184.refs_2_
  37.4 2.9 %shard_map.187.refs_3_.refs_2_ = bf16[2,128,4224]{2,1,0:T(8,128)(2,1)} custom-call(s32[1]{0:T(128)} %bitcast.3.refs_0_, s32[1]{0:T(128)} %bitcast.4.refs_1_, bf16[2,16,4224]{2,1,0:T(8,128)(2,1)S(1)} %shard_map.186.refs_2_, bf16[2,16,4224]{2,1,0:T(8,128)(2,1)S(1)} %collective-permute-done.refs_3_, bf16[2,16,4224]{2,1,0:T(8,128)(2,1)S(1)} %collective-permute-done.1.refs_4_, ...), custom_call_target="tpu_custom_call" | custom-call | bytes 4194304 | tf_op jit(solution)/shard_map/pallas_call | solution.py:105
  40.2 3.8 %all-to-all-done.refs_1_ = bf16[8,32,2176]{2,1,0:T(8,128)(2,1)} async-done(((bf16[8,32,2176]{2,1,0:T(8,128)(2,1)}), bf16[8,32,2176]{2,1,0:T(8,128)(2,1)}, u32[]{:S(2)}, u32[]{:S(2)}) %all-to-all-start) | async-done | bytes 1114144 | tf_op jit(solution)/shard_map/all_to_all | solution.py:40
  44.0 3.8 %shard_map.188 = (bf16[16,32,2048]{2,1,0:T(8,128)(2,1)S(1)}, bf16[512,256]{1,0:T(8,128)(2,1)}, bf16[512,256]{1,0:T(8,128)(2,1)}, bf16[16,512]{1,0:T(8,128)(2,1)S(1)}) custom-call(s32[1]{0:T(128)} %bitcast.refs_0_.refs_1_, bf16[8,32,2176]{2,1,0:T(8,128)(2,1)} %all-to-all-done.refs_1_, bf16[1,32,4096]{2,1,0:T(8,128)(2,1)} %shard_map.184.refs_2_, ...), custom_call_target="tpu_custom_call" | custom-call | flops 536870912 | bytes 4194304 | tf_op jit(solution)/shard_map/pallas_call | solution.py:105
  47.8 34.0 %all_to_all.45.refs_0_.refs_1_ = bf16[16,32,2048]{2,1,0:T(8,128)(2,1)S(1)} all-to-all(bf16[16,32,2048]{2,1,0:T(8,128)(2,1)S(1)} %get-tuple-element.23), channel_id=1, replica_groups=mesh['x'=4,'z'=8,'y'=4,'c'=2] {'x','y'}, dimensions={0} | all-to-all | bytes 4194304 | tf_op jit(solution)/shard_map/all_to_all | solution.py:40
  84.6 3.0 %collective-permute-done.7.refs_3_ = f32[4,128]{1,0:T(4,128)S(1)} collective-permute-done((f32[4,128]{1,0:T(4,128)S(1)}, f32[4,128]{1,0:T(4,128)S(1)}, u32[]{:S(2)}, u32[]{:S(2)}) %collective-permute-start.7) | collective-permute-done | bytes 2080 | tf_op jit(solution)/shard_map/ppermute | solution.py:32
  87.6 2.7 %shard_map.190 = (f32[512,384]{1,0:T(8,128)S(1)}, f32[512,384]{1,0:T(8,128)S(1)}) custom-call(s32[1]{0:T(128)} %bitcast.3.refs_0_, bf16[16,32,2048]{2,1,0:T(8,128)(2,1)S(1)} %all_to_all.45.refs_0_.refs_1_, f32[4,128]{1,0:T(4,128)S(1)} %shard_map.189.refs_2_, f32[4,128]{1,0:T(4,128)S(1)} %collective-permute-done.7.refs_3_, f32[32,128]{1,0:T(8,128)S(1)} %bitcast.18, ...), custom_call_target="tpu_custom_call" | custom-call | flops 1610612736 | bytes 8388608 | tf_op jit(solution)/shard_map/pallas_call | solution.py:105
  90.4 2.8 %shard_map.191.refs_1_ = bf16[512,384]{1,0:T(8,128)(2,1)S(1)} custom-call(s32[1]{0:T(128)} %bitcast.3.refs_0_, bf16[16,32,2048]{2,1,0:T(8,128)(2,1)S(1)} %collective-permute-done.6.refs_1_, f32[4,128]{1,0:T(4,128)S(1)} %shard_map.189.refs_2_, f32[4,128]{1,0:T(4,128)S(1)} %collective-permute-done.7.refs_3_, f32[32,128]{1,0:T(8,128)S(1)} %bitcast.19, ...), custom_call_target="tpu_custom_call" | custom-call | flops 1610612736 | bytes 8388608 | tf_op jit(solution)/shard_map/pallas_call | solution.py:105
  95.0 3.2 %shard_map.192 = bf16[16,32,2048]{2,1,0:T(8,128)(2,1)S(1)} custom-call(s32[1]{0:T(128)} %bitcast.3.refs_0_, bf16[512,384]{1,0:T(8,128)(2,1)S(1)} %shard_map.191.refs_1_, bf16[512,384]{1,0:T(8,128)(2,1)S(1)} %collective-permute-done.8.refs_2_, bf16[1,384,4096]{2,1,0:T(8,128)(2,1)S(1)} %copy-done.5, bf16[384,2048]{1,0:T(8,128)(2,1)} %collective-permute-done.4.refs_4_), custom_call_target="tpu_custom_call" | custom-call | flops 1610612736 | bytes 6291456 | tf_op jit(solution)/shard_map/pallas_call | solution.py:105
  98.2 30.6 %all_to_all.46.refs_5_ = bf16[16,32,2048]{2,1,0:T(8,128)(2,1)S(1)} all-to-all(bf16[16,32,2048]{2,1,0:T(8,128)(2,1)S(1)} %shard_map.192), channel_id=1, replica_groups=mesh['x'=4,'z'=8,'y'=4,'c'=2] {'x','y'}, dimensions={0} | all-to-all | bytes 4194304 | tf_op jit(solution)/shard_map/all_to_all | solution.py:40
  128.9 3.9 %shard_map.193 = (bf16[16,8,1024]{2,1,0:T(8,128)(2,1)}, f32[32,2048]{1,0:T(8,128)}, bf16[48,2048]{1,0:T(8,128)(2,1)}, bf16[48,2048]{1,0:T(8,128)(2,1)}, f32[4,32,2048]{2,1,0:T(8,128)}) custom-call(s32[1]{0:T(128)S(6)} %copy.21.refs_0_, s32[1]{0:T(128)} %bitcast.refs_0_.refs_1_, bf16[16,512]{1,0:T(8,128)(2,1)S(1)} %get-tuple-element.20.refs_2_, ...), custom_call_target="tpu_custom_call" | custom-call | flops 1073741824 | bytes 6291456 | tf_op jit(solution)/shard_map/pallas_call | solution.py:105
  132.8 17.3 %all_to_all.47.refs_0_ = bf16[16,8,1024]{2,1,0:T(8,128)(2,1)S(1)} all-to-all(bf16[16,8,1024]{2,1,0:T(8,128)(2,1)} %get-tuple-element.34), channel_id=1, replica_groups=mesh['x'=4,'z'=8,'y'=4,'c'=2] {'z','c'}, dimensions={0} | all-to-all | bytes 524288 | tf_op jit(solution)/shard_map/all_to_all | solution.py:40
  151.7 3.3 %all-to-all-start.4 = ((bf16[4,16,1024]{2,1,0:T(8,128)(2,1)}), bf16[4,16,1024]{2,1,0:T(8,128)(2,1)S(1)}, u32[]{:S(2)}, u32[]{:S(2)}) async-start(bf16[4,16,1024]{2,1,0:T(8,128)(2,1)} %shard_map.195), calls=%async_computation.4 | async-start | bytes 262144 | tf_op jit(solution)/shard_map/all_to_all | solution.py:40
  155.3 3.4 %collective-permute-start.10 = (bf16[48,2048]{1,0:T(8,128)(2,1)}, bf16[48,2048]{1,0:T(8,128)(2,1)S(1)}, u32[]{:S(2)}, u32[]{:S(2)}) collective-permute-start(bf16[48,2048]{1,0:T(8,128)(2,1)} %get-tuple-element.29), channel_id=1, source_target_pairs={{0,48},{8,56},{16,0},{24,8},{32,16},{40,24},{48,32},{56,40},{1,49}... | collective-permute-start | bytes 589832 | tf_op jit(solution)/shard_map/ppermute | solution.py:541
  162.1 3.3 %all-to-all-start.5 = ((bf16[8,32,128]{2,1,0:T(8,128)(2,1)}), bf16[8,32,128]{2,1,0:T(8,128)(2,1)S(1)}, u32[]{:S(2)}, u32[]{:S(2)}) async-start(bf16[8,32,128]{2,1,0:T(8,128)(2,1)} %shard_map.196), calls=%async_computation.5 | async-start | bytes 131072 | tf_op jit(solution)/shard_map/all_to_all | solution.py:40
  167.9 2.2 shard_map.194
  170.1 2.4 %all-to-all-done.5.refs_0_ = bf16[8,32,128]{2,1,0:T(8,128)(2,1)S(1)} async-done(((bf16[8,32,128]{2,1,0:T(8,128)(2,1)}), bf16[8,32,128]{2,1,0:T(8,128)(2,1)S(1)}, u32[]{:S(2)}, u32[]{:S(2)}) %all-to-all-start.5) | async-done | bytes 65568 | tf_op jit(solution)/shard_map/all_to_all | solution.py:40
  173.6 3.8 %all-to-all-start.6 = ((bf16[16,8,32,128]{3,2,1,0:T(8,128)(2,1)}), bf16[16,8,32,128]{3,2,1,0:T(8,128)(2,1)S(1)}, u32[]{:S(2)}, u32[]{:S(2)}) async-start(bf16[16,8,32,128]{3,2,1,0:T(8,128)(2,1)} %shard_map.197), calls=%async_computation.6 | async-start | bytes 2097152 | tf_op jit(solution)/shard_map/all_to_all | solution.py:40
  177.4 3.7 %collective-permute-start.14 = (bf16[32,2048]{1,0:T(8,128)(2,1)}, bf16[32,2048]{1,0:T(8,128)(2,1)S(1)}, u32[]{:S(2)}, u32[]{:S(2)}) collective-permute-start(bf16[32,2048]{1,0:T(8,128)(2,1)} %get-tuple-element.33), channel_id=1, source_target_pairs={{0,48},{8,56},{16,0},{24,8},{32,16},{40,24},{48,32},{56,40},{1,49}... | collective-permute-start | bytes 393224 | tf_op jit(solution)/shard_map/ppermute | solution.py:550
  182.5 3.6 %collective-permute-done.14.refs_5_ = bf16[32,2048]{1,0:T(8,128)(2,1)S(1)} collective-permute-done((bf16[32,2048]{1,0:T(8,128)(2,1)}, bf16[32,2048]{1,0:T(8,128)(2,1)S(1)}, u32[]{:S(2)}, u32[]{:S(2)}) %collective-permute-start.14) | collective-permute-done | bytes 131104 | tf_op jit(solution)/shard_map/ppermute | solution.py:550
  186.1 3.2 %collective-permute-done.13.refs_4_ = bf16[32,2048]{1,0:T(8,128)(2,1)S(1)} collective-permute-done((bf16[32,2048]{1,0:T(8,128)(2,1)}, bf16[32,2048]{1,0:T(8,128)(2,1)S(1)}, u32[]{:S(2)}, u32[]{:S(2)}) %collective-permute-start.13) | collective-permute-done | bytes 131104 | tf_op jit(solution)/shard_map/ppermute | solution.py:550
  190.6 3.6 %collective-permute-done.11.refs_2_ = bf16[32,2048]{1,0:T(8,128)(2,1)} collective-permute-done((bf16[32,2048]{1,0:T(8,128)(2,1)}, bf16[32,2048]{1,0:T(8,128)(2,1)}, u32[]{:S(2)}, u32[]{:S(2)}) %collective-permute-start.11) | collective-permute-done | bytes 131104 | tf_op jit(solution)/shard_map/ppermute | solution.py:550
  198.7 14.4 %all_to_all.48.refs_0_ = f32[32,4,128]{2,1,0:T(4,128)S(1)} all-to-all(f32[32,4,128]{2,1,0:T(4,128)} %get-tuple-element.35), channel_id=1, replica_groups=mesh['x'=4,'z'=8,'y'=4,'c'=2] {'x','y','c'}, dimensions={0} | all-to-all | bytes 131072 | tf_op jit(solution)/shard_map/all_to_all | solution.py:40
  213.8 3.3 %all-to-all-start.8 = ((f32[8,4,128]{2,1,0:T(4,128)}), f32[8,4,128]{2,1,0:T(4,128)S(1)}, u32[]{:S(2)}, u32[]{:S(2)}) async-start(f32[8,4,128]{2,1,0:T(4,128)} %shard_map.201), calls=%async_computation.8 | async-start | bytes 32768 | tf_op jit(solution)/shard_map/all_to_all | solution.py:40
  218.9 4.8 %all-to-all-done.8.refs_0_ = f32[8,4,128]{2,1,0:T(4,128)S(1)} async-done(((f32[8,4,128]{2,1,0:T(4,128)}), f32[8,4,128]{2,1,0:T(4,128)S(1)}, u32[]{:S(2)}, u32[]{:S(2)}) %all-to-all-start.8) | async-done | bytes 16416 | tf_op jit(solution)/shard_map/all_to_all | solution.py:40
  (82 shorter events, 31.8 us)
Async XLA Ops:
  0.6 43.4 %collective-permute-start.5 = (bf16[304,4096]{1,0:T(8,128)(2,1)}, bf16[304,4096]{1,0:T(8,128)(2,1)S(1)}, u32[]{:S(2)}, u32[]{:S(2)}) collective-permute-start(bf16[304,4096]{1,0:T(8,128)(2,1)} %refs_1_.7), channel_id=1, source_target_pairs={{0,1},{1,0},{2,3},{3,2},{4,5},{5,4},{6,7},{7,6},{8,9},{9,8},{10,11... | collective-permute-start | bytes 7471112 | tf_op jit(solution)/shard_map/ppermute | solution.py:32
  6.8 37.2 %all-to-all-start = ((bf16[8,32,2176]{2,1,0:T(8,128)(2,1)}), bf16[8,32,2176]{2,1,0:T(8,128)(2,1)}, u32[]{:S(2)}, u32[]{:S(2)}) async-start(bf16[8,32,2176]{2,1,0:T(8,128)(2,1)} %shard_map.185), calls=%async_computation | async-start | bytes 2228224 | tf_op jit(solution)/shard_map/all_to_all | solution.py:40
  14.3 9.3 %collective-permute-start = (bf16[2,16,4224]{2,1,0:T(8,128)(2,1)S(1)}, bf16[2,16,4224]{2,1,0:T(8,128)(2,1)S(1)}, u32[]{:S(2)}, u32[]{:S(2)}) collective-permute-start(bf16[2,16,4224]{2,1,0:T(8,128)(2,1)S(1)} %shard_map.186.refs_2_), channel_id=1, source_target_pairs={{0,2},{2,4},{4,6},{6,0},{1,3},{3,5},{5,7},{7,1},{8,10},{10,12},{12... | collective-permute-start | bytes 811016 | tf_op jit(solution)/shard_map/ppermute | solution.py:466
  15.6 14.8 %collective-permute-start.1 = (bf16[2,16,4224]{2,1,0:T(8,128)(2,1)S(1)}, bf16[2,16,4224]{2,1,0:T(8,128)(2,1)S(1)}, u32[]{:S(2)}, u32[]{:S(2)}) collective-permute-start(bf16[2,16,4224]{2,1,0:T(8,128)(2,1)S(1)} %shard_map.186.refs_2_), channel_id=1, source_target_pairs={{0,4},{2,6},{4,0},{6,2},{1,5},{3,7},{5,1},{7,3},{8,12},{10,14},{12... | collective-permute-start | bytes 811016 | tf_op jit(solution)/shard_map/ppermute | solution.py:466
  18.3 12.2 %collective-permute-start.2 = (bf16[2,16,4224]{2,1,0:T(8,128)(2,1)S(1)}, bf16[2,16,4224]{2,1,0:T(8,128)(2,1)}, u32[]{:S(2)}, u32[]{:S(2)}) collective-permute-start(bf16[2,16,4224]{2,1,0:T(8,128)(2,1)S(1)} %shard_map.186.refs_2_), channel_id=1, source_target_pairs={{0,6},{2,0},{4,2},{6,4},{1,7},{3,1},{5,3},{7,5},{8,14},{10,8},{12,... | collective-permute-start | bytes 811016 | tf_op jit(solution)/shard_map/ppermute | solution.py:466
  22.0 18.2 %collective-permute-start.4 = (bf16[384,2048]{1,0:T(8,128)(2,1)}, bf16[384,2048]{1,0:T(8,128)(2,1)}, u32[]{:S(2)}, u32[]{:S(2)}) collective-permute-start(bf16[384,2048]{1,0:T(8,128)(2,1)} %dynamic-slice_bitcast_fusion), channel_id=1, source_target_pairs={{0,1},{1,0},{2,3},{3,2},{4,5},{5,4},{6,7},{7,6},{8,9},{9,8},{10,11... | collective-permute-start | bytes 4718600 | tf_op jit(solution)/shard_map/ppermute | solution.py:32
  32.6 4.8 %collective-permute-start.3 = (bf16[4,2,16,4224]{3,2,1,0:T(8,128)(2,1)}, bf16[4,2,16,4224]{3,2,1,0:T(8,128)(2,1)}, u32[]{:S(2)}, u32[]{:S(2)}) collective-permute-start(bf16[4,2,16,4224]{3,2,1,0:T(8,128)(2,1)} %pad_maximum_fusion), channel_id=1, source_target_pairs={{0,1},{1,0},{2,3},{3,2},{4,5},{5,4},{6,7},{7,6},{8,9},{9,8},{10,11... | collective-permute-start | bytes 3244040 | tf_op jit(solution)/shard_map/ppermute | solution.py:32
  44.0 43.6 %copy-start.11 = (f32[4096]{0:T(1024)S(1)}, f32[4096]{0:T(1024)}, u32[]{:S(2)}) copy-start(f32[4096]{0:T(1024)} %param.23) | copy-start | bytes 49156
  47.8 39.8 %copy-start.1 = (bf16[1,4096,384]{2,1,0:T(8,128)(2,1)S(1)}, bf16[1,4096,384]{2,1,0:T(8,128)(2,1)}, u32[]{:S(2)}) copy-start(bf16[1,4096,384]{2,1,0:T(8,128)(2,1)} %refs_5_.3) | copy-start | bytes 9437188
  47.8 39.8 %copy-start.2 = (bf16[1,4096,384]{2,1,0:T(8,128)(2,1)S(1)}, bf16[1,4096,384]{2,1,0:T(8,128)(2,1)}, u32[]{:S(2)}) copy-start(bf16[1,4096,384]{2,1,0:T(8,128)(2,1)} %refs_6_.4) | copy-start | bytes 9437188
  81.8 8.5 %collective-permute-start.6 = (bf16[16,32,2048]{2,1,0:T(8,128)(2,1)S(1)}, bf16[16,32,2048]{2,1,0:T(8,128)(2,1)S(1)}, u32[]{:S(2)}, u32[]{:S(2)}) collective-permute-start(bf16[16,32,2048]{2,1,0:T(8,128)(2,1)S(1)} %all_to_all.45.refs_0_.refs_1_), channel_id=1, source_target_pairs={{0,1},{1,0},{2,3},{3,2},{4,5},{5,4},{6,7},{7,6},{8,9},{9,8},{10,11... | collective-permute-start | bytes 6291464 | tf_op jit(solution)/shard_map/ppermute | solution.py:32
  84.3 3.3 %collective-permute-start.7 = (f32[4,128]{1,0:T(4,128)S(1)}, f32[4,128]{1,0:T(4,128)S(1)}, u32[]{:S(2)}, u32[]{:S(2)}) collective-permute-start(f32[4,128]{1,0:T(4,128)S(1)} %shard_map.189.refs_2_), channel_id=1, source_target_pairs={{0,1},{1,0},{2,3},{3,2},{4,5},{5,4},{6,7},{7,6},{8,9},{9,8},{10,11... | collective-permute-start | bytes 6152 | tf_op jit(solution)/shard_map/ppermute | solution.py:32
  93.1 1.8 collective-permute-start.8
  98.2 30.7 %copy-start.7 = (bf16[32,2048]{1,0:T(8,128)(2,1)S(1)}, bf16[32,2048]{1,0:T(8,128)(2,1)}, u32[]{:S(2)}) copy-start(bf16[32,2048]{1,0:T(8,128)(2,1)} %refs_6_.5) | copy-start | bytes 393220
  128.9 31.8 %copy-start = (bf16[2,128,4224]{2,1,0:T(8,128)(2,1)S(1)}, bf16[2,128,4224]{2,1,0:T(8,128)(2,1)}, u32[]{:S(2)}) copy-start(bf16[2,128,4224]{2,1,0:T(8,128)(2,1)} %shard_map.187.refs_3_.refs_2_) | copy-start | bytes 6488068
  151.7 8.9 %all-to-all-start.4 = ((bf16[4,16,1024]{2,1,0:T(8,128)(2,1)}), bf16[4,16,1024]{2,1,0:T(8,128)(2,1)S(1)}, u32[]{:S(2)}, u32[]{:S(2)}) async-start(bf16[4,16,1024]{2,1,0:T(8,128)(2,1)} %shard_map.195), calls=%async_computation.4 | async-start | bytes 262144 | tf_op jit(solution)/shard_map/all_to_all | solution.py:40
  155.0 12.1 %collective-permute-start.9 = (bf16[48,2048]{1,0:T(8,128)(2,1)}, bf16[48,2048]{1,0:T(8,128)(2,1)S(1)}, u32[]{:S(2)}, u32[]{:S(2)}) collective-permute-start(bf16[48,2048]{1,0:T(8,128)(2,1)} %get-tuple-element.28), channel_id=1, source_target_pairs={{0,16},{8,24},{16,32},{24,40},{32,48},{40,56},{48,0},{56,8},{1,17}... | collective-permute-start | bytes 589832 | tf_op jit(solution)/shard_map/ppermute | solution.py:540
  155.3 12.0 %collective-permute-start.10 = (bf16[48,2048]{1,0:T(8,128)(2,1)}, bf16[48,2048]{1,0:T(8,128)(2,1)S(1)}, u32[]{:S(2)}, u32[]{:S(2)}) collective-permute-start(bf16[48,2048]{1,0:T(8,128)(2,1)} %get-tuple-element.29), channel_id=1, source_target_pairs={{0,48},{8,56},{16,0},{24,8},{32,16},{40,24},{48,32},{56,40},{1,49}... | collective-permute-start | bytes 589832 | tf_op jit(solution)/shard_map/ppermute | solution.py:541
  162.1 10.4 %all-to-all-start.5 = ((bf16[8,32,128]{2,1,0:T(8,128)(2,1)}), bf16[8,32,128]{2,1,0:T(8,128)(2,1)S(1)}, u32[]{:S(2)}, u32[]{:S(2)}) async-start(bf16[8,32,128]{2,1,0:T(8,128)(2,1)} %shard_map.196), calls=%async_computation.5 | async-start | bytes 131072 | tf_op jit(solution)/shard_map/all_to_all | solution.py:40
  172.5 21.7 %copy-start.4 = (bf16[304,4096]{1,0:T(8,128)(2,1)S(1)}, bf16[304,4096]{1,0:T(8,128)(2,1)}, u32[]{:S(2)}) copy-start(bf16[304,4096]{1,0:T(8,128)(2,1)} %copy-done.3) | copy-start | bytes 7471108
  173.6 20.6 %all-to-all-start.6 = ((bf16[16,8,32,128]{3,2,1,0:T(8,128)(2,1)}), bf16[16,8,32,128]{3,2,1,0:T(8,128)(2,1)S(1)}, u32[]{:S(2)}, u32[]{:S(2)}) async-start(bf16[16,8,32,128]{3,2,1,0:T(8,128)(2,1)} %shard_map.197), calls=%async_computation.6 | async-start | bytes 2097152 | tf_op jit(solution)/shard_map/all_to_all | solution.py:40
  177.4 8.7 %collective-permute-start.14 = (bf16[32,2048]{1,0:T(8,128)(2,1)}, bf16[32,2048]{1,0:T(8,128)(2,1)S(1)}, u32[]{:S(2)}, u32[]{:S(2)}) collective-permute-start(bf16[32,2048]{1,0:T(8,128)(2,1)} %get-tuple-element.33), channel_id=1, source_target_pairs={{0,48},{8,56},{16,0},{24,8},{32,16},{40,24},{48,32},{56,40},{1,49}... | collective-permute-start | bytes 393224 | tf_op jit(solution)/shard_map/ppermute | solution.py:550
  181.1 8.2 %collective-permute-start.13 = (bf16[32,2048]{1,0:T(8,128)(2,1)}, bf16[32,2048]{1,0:T(8,128)(2,1)S(1)}, u32[]{:S(2)}, u32[]{:S(2)}) collective-permute-start(bf16[32,2048]{1,0:T(8,128)(2,1)} %get-tuple-element.32), channel_id=1, source_target_pairs={{0,56},{8,0},{16,8},{24,16},{32,24},{40,32},{48,40},{56,48},{1,57}... | collective-permute-start | bytes 393224 | tf_op jit(solution)/shard_map/ppermute | solution.py:550
  181.1 8.3 %collective-permute-start.12 = (bf16[32,2048]{1,0:T(8,128)(2,1)}, bf16[32,2048]{1,0:T(8,128)(2,1)S(1)}, u32[]{:S(2)}, u32[]{:S(2)}) collective-permute-start(bf16[32,2048]{1,0:T(8,128)(2,1)} %get-tuple-element.31), channel_id=1, source_target_pairs={{0,16},{8,24},{16,32},{24,40},{32,48},{40,56},{48,0},{56,8},{1,17}... | collective-permute-start | bytes 393224 | tf_op jit(solution)/shard_map/ppermute | solution.py:550
  181.1 13.1 %collective-permute-start.11 = (bf16[32,2048]{1,0:T(8,128)(2,1)}, bf16[32,2048]{1,0:T(8,128)(2,1)}, u32[]{:S(2)}, u32[]{:S(2)}) collective-permute-start(bf16[32,2048]{1,0:T(8,128)(2,1)} %get-tuple-element.30.refs_1_), channel_id=1, source_target_pairs={{0,8},{8,16},{16,24},{24,32},{32,40},{40,48},{48,56},{56,0},{1,9},... | collective-permute-start | bytes 393224 | tf_op jit(solution)/shard_map/ppermute | solution.py:550
  195.0 22.2 %copy-start.8 = (bf16[32,2048]{1,0:T(8,128)(2,1)S(1)}, bf16[32,2048]{1,0:T(8,128)(2,1)}, u32[]{:S(2)}) copy-start(bf16[32,2048]{1,0:T(8,128)(2,1)} %refs_6_.5) | copy-start | bytes 393220
  195.0 22.2 %copy-start.15 = (bf16[32,2048]{1,0:T(8,128)(2,1)S(1)}, bf16[32,2048]{1,0:T(8,128)(2,1)}, u32[]{:S(2)}) copy-start(bf16[32,2048]{1,0:T(8,128)(2,1)} %copy-done.14) | copy-start | bytes 393220
  195.0 22.2 %copy-start.17 = (bf16[32,2048]{1,0:T(8,128)(2,1)S(1)}, bf16[32,2048]{1,0:T(8,128)(2,1)}, u32[]{:S(2)}) copy-start(bf16[32,2048]{1,0:T(8,128)(2,1)} %copy-done.16) | copy-start | bytes 393220
  195.0 22.2 %copy-start.19 = (bf16[32,2048]{1,0:T(8,128)(2,1)S(1)}, bf16[32,2048]{1,0:T(8,128)(2,1)}, u32[]{:S(2)}) copy-start(bf16[32,2048]{1,0:T(8,128)(2,1)} %copy-done.18) | copy-start | bytes 393220
  195.1 22.2 %copy-start.20 = (f32[32,2048]{1,0:T(8,128)S(1)}, f32[32,2048]{1,0:T(8,128)}, u32[]{:S(2)}) copy-start(f32[32,2048]{1,0:T(8,128)} %get-tuple-element.26) | copy-start | bytes 786436
  195.1 2.6 %collective-permute-start.15 = (f32[304,128]{1,0:T(8,128)S(1)}, f32[304,128]{1,0:T(8,128)S(1)}, u32[]{:S(2)}, u32[]{:S(2)}) collective-permute-start(f32[304,128]{1,0:T(8,128)S(1)} %shard_map.199), channel_id=1, source_target_pairs={{0,1},{1,0},{2,3},{3,2},{4,5},{5,4},{6,7},{7,6},{8,9},{9,8},{10,11... | collective-permute-start | bytes 466952 | tf_op jit(solution)/shard_map/ppermute | solution.py:32
  213.8 9.9 %all-to-all-start.8 = ((f32[8,4,128]{2,1,0:T(4,128)}), f32[8,4,128]{2,1,0:T(4,128)S(1)}, u32[]{:S(2)}, u32[]{:S(2)}) async-start(f32[8,4,128]{2,1,0:T(4,128)} %shard_map.201), calls=%async_computation.8 | async-start | bytes 32768 | tf_op jit(solution)/shard_map/all_to_all | solution.py:40
  (12 other events, 54.3 us)

commit v6 on v5

--- a/solution.py
+++ b/solution.py
@@ -265,14 +265,18 @@
     activation[...] = (silu(gate[...] + gate_part) * (up[...] + up_part)).astype(jnp.bfloat16)
 
 
-def down_kernel(core, own, other, down, other_down, finished):
-    rows = jnp.concatenate([own[...], other[...]], 1)
-    columns = pl.ds(pl.multiple_of(core[0] * HALF, HALF), HALF)
-    weights = jnp.concatenate([down[0, :, columns], other_down[...]], 0)
+def own_down_kernel(core, own, down, part):
     for piece in range(HALF // BLOCK):
         here = slice(piece * BLOCK, (piece + 1) * BLOCK)
-        part = dot32(rows, weights[:, here]).astype(jnp.bfloat16)
-        finished[:, :, here] = part.reshape(NPLANE, NZ * CAP, BLOCK)
+        columns = pl.ds(pl.multiple_of(core[0] * HALF + piece * BLOCK, BLOCK), BLOCK)
+        part[:, here] = dot32(own[...], down[0, :, columns])
+
+
+def other_down_kernel(part, other, other_down, finished):
+    for piece in range(HALF // BLOCK):
+        here = slice(piece * BLOCK, (piece + 1) * BLOCK)
+        whole_sum = part[:, here] + dot32(other[...], other_down[:, here])
+        finished[:, :, here] = whole_sum.astype(jnp.bfloat16).reshape(NPLANE, NZ * CAP, BLOCK)
 
 
 def combine_kernel(
@@ -511,12 +515,20 @@
         moved=8 << 20,
         scratch=[pltpu.VMEM((slots, HALF), bf16)],
     )
+    part = call(
+        own_down_kernel,
+        [core_at],
+        [activation, w_down],
+        like((slots, HALF), f32),
+        flops=2 * slots * HALF * units,
+        moved=6 << 20,
+    )
     finished = call(
-        down_kernel,
-        [core_at],
-        [activation, swap(activation), w_down, other_down],
+        other_down_kernel,
+        [],
+        [part, swap(activation), other_down],
         pltpu.VMEM((NPLANE, NZ * CAP, HALF), bf16),
-        flops=4 * slots * HALF * units,
+        flops=2 * slots * HALF * units,
         moved=6 << 20,
     )
     returned = exchange(finished, PLANE)

time: 227 us -> 225 us (level)
    ppermute x3, waiting for transfers between devices: 7.3 us -> 10.9 us  [on_device(): lax.ppermute(wide_w, 'y', around(NY, step))]
    ppermute x4, waiting for transfers between devices: 10.4 us -> 7.73 us  [on_device(): lax.ppermute(part, 'z', around(NZ, step))]
    pallas_call x19 -> x20, Pallas kernels: 36.5 us -> 37.2 us  [call(): pl.pallas_call(body, out_shape=list(outs), in_specs=[SMEM] * count + [who...]
  transfers between devices with their start and end apart: 21 -> 21, of which waited for: 14 -> 14; matrix products, arithmetic and copies ran while one was open for 3% -> 3% of each run, Pallas kernels for 7% -> 8%
where the time goes in v6:
time: 225 us; the launch traced here: 224 us
  blocking collectives  94.2 us (42%)
  starting transfers between devices  45.3 us (20%)
  Pallas kernels  37.2 us (17%)
  waiting for transfers between devices  36.4 us (16%)
  local copies, waits for them, and re-layouts  5.08 us (2%)
  other arithmetic  3.75 us (2%)
    all_to_all x4, blocking collectives, exchange(): return lax.all_to_all(value, axes, 0, 0, tiled=True)  94.2 us
    pallas_call x20, Pallas kernels, call(): pl.pallas_call(body, out_shape=list(outs), in_specs=[SMEM] * count + [who...  37.2 us
    all_to_all x5, starting transfers between devices, exchange(): return lax.all_to_all(value, axes, 0, 0, tiled=True)  21.5 us
    all_to_all x5, waiting for transfers between devices, exchange(): return lax.all_to_all(value, axes, 0, 0, tiled=True)  12.6 us
    ppermute x3, waiting for transfers between devices, on_device(): lax.ppermute(wide_w, 'y', around(NY, step))  10.9 us
    ppermute x7, starting transfers between devices, swap(): return lax.ppermute(value, TP, SWAP)  10.9 us
    ppermute x4, waiting for transfers between devices, on_device(): lax.ppermute(part, 'z', around(NZ, step))  7.73 us
    ppermute x4, starting transfers between devices, on_device(): lax.ppermute(part, 'z', around(NZ, step))  5.44 us
  transfers between devices with their start and end apart: 21, of which 14 were waited for; matrix products, arithmetic and copies ran while one was open for 3% of the time, Pallas kernels for 8%

profile of v6, /device:TPU:1, one launch (start us, length us, event | category | flops | bytes accessed | tf_op | source)
XLA Modules:
  0.0 224.1 jit_solution(8105208135151338164)
XLA Ops:
  0.6 3.3 %collective-permute-start.5 = (bf16[304,4096]{1,0:T(8,128)(2,1)}, bf16[304,4096]{1,0:T(8,128)(2,1)S(1)}, u32[]{:S(2)}, u32[]{:S(2)}) collective-permute-start(bf16[304,4096]{1,0:T(8,128)(2,1)} %refs_1_.7), channel_id=1, source_target_pairs={{0,1},{1,0},{2,3},{3,2},{4,5},{5,4},{6,7},{7,6},{8,9},{9,8},{10,11... | collective-permute-start | bytes 7471112 | tf_op jit(solution)/shard_map/ppermute | solution.py:32
  4.6 2.2 shard_map.185
  6.8 6.5 %all-to-all-start = ((bf16[8,32,2176]{2,1,0:T(8,128)(2,1)}), bf16[8,32,2176]{2,1,0:T(8,128)(2,1)}, u32[]{:S(2)}, u32[]{:S(2)}) async-start(bf16[8,32,2176]{2,1,0:T(8,128)(2,1)} %shard_map.185), calls=%async_computation | async-start | bytes 2228224 | tf_op jit(solution)/shard_map/all_to_all | solution.py:40
  14.3 2.8 %collective-permute-start.2 = (bf16[2,16,4224]{2,1,0:T(8,128)(2,1)S(1)}, bf16[2,16,4224]{2,1,0:T(8,128)(2,1)S(1)}, u32[]{:S(2)}, u32[]{:S(2)}) collective-permute-start(bf16[2,16,4224]{2,1,0:T(8,128)(2,1)S(1)} %shard_map.186.refs_2_), channel_id=1, source_target_pairs={{0,6},{2,0},{4,2},{6,4},{1,7},{3,1},{5,3},{7,5},{8,14},{10,8},{12,... | collective-permute-start | bytes 811016 | tf_op jit(solution)/shard_map/ppermute | solution.py:470
  18.1 2.7 %dynamic-slice_bitcast_fusion = bf16[384,2048]{1,0:T(8,128)(2,1)} fusion(bf16[1,384,4096]{2,1,0:T(8,128)(2,1)} %refs_2_.3, s32[]{:T(128)S(6)} %select_n.3), kind=kLoop, calls=%fused_computation | loop fusion | bytes 3145732 | tf_op jit(solution)/shard_map/dynamic_slice | solution.py:478
  22.0 6.3 %collective-permute-done.2.refs_5_ = bf16[2,16,4224]{2,1,0:T(8,128)(2,1)S(1)} collective-permute-done((bf16[2,16,4224]{2,1,0:T(8,128)(2,1)S(1)}, bf16[2,16,4224]{2,1,0:T(8,128)(2,1)S(1)}, u32[]{:S(2)}, u32[]{:S(2)}) %collective-permute-start.2) | collective-permute-done | bytes 270368 | tf_op jit(solution)/shard_map/ppermute | solution.py:470
  28.3 4.6 %collective-permute-done.refs_3_ = bf16[2,16,4224]{2,1,0:T(8,128)(2,1)} collective-permute-done((bf16[2,16,4224]{2,1,0:T(8,128)(2,1)S(1)}, bf16[2,16,4224]{2,1,0:T(8,128)(2,1)}, u32[]{:S(2)}, u32[]{:S(2)}) %collective-permute-start) | collective-permute-done | bytes 270368 | tf_op jit(solution)/shard_map/ppermute | solution.py:470
  32.9 2.1 pad_maximum_fusion
  37.1 2.1 shard_map.184.refs_2_
  39.2 2.9 %shard_map.187.refs_3_.refs_2_ = bf16[2,128,4224]{2,1,0:T(8,128)(2,1)} custom-call(s32[1]{0:T(128)} %bitcast.3.refs_0_, s32[1]{0:T(128)} %bitcast.4.refs_1_, bf16[2,16,4224]{2,1,0:T(8,128)(2,1)S(1)} %shard_map.186.refs_2_, bf16[2,16,4224]{2,1,0:T(8,128)(2,1)} %collective-permute-done.refs_3_, bf16[2,16,4224]{2,1,0:T(8,128)(2,1)S(1)} %collective-permute-done.1.refs_4_, ...), custom_call_target="tpu_custom_call" | custom-call | bytes 4194304 | tf_op jit(solution)/shard_map/pallas_call | solution.py:105
  44.0 3.8 %shard_map.188 = (bf16[16,32,2048]{2,1,0:T(8,128)(2,1)S(1)}, bf16[512,256]{1,0:T(8,128)(2,1)}, bf16[512,256]{1,0:T(8,128)(2,1)}, bf16[16,512]{1,0:T(8,128)(2,1)S(1)}) custom-call(s32[1]{0:T(128)} %bitcast.refs_0_.refs_1_, bf16[8,32,2176]{2,1,0:T(8,128)(2,1)} %all-to-all-done.refs_1_, bf16[1,32,4096]{2,1,0:T(8,128)(2,1)} %shard_map.184.refs_2_, ...), custom_call_target="tpu_custom_call" | custom-call | flops 536870912 | bytes 4194304 | tf_op jit(solution)/shard_map/pallas_call | solution.py:105
  47.8 34.0 %all_to_all.45.refs_0_.refs_1_ = bf16[16,32,2048]{2,1,0:T(8,128)(2,1)S(1)} all-to-all(bf16[16,32,2048]{2,1,0:T(8,128)(2,1)S(1)} %get-tuple-element.23), channel_id=1, replica_groups=mesh['x'=4,'z'=8,'y'=4,'c'=2] {'x','y'}, dimensions={0} | all-to-all | bytes 4194304 | tf_op jit(solution)/shard_map/all_to_all | solution.py:40
  81.8 2.0 collective-permute-start.6
  84.6 3.0 %collective-permute-done.7.refs_3_ = f32[4,128]{1,0:T(4,128)S(1)} collective-permute-done((f32[4,128]{1,0:T(4,128)S(1)}, f32[4,128]{1,0:T(4,128)S(1)}, u32[]{:S(2)}, u32[]{:S(2)}) %collective-permute-start.7) | collective-permute-done | bytes 2080 | tf_op jit(solution)/shard_map/ppermute | solution.py:32
  87.6 2.7 %shard_map.190 = (f32[512,384]{1,0:T(8,128)S(1)}, f32[512,384]{1,0:T(8,128)S(1)}) custom-call(s32[1]{0:T(128)} %bitcast.3.refs_0_, bf16[16,32,2048]{2,1,0:T(8,128)(2,1)S(1)} %all_to_all.45.refs_0_.refs_1_, f32[4,128]{1,0:T(4,128)S(1)} %shard_map.189.refs_2_, f32[4,128]{1,0:T(4,128)S(1)} %collective-permute-done.7.refs_3_, f32[32,128]{1,0:T(8,128)S(1)} %bitcast.18, ...), custom_call_target="tpu_custom_call" | custom-call | flops 1610612736 | bytes 8388608 | tf_op jit(solution)/shard_map/pallas_call | solution.py:105
  90.4 2.8 %shard_map.191.refs_1_ = bf16[512,384]{1,0:T(8,128)(2,1)S(1)} custom-call(s32[1]{0:T(128)} %bitcast.3.refs_0_, bf16[16,32,2048]{2,1,0:T(8,128)(2,1)S(1)} %collective-permute-done.6.refs_1_, f32[4,128]{1,0:T(4,128)S(1)} %shard_map.189.refs_2_, f32[4,128]{1,0:T(4,128)S(1)} %collective-permute-done.7.refs_3_, f32[32,128]{1,0:T(8,128)S(1)} %bitcast.19, ...), custom_call_target="tpu_custom_call" | custom-call | flops 1610612736 | bytes 8388608 | tf_op jit(solution)/shard_map/pallas_call | solution.py:105
  95.0 2.7 %shard_map.193 = bf16[16,32,2048]{2,1,0:T(8,128)(2,1)S(1)} custom-call(f32[512,2048]{1,0:T(8,128)S(1)} %shard_map.192.refs_0_, bf16[512,384]{1,0:T(8,128)(2,1)S(1)} %collective-permute-done.8.refs_1_, bf16[384,2048]{1,0:T(8,128)(2,1)} %collective-permute-done.4.refs_4_.refs_2_), custom_call_target="tpu_custom_call" | custom-call | flops 805306368 | bytes 6291456 | tf_op jit(solution)/shard_map/pallas_call | solution.py:105
  97.7 30.7 %all_to_all.46.refs_5_ = bf16[16,32,2048]{2,1,0:T(8,128)(2,1)S(1)} all-to-all(bf16[16,32,2048]{2,1,0:T(8,128)(2,1)S(1)} %shard_map.193), channel_id=1, replica_groups=mesh['x'=4,'z'=8,'y'=4,'c'=2] {'x','y'}, dimensions={0} | all-to-all | bytes 4194304 | tf_op jit(solution)/shard_map/all_to_all | solution.py:40
  128.3 3.9 %shard_map.194 = (bf16[16,8,1024]{2,1,0:T(8,128)(2,1)}, f32[32,2048]{1,0:T(8,128)}, bf16[48,2048]{1,0:T(8,128)(2,1)}, bf16[48,2048]{1,0:T(8,128)(2,1)}, f32[4,32,2048]{2,1,0:T(8,128)}) custom-call(s32[1]{0:T(128)S(6)} %copy.21.refs_0_, s32[1]{0:T(128)} %bitcast.refs_0_.refs_1_, bf16[16,512]{1,0:T(8,128)(2,1)S(1)} %get-tuple-element.20.refs_2_, ...), custom_call_target="tpu_custom_call" | custom-call | flops 1073741824 | bytes 6291456 | tf_op jit(solution)/shard_map/pallas_call | solution.py:105
  132.3 17.2 %all_to_all.47.refs_0_ = bf16[16,8,1024]{2,1,0:T(8,128)(2,1)S(1)} all-to-all(bf16[16,8,1024]{2,1,0:T(8,128)(2,1)} %get-tuple-element.34), channel_id=1, replica_groups=mesh['x'=4,'z'=8,'y'=4,'c'=2] {'z','c'}, dimensions={0} | all-to-all | bytes 524288 | tf_op jit(solution)/shard_map/all_to_all | solution.py:40
  151.1 3.3 %all-to-all-start.4 = ((bf16[4,16,1024]{2,1,0:T(8,128)(2,1)}), bf16[4,16,1024]{2,1,0:T(8,128)(2,1)S(1)}, u32[]{:S(2)}, u32[]{:S(2)}) async-start(bf16[4,16,1024]{2,1,0:T(8,128)(2,1)} %shard_map.196), calls=%async_computation.4 | async-start | bytes 262144 | tf_op jit(solution)/shard_map/all_to_all | solution.py:40
  154.7 3.4 %collective-permute-start.10 = (bf16[48,2048]{1,0:T(8,128)(2,1)}, bf16[48,2048]{1,0:T(8,128)(2,1)S(1)}, u32[]{:S(2)}, u32[]{:S(2)}) collective-permute-start(bf16[48,2048]{1,0:T(8,128)(2,1)} %get-tuple-element.29), channel_id=1, source_target_pairs={{0,48},{8,56},{16,0},{24,8},{32,16},{40,24},{48,32},{56,40},{1,49}... | collective-permute-start | bytes 589832 | tf_op jit(solution)/shard_map/ppermute | solution.py:553
  161.5 3.3 %all-to-all-start.5 = ((bf16[8,32,128]{2,1,0:T(8,128)(2,1)}), bf16[8,32,128]{2,1,0:T(8,128)(2,1)S(1)}, u32[]{:S(2)}, u32[]{:S(2)}) async-start(bf16[8,32,128]{2,1,0:T(8,128)(2,1)} %shard_map.197), calls=%async_computation.5 | async-start | bytes 131072 | tf_op jit(solution)/shard_map/all_to_all | solution.py:40
  167.3 2.1 shard_map.195
  169.5 2.4 %all-to-all-done.5.refs_0_ = bf16[8,32,128]{2,1,0:T(8,128)(2,1)S(1)} async-done(((bf16[8,32,128]{2,1,0:T(8,128)(2,1)}), bf16[8,32,128]{2,1,0:T(8,128)(2,1)S(1)}, u32[]{:S(2)}, u32[]{:S(2)}) %all-to-all-start.5) | async-done | bytes 65568 | tf_op jit(solution)/shard_map/all_to_all | solution.py:40
  173.0 3.8 %all-to-all-start.6 = ((bf16[16,8,32,128]{3,2,1,0:T(8,128)(2,1)}), bf16[16,8,32,128]{3,2,1,0:T(8,128)(2,1)S(1)}, u32[]{:S(2)}, u32[]{:S(2)}) async-start(bf16[16,8,32,128]{3,2,1,0:T(8,128)(2,1)} %shard_map.198), calls=%async_computation.6 | async-start | bytes 2097152 | tf_op jit(solution)/shard_map/all_to_all | solution.py:40
  182.3 4.8 %collective-permute-done.12.refs_3_ = bf16[32,2048]{1,0:T(8,128)(2,1)S(1)} collective-permute-done((bf16[32,2048]{1,0:T(8,128)(2,1)}, bf16[32,2048]{1,0:T(8,128)(2,1)S(1)}, u32[]{:S(2)}, u32[]{:S(2)}) %collective-permute-start.12) | collective-permute-done | bytes 131104 | tf_op jit(solution)/shard_map/ppermute | solution.py:562
  187.0 3.0 %collective-permute-done.14.refs_5_ = bf16[32,2048]{1,0:T(8,128)(2,1)S(1)} collective-permute-done((bf16[32,2048]{1,0:T(8,128)(2,1)}, bf16[32,2048]{1,0:T(8,128)(2,1)S(1)}, u32[]{:S(2)}, u32[]{:S(2)}) %collective-permute-start.14) | collective-permute-done | bytes 131104 | tf_op jit(solution)/shard_map/ppermute | solution.py:562
  192.9 3.2 %collective-permute-start.15 = (f32[304,128]{1,0:T(8,128)S(1)}, f32[304,128]{1,0:T(8,128)S(1)}, u32[]{:S(2)}, u32[]{:S(2)}) collective-permute-start(f32[304,128]{1,0:T(8,128)S(1)} %shard_map.200), channel_id=1, source_target_pairs={{0,1},{1,0},{2,3},{3,2},{4,5},{5,4},{6,7},{7,6},{8,9},{9,8},{10,11... | collective-permute-start | bytes 466952 | tf_op jit(solution)/shard_map/ppermute | solution.py:32
  198.2 12.3 %all_to_all.48.refs_0_ = f32[32,4,128]{2,1,0:T(4,128)S(1)} all-to-all(f32[32,4,128]{2,1,0:T(4,128)} %get-tuple-element.35), channel_id=1, replica_groups=mesh['x'=4,'z'=8,'y'=4,'c'=2] {'x','y','c'}, dimensions={0} | all-to-all | bytes 131072 | tf_op jit(solution)/shard_map/all_to_all | solution.py:40
  211.1 4.6 %all-to-all-start.8 = ((f32[8,4,128]{2,1,0:T(4,128)}), f32[8,4,128]{2,1,0:T(4,128)S(1)}, u32[]{:S(2)}, u32[]{:S(2)}) async-start(f32[8,4,128]{2,1,0:T(4,128)} %shard_map.202), calls=%async_computation.8 | async-start | bytes 32768 | tf_op jit(solution)/shard_map/all_to_all | solution.py:40
  217.4 4.9 %all-to-all-done.8.refs_0_ = f32[8,4,128]{2,1,0:T(4,128)S(1)} async-done(((f32[8,4,128]{2,1,0:T(4,128)}), f32[8,4,128]{2,1,0:T(4,128)S(1)}, u32[]{:S(2)}, u32[]{:S(2)}) %all-to-all-start.8) | async-done | bytes 16416 | tf_op jit(solution)/shard_map/all_to_all | solution.py:40
  (83 shorter events, 32.5 us)
Async XLA Ops:
  0.6 43.4 %collective-permute-start.5 = (bf16[304,4096]{1,0:T(8,128)(2,1)}, bf16[304,4096]{1,0:T(8,128)(2,1)S(1)}, u32[]{:S(2)}, u32[]{:S(2)}) collective-permute-start(bf16[304,4096]{1,0:T(8,128)(2,1)} %refs_1_.7), channel_id=1, source_target_pairs={{0,1},{1,0},{2,3},{3,2},{4,5},{5,4},{6,7},{7,6},{8,9},{9,8},{10,11... | collective-permute-start | bytes 7471112 | tf_op jit(solution)/shard_map/ppermute | solution.py:32
  6.8 37.2 %all-to-all-start = ((bf16[8,32,2176]{2,1,0:T(8,128)(2,1)}), bf16[8,32,2176]{2,1,0:T(8,128)(2,1)}, u32[]{:S(2)}, u32[]{:S(2)}) async-start(bf16[8,32,2176]{2,1,0:T(8,128)(2,1)} %shard_map.185), calls=%async_computation | async-start | bytes 2228224 | tf_op jit(solution)/shard_map/all_to_all | solution.py:40
  14.3 14.0 %collective-permute-start.2 = (bf16[2,16,4224]{2,1,0:T(8,128)(2,1)S(1)}, bf16[2,16,4224]{2,1,0:T(8,128)(2,1)S(1)}, u32[]{:S(2)}, u32[]{:S(2)}) collective-permute-start(bf16[2,16,4224]{2,1,0:T(8,128)(2,1)S(1)} %shard_map.186.refs_2_), channel_id=1, source_target_pairs={{0,6},{2,0},{4,2},{6,4},{1,7},{3,1},{5,3},{7,5},{8,14},{10,8},{12,... | collective-permute-start | bytes 811016 | tf_op jit(solution)/shard_map/ppermute | solution.py:470
  17.1 11.2 %collective-permute-start.1 = (bf16[2,16,4224]{2,1,0:T(8,128)(2,1)S(1)}, bf16[2,16,4224]{2,1,0:T(8,128)(2,1)S(1)}, u32[]{:S(2)}, u32[]{:S(2)}) collective-permute-start(bf16[2,16,4224]{2,1,0:T(8,128)(2,1)S(1)} %shard_map.186.refs_2_), channel_id=1, source_target_pairs={{0,4},{2,6},{4,0},{6,2},{1,5},{3,7},{5,1},{7,3},{8,12},{10,14},{12... | collective-permute-start | bytes 811016 | tf_op jit(solution)/shard_map/ppermute | solution.py:470
  17.4 15.5 %collective-permute-start = (bf16[2,16,4224]{2,1,0:T(8,128)(2,1)S(1)}, bf16[2,16,4224]{2,1,0:T(8,128)(2,1)}, u32[]{:S(2)}, u32[]{:S(2)}) collective-permute-start(bf16[2,16,4224]{2,1,0:T(8,128)(2,1)S(1)} %shard_map.186.refs_2_), channel_id=1, source_target_pairs={{0,2},{2,4},{4,6},{6,0},{1,3},{3,5},{5,7},{7,1},{8,10},{10,12},{12... | collective-permute-start | bytes 811016 | tf_op jit(solution)/shard_map/ppermute | solution.py:470
  20.8 21.3 %collective-permute-start.4 = (bf16[384,2048]{1,0:T(8,128)(2,1)}, bf16[384,2048]{1,0:T(8,128)(2,1)}, u32[]{:S(2)}, u32[]{:S(2)}) collective-permute-start(bf16[384,2048]{1,0:T(8,128)(2,1)} %dynamic-slice_bitcast_fusion), channel_id=1, source_target_pairs={{0,1},{1,0},{2,3},{3,2},{4,5},{5,4},{6,7},{7,6},{8,9},{9,8},{10,11... | collective-permute-start | bytes 4718600 | tf_op jit(solution)/shard_map/ppermute | solution.py:32
  35.0 4.3 %collective-permute-start.3 = (bf16[4,2,16,4224]{3,2,1,0:T(8,128)(2,1)}, bf16[4,2,16,4224]{3,2,1,0:T(8,128)(2,1)}, u32[]{:S(2)}, u32[]{:S(2)}) collective-permute-start(bf16[4,2,16,4224]{3,2,1,0:T(8,128)(2,1)} %pad_maximum_fusion), channel_id=1, source_target_pairs={{0,1},{1,0},{2,3},{3,2},{4,5},{5,4},{6,7},{7,6},{8,9},{9,8},{10,11... | collective-permute-start | bytes 3244040 | tf_op jit(solution)/shard_map/ppermute | solution.py:32
  44.0 43.6 %copy-start.11 = (f32[4096]{0:T(1024)S(1)}, f32[4096]{0:T(1024)}, u32[]{:S(2)}) copy-start(f32[4096]{0:T(1024)} %param.23) | copy-start | bytes 49156
  47.8 39.8 %copy-start.1 = (bf16[1,4096,384]{2,1,0:T(8,128)(2,1)S(1)}, bf16[1,4096,384]{2,1,0:T(8,128)(2,1)}, u32[]{:S(2)}) copy-start(bf16[1,4096,384]{2,1,0:T(8,128)(2,1)} %refs_5_.3) | copy-start | bytes 9437188
  47.8 39.8 %copy-start.2 = (bf16[1,4096,384]{2,1,0:T(8,128)(2,1)S(1)}, bf16[1,4096,384]{2,1,0:T(8,128)(2,1)}, u32[]{:S(2)}) copy-start(bf16[1,4096,384]{2,1,0:T(8,128)(2,1)} %refs_6_.4) | copy-start | bytes 9437188
  81.8 8.5 %collective-permute-start.6 = (bf16[16,32,2048]{2,1,0:T(8,128)(2,1)S(1)}, bf16[16,32,2048]{2,1,0:T(8,128)(2,1)S(1)}, u32[]{:S(2)}, u32[]{:S(2)}) collective-permute-start(bf16[16,32,2048]{2,1,0:T(8,128)(2,1)S(1)} %all_to_all.45.refs_0_.refs_1_), channel_id=1, source_target_pairs={{0,1},{1,0},{2,3},{3,2},{4,5},{5,4},{6,7},{7,6},{8,9},{9,8},{10,11... | collective-permute-start | bytes 6291464 | tf_op jit(solution)/shard_map/ppermute | solution.py:32
  84.3 3.3 %collective-permute-start.7 = (f32[4,128]{1,0:T(4,128)S(1)}, f32[4,128]{1,0:T(4,128)S(1)}, u32[]{:S(2)}, u32[]{:S(2)}) collective-permute-start(f32[4,128]{1,0:T(4,128)S(1)} %shard_map.189.refs_2_), channel_id=1, source_target_pairs={{0,1},{1,0},{2,3},{3,2},{4,5},{5,4},{6,7},{7,6},{8,9},{9,8},{10,11... | collective-permute-start | bytes 6152 | tf_op jit(solution)/shard_map/ppermute | solution.py:32
  93.1 1.8 collective-permute-start.8
  97.6 30.7 %copy-start.7 = (bf16[32,2048]{1,0:T(8,128)(2,1)S(1)}, bf16[32,2048]{1,0:T(8,128)(2,1)}, u32[]{:S(2)}) copy-start(bf16[32,2048]{1,0:T(8,128)(2,1)} %refs_6_.5) | copy-start | bytes 393220
  128.3 31.7 %copy-start = (bf16[2,128,4224]{2,1,0:T(8,128)(2,1)S(1)}, bf16[2,128,4224]{2,1,0:T(8,128)(2,1)}, u32[]{:S(2)}) copy-start(bf16[2,128,4224]{2,1,0:T(8,128)(2,1)} %shard_map.187.refs_3_.refs_2_) | copy-start | bytes 6488068
  151.1 8.9 %all-to-all-start.4 = ((bf16[4,16,1024]{2,1,0:T(8,128)(2,1)}), bf16[4,16,1024]{2,1,0:T(8,128)(2,1)S(1)}, u32[]{:S(2)}, u32[]{:S(2)}) async-start(bf16[4,16,1024]{2,1,0:T(8,128)(2,1)} %shard_map.196), calls=%async_computation.4 | async-start | bytes 262144 | tf_op jit(solution)/shard_map/all_to_all | solution.py:40
  154.4 12.1 %collective-permute-start.9 = (bf16[48,2048]{1,0:T(8,128)(2,1)}, bf16[48,2048]{1,0:T(8,128)(2,1)S(1)}, u32[]{:S(2)}, u32[]{:S(2)}) collective-permute-start(bf16[48,2048]{1,0:T(8,128)(2,1)} %get-tuple-element.28), channel_id=1, source_target_pairs={{0,16},{8,24},{16,32},{24,40},{32,48},{40,56},{48,0},{56,8},{1,17}... | collective-permute-start | bytes 589832 | tf_op jit(solution)/shard_map/ppermute | solution.py:552
  154.7 12.0 %collective-permute-start.10 = (bf16[48,2048]{1,0:T(8,128)(2,1)}, bf16[48,2048]{1,0:T(8,128)(2,1)S(1)}, u32[]{:S(2)}, u32[]{:S(2)}) collective-permute-start(bf16[48,2048]{1,0:T(8,128)(2,1)} %get-tuple-element.29), channel_id=1, source_target_pairs={{0,48},{8,56},{16,0},{24,8},{32,16},{40,24},{48,32},{56,40},{1,49}... | collective-permute-start | bytes 589832 | tf_op jit(solution)/shard_map/ppermute | solution.py:553
  161.5 10.4 %all-to-all-start.5 = ((bf16[8,32,128]{2,1,0:T(8,128)(2,1)}), bf16[8,32,128]{2,1,0:T(8,128)(2,1)S(1)}, u32[]{:S(2)}, u32[]{:S(2)}) async-start(bf16[8,32,128]{2,1,0:T(8,128)(2,1)} %shard_map.197), calls=%async_computation.5 | async-start | bytes 131072 | tf_op jit(solution)/shard_map/all_to_all | solution.py:40
  171.9 20.1 %copy-start.4 = (bf16[304,4096]{1,0:T(8,128)(2,1)S(1)}, bf16[304,4096]{1,0:T(8,128)(2,1)}, u32[]{:S(2)}) copy-start(bf16[304,4096]{1,0:T(8,128)(2,1)} %copy-done.3) | copy-start | bytes 7471108
  173.0 19.0 %all-to-all-start.6 = ((bf16[16,8,32,128]{3,2,1,0:T(8,128)(2,1)}), bf16[16,8,32,128]{3,2,1,0:T(8,128)(2,1)S(1)}, u32[]{:S(2)}, u32[]{:S(2)}) async-start(bf16[16,8,32,128]{3,2,1,0:T(8,128)(2,1)} %shard_map.198), calls=%async_computation.6 | async-start | bytes 2097152 | tf_op jit(solution)/shard_map/all_to_all | solution.py:40
  176.8 10.2 %collective-permute-start.12 = (bf16[32,2048]{1,0:T(8,128)(2,1)}, bf16[32,2048]{1,0:T(8,128)(2,1)S(1)}, u32[]{:S(2)}, u32[]{:S(2)}) collective-permute-start(bf16[32,2048]{1,0:T(8,128)(2,1)} %get-tuple-element.31), channel_id=1, source_target_pairs={{0,16},{8,24},{16,32},{24,40},{32,48},{40,56},{48,0},{56,8},{1,17}... | collective-permute-start | bytes 393224 | tf_op jit(solution)/shard_map/ppermute | solution.py:562
  177.9 9.1 %collective-permute-start.13 = (bf16[32,2048]{1,0:T(8,128)(2,1)}, bf16[32,2048]{1,0:T(8,128)(2,1)S(1)}, u32[]{:S(2)}, u32[]{:S(2)}) collective-permute-start(bf16[32,2048]{1,0:T(8,128)(2,1)} %get-tuple-element.32), channel_id=1, source_target_pairs={{0,56},{8,0},{16,8},{24,16},{32,24},{40,32},{48,40},{56,48},{1,57}... | collective-permute-start | bytes 393224 | tf_op jit(solution)/shard_map/ppermute | solution.py:562
  179.6 10.4 %collective-permute-start.14 = (bf16[32,2048]{1,0:T(8,128)(2,1)}, bf16[32,2048]{1,0:T(8,128)(2,1)S(1)}, u32[]{:S(2)}, u32[]{:S(2)}) collective-permute-start(bf16[32,2048]{1,0:T(8,128)(2,1)} %get-tuple-element.33), channel_id=1, source_target_pairs={{0,48},{8,56},{16,0},{24,8},{32,16},{40,24},{48,32},{56,40},{1,49}... | collective-permute-start | bytes 393224 | tf_op jit(solution)/shard_map/ppermute | solution.py:562
  180.9 9.8 %collective-permute-start.11 = (bf16[32,2048]{1,0:T(8,128)(2,1)}, bf16[32,2048]{1,0:T(8,128)(2,1)}, u32[]{:S(2)}, u32[]{:S(2)}) collective-permute-start(bf16[32,2048]{1,0:T(8,128)(2,1)} %get-tuple-element.30.refs_1_), channel_id=1, source_target_pairs={{0,8},{8,16},{16,24},{24,32},{32,40},{40,48},{48,56},{56,0},{1,9},... | collective-permute-start | bytes 393224 | tf_op jit(solution)/shard_map/ppermute | solution.py:562
  192.9 22.8 %copy-start.8 = (bf16[32,2048]{1,0:T(8,128)(2,1)S(1)}, bf16[32,2048]{1,0:T(8,128)(2,1)}, u32[]{:S(2)}) copy-start(bf16[32,2048]{1,0:T(8,128)(2,1)} %refs_6_.5) | copy-start | bytes 393220
  192.9 22.8 %copy-start.15 = (bf16[32,2048]{1,0:T(8,128)(2,1)S(1)}, bf16[32,2048]{1,0:T(8,128)(2,1)}, u32[]{:S(2)}) copy-start(bf16[32,2048]{1,0:T(8,128)(2,1)} %copy-done.14) | copy-start | bytes 393220
  192.9 22.8 %copy-start.17 = (bf16[32,2048]{1,0:T(8,128)(2,1)S(1)}, bf16[32,2048]{1,0:T(8,128)(2,1)}, u32[]{:S(2)}) copy-start(bf16[32,2048]{1,0:T(8,128)(2,1)} %copy-done.16) | copy-start | bytes 393220
  192.9 22.8 %copy-start.19 = (bf16[32,2048]{1,0:T(8,128)(2,1)S(1)}, bf16[32,2048]{1,0:T(8,128)(2,1)}, u32[]{:S(2)}) copy-start(bf16[32,2048]{1,0:T(8,128)(2,1)} %copy-done.18) | copy-start | bytes 393220
  192.9 22.8 %copy-start.20 = (f32[32,2048]{1,0:T(8,128)S(1)}, f32[32,2048]{1,0:T(8,128)}, u32[]{:S(2)}) copy-start(f32[32,2048]{1,0:T(8,128)} %get-tuple-element.26) | copy-start | bytes 786436
  192.9 4.2 %collective-permute-start.15 = (f32[304,128]{1,0:T(8,128)S(1)}, f32[304,128]{1,0:T(8,128)S(1)}, u32[]{:S(2)}, u32[]{:S(2)}) collective-permute-start(f32[304,128]{1,0:T(8,128)S(1)} %shard_map.200), channel_id=1, source_target_pairs={{0,1},{1,0},{2,3},{3,2},{4,5},{5,4},{6,7},{7,6},{8,9},{9,8},{10,11... | collective-permute-start | bytes 466952 | tf_op jit(solution)/shard_map/ppermute | solution.py:32
  211.1 11.2 %all-to-all-start.8 = ((f32[8,4,128]{2,1,0:T(4,128)}), f32[8,4,128]{2,1,0:T(4,128)S(1)}, u32[]{:S(2)}, u32[]{:S(2)}) async-start(f32[8,4,128]{2,1,0:T(4,128)} %shard_map.202), calls=%async_computation.8 | async-start | bytes 32768 | tf_op jit(solution)/shard_map/all_to_all | solution.py:40
  (12 other events, 65.9 us)

commit v7 on v6

--- a/solution.py
+++ b/solution.py
@@ -414,8 +414,19 @@
 def finish_kernel(stats, logits, logprob):
     top, sums = merged(stats[...])
     shift = top + jnp.log(sums)
-    for head in range(2):
-        logprob[head] = logits[head] - shift[head : head + 1, :]
+    own = jnp.where(pl.program_id(0) == 0, shift[0:1], shift[1:2])
+    logprob[0] = logits[0] - own
+
+
+def finish(stats, logits):
+    head = pl.BlockSpec((1,) + logits.shape[1:], lambda i: (i, 0, 0))
+    return pl.pallas_call(
+        finish_kernel,
+        out_shape=like(logits.shape, jnp.float32),
+        grid=(2,),
+        in_specs=[whole(stats), head],
+        out_specs=head,
+    )(stats, in_hbm(logits))
 
 
 def on_device(
@@ -617,7 +628,7 @@
     stats = exchange(stats, ("x", "y", "c"))
     stats = call(merge_kernel, [], [stats], pltpu.HBM((NZ, 4, EXPERTS), f32))
     stats = exchange(stats, "z")
-    logprob = call(finish_kernel, [], [stats, in_hbm(logits)], like((2, vocab, EXPERTS), f32))
+    logprob = finish(stats, logits)
     return (attended, layer_out, jnp.transpose(logprob, (0, 2, 1)))
 
 

time: 225 us -> 226 us (level)
    pallas_call x20 -> x19, Pallas kernels: 37.2 us -> 35.5 us  [call(): pl.pallas_call(body, out_shape=list(outs), in_specs=[SMEM] * count + [who...]
where the time goes in v7:
time: 226 us; the launch traced here: 225 us
  blocking collectives  94.2 us (42%)
  starting transfers between devices  45.3 us (20%)
  Pallas kernels  37.2 us (16%)
  waiting for transfers between devices  36.3 us (16%)
  local copies, waits for them, and re-layouts  5.69 us (3%)
  other arithmetic  3.76 us (2%)
    all_to_all x4, blocking collectives, exchange(): return lax.all_to_all(value, axes, 0, 0, tiled=True)  94.2 us
    pallas_call x19, Pallas kernels, call(): pl.pallas_call(body, out_shape=list(outs), in_specs=[SMEM] * count + [who...  35.5 us
    all_to_all x5, starting transfers between devices, exchange(): return lax.all_to_all(value, axes, 0, 0, tiled=True)  21.5 us
    all_to_all x5, waiting for transfers between devices, exchange(): return lax.all_to_all(value, axes, 0, 0, tiled=True)  12.6 us
    ppermute x3, waiting for transfers between devices, on_device(): lax.ppermute(wide_w, 'y', around(NY, step))  10.9 us
    ppermute x7, starting transfers between devices, swap(): return lax.ppermute(value, TP, SWAP)  10.9 us
    ppermute x4, waiting for transfers between devices, on_device(): lax.ppermute(part, 'z', around(NZ, step))  7.74 us
    ppermute x4, starting transfers between devices, on_device(): lax.ppermute(part, 'z', around(NZ, step))  5.45 us
  transfers between devices with their start and end apart: 21, of which 14 were waited for; matrix products, arithmetic and copies ran while one was open for 3% of the time, Pallas kernels for 8%

profile of v7, /device:TPU:1, one launch (start us, length us, event | category | flops | bytes accessed | tf_op | source)
XLA Modules:
  0.0 224.6 jit_solution(4964403265195440263)
XLA Ops:
  0.6 3.3 %collective-permute-start.5 = (bf16[304,4096]{1,0:T(8,128)(2,1)}, bf16[304,4096]{1,0:T(8,128)(2,1)S(1)}, u32[]{:S(2)}, u32[]{:S(2)}) collective-permute-start(bf16[304,4096]{1,0:T(8,128)(2,1)} %refs_1_.7), channel_id=1, source_target_pairs={{0,1},{1,0},{2,3},{3,2},{4,5},{5,4},{6,7},{7,6},{8,9},{9,8},{10,11... | collective-permute-start | bytes 7471112 | tf_op jit(solution)/shard_map/ppermute | solution.py:32
  4.6 2.2 shard_map.185
  6.8 6.5 %all-to-all-start = ((bf16[8,32,2176]{2,1,0:T(8,128)(2,1)}), bf16[8,32,2176]{2,1,0:T(8,128)(2,1)}, u32[]{:S(2)}, u32[]{:S(2)}) async-start(bf16[8,32,2176]{2,1,0:T(8,128)(2,1)} %shard_map.185), calls=%async_computation | async-start | bytes 2228224 | tf_op jit(solution)/shard_map/all_to_all | solution.py:40
  14.3 2.8 %collective-permute-start.2 = (bf16[2,16,4224]{2,1,0:T(8,128)(2,1)S(1)}, bf16[2,16,4224]{2,1,0:T(8,128)(2,1)S(1)}, u32[]{:S(2)}, u32[]{:S(2)}) collective-permute-start(bf16[2,16,4224]{2,1,0:T(8,128)(2,1)S(1)} %shard_map.186.refs_2_), channel_id=1, source_target_pairs={{0,6},{2,0},{4,2},{6,4},{1,7},{3,1},{5,3},{7,5},{8,14},{10,8},{12,... | collective-permute-start | bytes 811016 | tf_op jit(solution)/shard_map/ppermute | solution.py:481
  18.1 2.7 %dynamic-slice_bitcast_fusion = bf16[384,2048]{1,0:T(8,128)(2,1)} fusion(bf16[1,384,4096]{2,1,0:T(8,128)(2,1)} %refs_2_.3, s32[]{:T(128)S(6)} %select_n.3), kind=kLoop, calls=%fused_computation | loop fusion | bytes 3145732 | tf_op jit(solution)/shard_map/dynamic_slice | solution.py:489
  22.0 6.3 %collective-permute-done.2.refs_5_ = bf16[2,16,4224]{2,1,0:T(8,128)(2,1)S(1)} collective-permute-done((bf16[2,16,4224]{2,1,0:T(8,128)(2,1)S(1)}, bf16[2,16,4224]{2,1,0:T(8,128)(2,1)S(1)}, u32[]{:S(2)}, u32[]{:S(2)}) %collective-permute-start.2) | collective-permute-done | bytes 270368 | tf_op jit(solution)/shard_map/ppermute | solution.py:481
  28.3 4.6 %collective-permute-done.refs_3_ = bf16[2,16,4224]{2,1,0:T(8,128)(2,1)} collective-permute-done((bf16[2,16,4224]{2,1,0:T(8,128)(2,1)S(1)}, bf16[2,16,4224]{2,1,0:T(8,128)(2,1)}, u32[]{:S(2)}, u32[]{:S(2)}) %collective-permute-start) | collective-permute-done | bytes 270368 | tf_op jit(solution)/shard_map/ppermute | solution.py:481
  32.9 2.1 pad_maximum_fusion
  37.1 2.1 shard_map.184.refs_2_
  39.3 2.8 %shard_map.187.refs_3_.refs_2_ = bf16[2,128,4224]{2,1,0:T(8,128)(2,1)} custom-call(s32[1]{0:T(128)} %bitcast.3.refs_0_, s32[1]{0:T(128)} %bitcast.4.refs_1_, bf16[2,16,4224]{2,1,0:T(8,128)(2,1)S(1)} %shard_map.186.refs_2_, bf16[2,16,4224]{2,1,0:T(8,128)(2,1)} %collective-permute-done.refs_3_, bf16[2,16,4224]{2,1,0:T(8,128)(2,1)S(1)} %collective-permute-done.1.refs_4_, ...), custom_call_target="tpu_custom_call" | custom-call | bytes 4194304 | tf_op jit(solution)/shard_map/pallas_call | solution.py:105
  44.0 3.8 %shard_map.188 = (bf16[16,32,2048]{2,1,0:T(8,128)(2,1)S(1)}, bf16[512,256]{1,0:T(8,128)(2,1)}, bf16[512,256]{1,0:T(8,128)(2,1)}, bf16[16,512]{1,0:T(8,128)(2,1)S(1)}) custom-call(s32[1]{0:T(128)} %bitcast.refs_0_.refs_1_, bf16[8,32,2176]{2,1,0:T(8,128)(2,1)} %all-to-all-done.refs_1_, bf16[1,32,4096]{2,1,0:T(8,128)(2,1)} %shard_map.184.refs_2_, ...), custom_call_target="tpu_custom_call" | custom-call | flops 536870912 | bytes 4194304 | tf_op jit(solution)/shard_map/pallas_call | solution.py:105
  47.8 34.0 %all_to_all.45.refs_0_.refs_1_ = bf16[16,32,2048]{2,1,0:T(8,128)(2,1)S(1)} all-to-all(bf16[16,32,2048]{2,1,0:T(8,128)(2,1)S(1)} %get-tuple-element.23), channel_id=1, replica_groups=mesh['x'=4,'z'=8,'y'=4,'c'=2] {'x','y'}, dimensions={0} | all-to-all | bytes 4194304 | tf_op jit(solution)/shard_map/all_to_all | solution.py:40
  81.8 2.0 collective-permute-start.6
  84.6 3.0 %collective-permute-done.7.refs_3_ = f32[4,128]{1,0:T(4,128)S(1)} collective-permute-done((f32[4,128]{1,0:T(4,128)S(1)}, f32[4,128]{1,0:T(4,128)S(1)}, u32[]{:S(2)}, u32[]{:S(2)}) %collective-permute-start.7) | collective-permute-done | bytes 2080 | tf_op jit(solution)/shard_map/ppermute | solution.py:32
  87.6 2.7 %shard_map.190 = (f32[512,384]{1,0:T(8,128)S(1)}, f32[512,384]{1,0:T(8,128)S(1)}) custom-call(s32[1]{0:T(128)} %bitcast.3.refs_0_, bf16[16,32,2048]{2,1,0:T(8,128)(2,1)S(1)} %all_to_all.45.refs_0_.refs_1_, f32[4,128]{1,0:T(4,128)S(1)} %shard_map.189.refs_2_, f32[4,128]{1,0:T(4,128)S(1)} %collective-permute-done.7.refs_3_, f32[32,128]{1,0:T(8,128)S(1)} %bitcast.18, ...), custom_call_target="tpu_custom_call" | custom-call | flops 1610612736 | bytes 8388608 | tf_op jit(solution)/shard_map/pallas_call | solution.py:105
  90.4 2.8 %shard_map.191.refs_1_ = bf16[512,384]{1,0:T(8,128)(2,1)S(1)} custom-call(s32[1]{0:T(128)} %bitcast.3.refs_0_, bf16[16,32,2048]{2,1,0:T(8,128)(2,1)S(1)} %collective-permute-done.6.refs_1_, f32[4,128]{1,0:T(4,128)S(1)} %shard_map.189.refs_2_, f32[4,128]{1,0:T(4,128)S(1)} %collective-permute-done.7.refs_3_, f32[32,128]{1,0:T(8,128)S(1)} %bitcast.19, ...), custom_call_target="tpu_custom_call" | custom-call | flops 1610612736 | bytes 8388608 | tf_op jit(solution)/shard_map/pallas_call | solution.py:105
  95.0 2.7 %shard_map.193 = bf16[16,32,2048]{2,1,0:T(8,128)(2,1)S(1)} custom-call(f32[512,2048]{1,0:T(8,128)S(1)} %shard_map.192.refs_0_, bf16[512,384]{1,0:T(8,128)(2,1)S(1)} %collective-permute-done.8.refs_1_, bf16[384,2048]{1,0:T(8,128)(2,1)} %collective-permute-done.4.refs_4_.refs_2_), custom_call_target="tpu_custom_call" | custom-call | flops 805306368 | bytes 6291456 | tf_op jit(solution)/shard_map/pallas_call | solution.py:105
  97.6 30.7 %all_to_all.46.refs_5_ = bf16[16,32,2048]{2,1,0:T(8,128)(2,1)S(1)} all-to-all(bf16[16,32,2048]{2,1,0:T(8,128)(2,1)S(1)} %shard_map.193), channel_id=1, replica_groups=mesh['x'=4,'z'=8,'y'=4,'c'=2] {'x','y'}, dimensions={0} | all-to-all | bytes 4194304 | tf_op jit(solution)/shard_map/all_to_all | solution.py:40
  128.3 4.0 %shard_map.194 = (bf16[16,8,1024]{2,1,0:T(8,128)(2,1)}, f32[32,2048]{1,0:T(8,128)}, bf16[48,2048]{1,0:T(8,128)(2,1)}, bf16[48,2048]{1,0:T(8,128)(2,1)}, f32[4,32,2048]{2,1,0:T(8,128)}) custom-call(s32[1]{0:T(128)S(6)} %copy.21.refs_0_, s32[1]{0:T(128)} %bitcast.refs_0_.refs_1_, bf16[16,512]{1,0:T(8,128)(2,1)S(1)} %get-tuple-element.20.refs_2_, ...), custom_call_target="tpu_custom_call" | custom-call | flops 1073741824 | bytes 6291456 | tf_op jit(solution)/shard_map/pallas_call | solution.py:105
  132.3 17.2 %all_to_all.47.refs_0_ = bf16[16,8,1024]{2,1,0:T(8,128)(2,1)S(1)} all-to-all(bf16[16,8,1024]{2,1,0:T(8,128)(2,1)} %get-tuple-element.34), channel_id=1, replica_groups=mesh['x'=4,'z'=8,'y'=4,'c'=2] {'z','c'}, dimensions={0} | all-to-all | bytes 524288 | tf_op jit(solution)/shard_map/all_to_all | solution.py:40
  151.1 3.3 %all-to-all-start.4 = ((bf16[4,16,1024]{2,1,0:T(8,128)(2,1)}), bf16[4,16,1024]{2,1,0:T(8,128)(2,1)S(1)}, u32[]{:S(2)}, u32[]{:S(2)}) async-start(bf16[4,16,1024]{2,1,0:T(8,128)(2,1)} %shard_map.196), calls=%async_computation.4 | async-start | bytes 262144 | tf_op jit(solution)/shard_map/all_to_all | solution.py:40
  154.7 3.4 %collective-permute-start.10 = (bf16[48,2048]{1,0:T(8,128)(2,1)}, bf16[48,2048]{1,0:T(8,128)(2,1)S(1)}, u32[]{:S(2)}, u32[]{:S(2)}) collective-permute-start(bf16[48,2048]{1,0:T(8,128)(2,1)} %get-tuple-element.29), channel_id=1, source_target_pairs={{0,48},{8,56},{16,0},{24,8},{32,16},{40,24},{48,32},{56,40},{1,49}... | collective-permute-start | bytes 589832 | tf_op jit(solution)/shard_map/ppermute | solution.py:564
  161.5 3.3 %all-to-all-start.5 = ((bf16[8,32,128]{2,1,0:T(8,128)(2,1)}), bf16[8,32,128]{2,1,0:T(8,128)(2,1)S(1)}, u32[]{:S(2)}, u32[]{:S(2)}) async-start(bf16[8,32,128]{2,1,0:T(8,128)(2,1)} %shard_map.197), calls=%async_computation.5 | async-start | bytes 131072 | tf_op jit(solution)/shard_map/all_to_all | solution.py:40
  167.3 2.1 shard_map.195
  169.5 2.4 %all-to-all-done.5.refs_0_ = bf16[8,32,128]{2,1,0:T(8,128)(2,1)S(1)} async-done(((bf16[8,32,128]{2,1,0:T(8,128)(2,1)}), bf16[8,32,128]{2,1,0:T(8,128)(2,1)S(1)}, u32[]{:S(2)}, u32[]{:S(2)}) %all-to-all-start.5) | async-done | bytes 65568 | tf_op jit(solution)/shard_map/all_to_all | solution.py:40
  173.0 3.8 %all-to-all-start.6 = ((bf16[16,8,32,128]{3,2,1,0:T(8,128)(2,1)}), bf16[16,8,32,128]{3,2,1,0:T(8,128)(2,1)S(1)}, u32[]{:S(2)}, u32[]{:S(2)}) async-start(bf16[16,8,32,128]{3,2,1,0:T(8,128)(2,1)} %shard_map.198), calls=%async_computation.6 | async-start | bytes 2097152 | tf_op jit(solution)/shard_map/all_to_all | solution.py:40
  182.3 4.8 %collective-permute-done.12.refs_3_ = bf16[32,2048]{1,0:T(8,128)(2,1)S(1)} collective-permute-done((bf16[32,2048]{1,0:T(8,128)(2,1)}, bf16[32,2048]{1,0:T(8,128)(2,1)S(1)}, u32[]{:S(2)}, u32[]{:S(2)}) %collective-permute-start.12) | collective-permute-done | bytes 131104 | tf_op jit(solution)/shard_map/ppermute | solution.py:573
  187.0 3.0 %collective-permute-done.14.refs_5_ = bf16[32,2048]{1,0:T(8,128)(2,1)S(1)} collective-permute-done((bf16[32,2048]{1,0:T(8,128)(2,1)}, bf16[32,2048]{1,0:T(8,128)(2,1)S(1)}, u32[]{:S(2)}, u32[]{:S(2)}) %collective-permute-start.14) | collective-permute-done | bytes 131104 | tf_op jit(solution)/shard_map/ppermute | solution.py:573
  192.9 3.2 %collective-permute-start.15 = (f32[304,128]{1,0:T(8,128)S(1)}, f32[304,128]{1,0:T(8,128)S(1)}, u32[]{:S(2)}, u32[]{:S(2)}) collective-permute-start(f32[304,128]{1,0:T(8,128)S(1)} %shard_map.200), channel_id=1, source_target_pairs={{0,1},{1,0},{2,3},{3,2},{4,5},{5,4},{6,7},{7,6},{8,9},{9,8},{10,11... | collective-permute-start | bytes 466952 | tf_op jit(solution)/shard_map/ppermute | solution.py:32
  198.2 12.3 %all_to_all.48.refs_0_ = f32[32,4,128]{2,1,0:T(4,128)S(1)} all-to-all(f32[32,4,128]{2,1,0:T(4,128)} %get-tuple-element.35), channel_id=1, replica_groups=mesh['x'=4,'z'=8,'y'=4,'c'=2] {'x','y','c'}, dimensions={0} | all-to-all | bytes 131072 | tf_op jit(solution)/shard_map/all_to_all | solution.py:40
  211.1 4.6 %all-to-all-start.8 = ((f32[8,4,128]{2,1,0:T(4,128)}), f32[8,4,128]{2,1,0:T(4,128)S(1)}, u32[]{:S(2)}, u32[]{:S(2)}) async-start(f32[8,4,128]{2,1,0:T(4,128)} %shard_map.202), calls=%async_computation.8 | async-start | bytes 32768 | tf_op jit(solution)/shard_map/all_to_all | solution.py:40
  217.4 4.9 %all-to-all-done.8.stats = f32[8,4,128]{2,1,0:T(4,128)S(1)} async-done(((f32[8,4,128]{2,1,0:T(4,128)}), f32[8,4,128]{2,1,0:T(4,128)S(1)}, u32[]{:S(2)}, u32[]{:S(2)}) %all-to-all-start.8) | async-done | bytes 16416 | tf_op jit(solution)/shard_map/all_to_all | solution.py:40
  (85 shorter events, 33.1 us)
Async XLA Ops:
  0.6 43.4 %collective-permute-start.5 = (bf16[304,4096]{1,0:T(8,128)(2,1)}, bf16[304,4096]{1,0:T(8,128)(2,1)S(1)}, u32[]{:S(2)}, u32[]{:S(2)}) collective-permute-start(bf16[304,4096]{1,0:T(8,128)(2,1)} %refs_1_.7), channel_id=1, source_target_pairs={{0,1},{1,0},{2,3},{3,2},{4,5},{5,4},{6,7},{7,6},{8,9},{9,8},{10,11... | collective-permute-start | bytes 7471112 | tf_op jit(solution)/shard_map/ppermute | solution.py:32
  6.8 37.2 %all-to-all-start = ((bf16[8,32,2176]{2,1,0:T(8,128)(2,1)}), bf16[8,32,2176]{2,1,0:T(8,128)(2,1)}, u32[]{:S(2)}, u32[]{:S(2)}) async-start(bf16[8,32,2176]{2,1,0:T(8,128)(2,1)} %shard_map.185), calls=%async_computation | async-start | bytes 2228224 | tf_op jit(solution)/shard_map/all_to_all | solution.py:40
  14.3 14.0 %collective-permute-start.2 = (bf16[2,16,4224]{2,1,0:T(8,128)(2,1)S(1)}, bf16[2,16,4224]{2,1,0:T(8,128)(2,1)S(1)}, u32[]{:S(2)}, u32[]{:S(2)}) collective-permute-start(bf16[2,16,4224]{2,1,0:T(8,128)(2,1)S(1)} %shard_map.186.refs_2_), channel_id=1, source_target_pairs={{0,6},{2,0},{4,2},{6,4},{1,7},{3,1},{5,3},{7,5},{8,14},{10,8},{12,... | collective-permute-start | bytes 811016 | tf_op jit(solution)/shard_map/ppermute | solution.py:481
  17.1 11.2 %collective-permute-start.1 = (bf16[2,16,4224]{2,1,0:T(8,128)(2,1)S(1)}, bf16[2,16,4224]{2,1,0:T(8,128)(2,1)S(1)}, u32[]{:S(2)}, u32[]{:S(2)}) collective-permute-start(bf16[2,16,4224]{2,1,0:T(8,128)(2,1)S(1)} %shard_map.186.refs_2_), channel_id=1, source_target_pairs={{0,4},{2,6},{4,0},{6,2},{1,5},{3,7},{5,1},{7,3},{8,12},{10,14},{12... | collective-permute-start | bytes 811016 | tf_op jit(solution)/shard_map/ppermute | solution.py:481
  17.4 15.5 %collective-permute-start = (bf16[2,16,4224]{2,1,0:T(8,128)(2,1)S(1)}, bf16[2,16,4224]{2,1,0:T(8,128)(2,1)}, u32[]{:S(2)}, u32[]{:S(2)}) collective-permute-start(bf16[2,16,4224]{2,1,0:T(8,128)(2,1)S(1)} %shard_map.186.refs_2_), channel_id=1, source_target_pairs={{0,2},{2,4},{4,6},{6,0},{1,3},{3,5},{5,7},{7,1},{8,10},{10,12},{12... | collective-permute-start | bytes 811016 | tf_op jit(solution)/shard_map/ppermute | solution.py:481
  20.8 21.3 %collective-permute-start.4 = (bf16[384,2048]{1,0:T(8,128)(2,1)}, bf16[384,2048]{1,0:T(8,128)(2,1)}, u32[]{:S(2)}, u32[]{:S(2)}) collective-permute-start(bf16[384,2048]{1,0:T(8,128)(2,1)} %dynamic-slice_bitcast_fusion), channel_id=1, source_target_pairs={{0,1},{1,0},{2,3},{3,2},{4,5},{5,4},{6,7},{7,6},{8,9},{9,8},{10,11... | collective-permute-start | bytes 4718600 | tf_op jit(solution)/shard_map/ppermute | solution.py:32
  35.0 4.3 %collective-permute-start.3 = (bf16[4,2,16,4224]{3,2,1,0:T(8,128)(2,1)}, bf16[4,2,16,4224]{3,2,1,0:T(8,128)(2,1)}, u32[]{:S(2)}, u32[]{:S(2)}) collective-permute-start(bf16[4,2,16,4224]{3,2,1,0:T(8,128)(2,1)} %pad_maximum_fusion), channel_id=1, source_target_pairs={{0,1},{1,0},{2,3},{3,2},{4,5},{5,4},{6,7},{7,6},{8,9},{9,8},{10,11... | collective-permute-start | bytes 3244040 | tf_op jit(solution)/shard_map/ppermute | solution.py:32
  44.0 43.6 %copy-start.11 = (f32[4096]{0:T(1024)S(1)}, f32[4096]{0:T(1024)}, u32[]{:S(2)}) copy-start(f32[4096]{0:T(1024)} %param.23) | copy-start | bytes 49156
  47.8 39.8 %copy-start.1 = (bf16[1,4096,384]{2,1,0:T(8,128)(2,1)S(1)}, bf16[1,4096,384]{2,1,0:T(8,128)(2,1)}, u32[]{:S(2)}) copy-start(bf16[1,4096,384]{2,1,0:T(8,128)(2,1)} %refs_5_.3) | copy-start | bytes 9437188
  47.8 39.8 %copy-start.2 = (bf16[1,4096,384]{2,1,0:T(8,128)(2,1)S(1)}, bf16[1,4096,384]{2,1,0:T(8,128)(2,1)}, u32[]{:S(2)}) copy-start(bf16[1,4096,384]{2,1,0:T(8,128)(2,1)} %refs_6_.4) | copy-start | bytes 9437188
  81.8 8.5 %collective-permute-start.6 = (bf16[16,32,2048]{2,1,0:T(8,128)(2,1)S(1)}, bf16[16,32,2048]{2,1,0:T(8,128)(2,1)S(1)}, u32[]{:S(2)}, u32[]{:S(2)}) collective-permute-start(bf16[16,32,2048]{2,1,0:T(8,128)(2,1)S(1)} %all_to_all.45.refs_0_.refs_1_), channel_id=1, source_target_pairs={{0,1},{1,0},{2,3},{3,2},{4,5},{5,4},{6,7},{7,6},{8,9},{9,8},{10,11... | collective-permute-start | bytes 6291464 | tf_op jit(solution)/shard_map/ppermute | solution.py:32
  84.3 3.3 %collective-permute-start.7 = (f32[4,128]{1,0:T(4,128)S(1)}, f32[4,128]{1,0:T(4,128)S(1)}, u32[]{:S(2)}, u32[]{:S(2)}) collective-permute-start(f32[4,128]{1,0:T(4,128)S(1)} %shard_map.189.refs_2_), channel_id=1, source_target_pairs={{0,1},{1,0},{2,3},{3,2},{4,5},{5,4},{6,7},{7,6},{8,9},{9,8},{10,11... | collective-permute-start | bytes 6152 | tf_op jit(solution)/shard_map/ppermute | solution.py:32
  93.1 1.8 collective-permute-start.8
  97.6 30.7 %copy-start.7 = (bf16[32,2048]{1,0:T(8,128)(2,1)S(1)}, bf16[32,2048]{1,0:T(8,128)(2,1)}, u32[]{:S(2)}) copy-start(bf16[32,2048]{1,0:T(8,128)(2,1)} %refs_6_.5) | copy-start | bytes 393220
  128.3 31.8 %copy-start = (bf16[2,128,4224]{2,1,0:T(8,128)(2,1)S(1)}, bf16[2,128,4224]{2,1,0:T(8,128)(2,1)}, u32[]{:S(2)}) copy-start(bf16[2,128,4224]{2,1,0:T(8,128)(2,1)} %shard_map.187.refs_3_.refs_2_) | copy-start | bytes 6488068
  151.1 8.9 %all-to-all-start.4 = ((bf16[4,16,1024]{2,1,0:T(8,128)(2,1)}), bf16[4,16,1024]{2,1,0:T(8,128)(2,1)S(1)}, u32[]{:S(2)}, u32[]{:S(2)}) async-start(bf16[4,16,1024]{2,1,0:T(8,128)(2,1)} %shard_map.196), calls=%async_computation.4 | async-start | bytes 262144 | tf_op jit(solution)/shard_map/all_to_all | solution.py:40
  154.5 12.1 %collective-permute-start.9 = (bf16[48,2048]{1,0:T(8,128)(2,1)}, bf16[48,2048]{1,0:T(8,128)(2,1)S(1)}, u32[]{:S(2)}, u32[]{:S(2)}) collective-permute-start(bf16[48,2048]{1,0:T(8,128)(2,1)} %get-tuple-element.28), channel_id=1, source_target_pairs={{0,16},{8,24},{16,32},{24,40},{32,48},{40,56},{48,0},{56,8},{1,17}... | collective-permute-start | bytes 589832 | tf_op jit(solution)/shard_map/ppermute | solution.py:563
  154.7 12.0 %collective-permute-start.10 = (bf16[48,2048]{1,0:T(8,128)(2,1)}, bf16[48,2048]{1,0:T(8,128)(2,1)S(1)}, u32[]{:S(2)}, u32[]{:S(2)}) collective-permute-start(bf16[48,2048]{1,0:T(8,128)(2,1)} %get-tuple-element.29), channel_id=1, source_target_pairs={{0,48},{8,56},{16,0},{24,8},{32,16},{40,24},{48,32},{56,40},{1,49}... | collective-permute-start | bytes 589832 | tf_op jit(solution)/shard_map/ppermute | solution.py:564
  161.5 10.4 %all-to-all-start.5 = ((bf16[8,32,128]{2,1,0:T(8,128)(2,1)}), bf16[8,32,128]{2,1,0:T(8,128)(2,1)S(1)}, u32[]{:S(2)}, u32[]{:S(2)}) async-start(bf16[8,32,128]{2,1,0:T(8,128)(2,1)} %shard_map.197), calls=%async_computation.5 | async-start | bytes 131072 | tf_op jit(solution)/shard_map/all_to_all | solution.py:40
  171.9 20.1 %copy-start.4 = (bf16[304,4096]{1,0:T(8,128)(2,1)S(1)}, bf16[304,4096]{1,0:T(8,128)(2,1)}, u32[]{:S(2)}) copy-start(bf16[304,4096]{1,0:T(8,128)(2,1)} %copy-done.3) | copy-start | bytes 7471108
  173.0 19.0 %all-to-all-start.6 = ((bf16[16,8,32,128]{3,2,1,0:T(8,128)(2,1)}), bf16[16,8,32,128]{3,2,1,0:T(8,128)(2,1)S(1)}, u32[]{:S(2)}, u32[]{:S(2)}) async-start(bf16[16,8,32,128]{3,2,1,0:T(8,128)(2,1)} %shard_map.198), calls=%async_computation.6 | async-start | bytes 2097152 | tf_op jit(solution)/shard_map/all_to_all | solution.py:40
  176.8 10.2 %collective-permute-start.12 = (bf16[32,2048]{1,0:T(8,128)(2,1)}, bf16[32,2048]{1,0:T(8,128)(2,1)S(1)}, u32[]{:S(2)}, u32[]{:S(2)}) collective-permute-start(bf16[32,2048]{1,0:T(8,128)(2,1)} %get-tuple-element.31), channel_id=1, source_target_pairs={{0,16},{8,24},{16,32},{24,40},{32,48},{40,56},{48,0},{56,8},{1,17}... | collective-permute-start | bytes 393224 | tf_op jit(solution)/shard_map/ppermute | solution.py:573
  177.9 9.1 %collective-permute-start.13 = (bf16[32,2048]{1,0:T(8,128)(2,1)}, bf16[32,2048]{1,0:T(8,128)(2,1)S(1)}, u32[]{:S(2)}, u32[]{:S(2)}) collective-permute-start(bf16[32,2048]{1,0:T(8,128)(2,1)} %get-tuple-element.32), channel_id=1, source_target_pairs={{0,56},{8,0},{16,8},{24,16},{32,24},{40,32},{48,40},{56,48},{1,57}... | collective-permute-start | bytes 393224 | tf_op jit(solution)/shard_map/ppermute | solution.py:573
  179.6 10.4 %collective-permute-start.14 = (bf16[32,2048]{1,0:T(8,128)(2,1)}, bf16[32,2048]{1,0:T(8,128)(2,1)S(1)}, u32[]{:S(2)}, u32[]{:S(2)}) collective-permute-start(bf16[32,2048]{1,0:T(8,128)(2,1)} %get-tuple-element.33), channel_id=1, source_target_pairs={{0,48},{8,56},{16,0},{24,8},{32,16},{40,24},{48,32},{56,40},{1,49}... | collective-permute-start | bytes 393224 | tf_op jit(solution)/shard_map/ppermute | solution.py:573
  180.9 9.8 %collective-permute-start.11 = (bf16[32,2048]{1,0:T(8,128)(2,1)}, bf16[32,2048]{1,0:T(8,128)(2,1)}, u32[]{:S(2)}, u32[]{:S(2)}) collective-permute-start(bf16[32,2048]{1,0:T(8,128)(2,1)} %get-tuple-element.30.refs_1_), channel_id=1, source_target_pairs={{0,8},{8,16},{16,24},{24,32},{32,40},{40,48},{48,56},{56,0},{1,9},... | collective-permute-start | bytes 393224 | tf_op jit(solution)/shard_map/ppermute | solution.py:573
  192.9 22.8 %copy-start.8 = (bf16[32,2048]{1,0:T(8,128)(2,1)S(1)}, bf16[32,2048]{1,0:T(8,128)(2,1)}, u32[]{:S(2)}) copy-start(bf16[32,2048]{1,0:T(8,128)(2,1)} %refs_6_.5) | copy-start | bytes 393220
  192.9 22.8 %copy-start.15 = (bf16[32,2048]{1,0:T(8,128)(2,1)S(1)}, bf16[32,2048]{1,0:T(8,128)(2,1)}, u32[]{:S(2)}) copy-start(bf16[32,2048]{1,0:T(8,128)(2,1)} %copy-done.14) | copy-start | bytes 393220
  192.9 22.8 %copy-start.17 = (bf16[32,2048]{1,0:T(8,128)(2,1)S(1)}, bf16[32,2048]{1,0:T(8,128)(2,1)}, u32[]{:S(2)}) copy-start(bf16[32,2048]{1,0:T(8,128)(2,1)} %copy-done.16) | copy-start | bytes 393220
  192.9 22.8 %copy-start.19 = (bf16[32,2048]{1,0:T(8,128)(2,1)S(1)}, bf16[32,2048]{1,0:T(8,128)(2,1)}, u32[]{:S(2)}) copy-start(bf16[32,2048]{1,0:T(8,128)(2,1)} %copy-done.18) | copy-start | bytes 393220
  192.9 22.8 %copy-start.20 = (f32[32,2048]{1,0:T(8,128)S(1)}, f32[32,2048]{1,0:T(8,128)}, u32[]{:S(2)}) copy-start(f32[32,2048]{1,0:T(8,128)} %get-tuple-element.26) | copy-start | bytes 786436
  192.9 4.2 %collective-permute-start.15 = (f32[304,128]{1,0:T(8,128)S(1)}, f32[304,128]{1,0:T(8,128)S(1)}, u32[]{:S(2)}, u32[]{:S(2)}) collective-permute-start(f32[304,128]{1,0:T(8,128)S(1)} %shard_map.200), channel_id=1, source_target_pairs={{0,1},{1,0},{2,3},{3,2},{4,5},{5,4},{6,7},{7,6},{8,9},{9,8},{10,11... | collective-permute-start | bytes 466952 | tf_op jit(solution)/shard_map/ppermute | solution.py:32
  211.1 11.2 %all-to-all-start.8 = ((f32[8,4,128]{2,1,0:T(4,128)}), f32[8,4,128]{2,1,0:T(4,128)S(1)}, u32[]{:S(2)}, u32[]{:S(2)}) async-start(f32[8,4,128]{2,1,0:T(4,128)} %shard_map.202), calls=%async_computation.8 | async-start | bytes 32768 | tf_op jit(solution)/shard_map/all_to_all | solution.py:40
  (13 other events, 66.5 us)
